TPU v7x, 256 devices: a whole 4x4x8 slice. The times are simulated.
256 devices in a mesh: seq: 32 (over y, z), head: 8 (over x, core).
Axes of the slice: x: 4, y: 4, z: 8, core: 2. Of those that a mesh axis runs over, the one named last changes fastest.
Arguments:
- tokens: bfloat16 [8192, 2048], P('seq'), may hold values from -12 to 12
- w_qk: bfloat16 [2048, 2, 2048], P(None, None, 'head'), may hold values from -0.125 to 0.125
- w_vz: bfloat16 [2048, 2, 4096], P(None, None, 'head'), may hold values from -0.125 to 0.125
- w_ab: bfloat16 [2048, 2, 32], P(None, None, 'head'), may hold values from -1 to 1
- conv_qk: float32 [4, 2, 2048], P(None, None, 'head'), may hold values from -3 to 3
- conv_v: float32 [4, 4096], P(None, 'head'), may hold values from -3 to 3
- a_log: float32 [32], P('head'), may hold values from -4 to -1
- dt_bias: float32 [32], P('head'), may hold values from -13 to 2
- beta_bias: float32 [32], P('head'), may hold values from -7 to 1
- norm_gain: float32 [128], replicated, may hold values from 0.1 to 1.9
- w_out: bfloat16 [4096, 2048], P('head'), may hold values from -0.125 to 0.125
Outputs:
- mixed: bfloat16 [8192, 2048], P('seq', 'head')
All inputs are finite; a program needn't handle non-finite values.
Results may differ from a plain program's by a relative error of at most 0.0049.
Values sent between devices are 32-bit elements; how exact they have to be, the bound alone decides.
No kernel may reach another device: no remote copies, remote signals or barrier semaphores. Data moves between devices by JAX's collectives and lax.ppermute only.
A program may use at most 128 MiB of HBM per device.

v0:
```python
import jax
import jax.numpy as jnp
from jax import lax
from jax.sharding import PartitionSpec as P

MATCHING_COUNT = 16
V_HEADS = 32
DK = 128
SPAN = 64


highest_setting = lax.Precision.HIGHEST


def from_behind(block, axis, distance):
    devices = range(lax.axis_size(axis))
    route = [(i - distance, i) for i in devices if i - distance in devices]
    return lax.ppermute(block, axis, route)


def unit_rows(vectors):
    return vectors * lax.rsqrt(jnp.sum(vectors * vectors, -1, keepdims=True) + 1e-06)


def by_blocks(series, block_len):
    tok_count, attention_number, depth = series.shape
    return series.reshape(tok_count // block_len, block_len, attention_number, depth).transpose(
        0, 2, 1, 3
    )


def chain_maps(earlier, later):
    first_a, first_b = earlier
    second_a, second_b = later
    joined_a = jnp.einsum("hij,hjk->hik", second_a, first_a, precision=highest_setting)
    joined_b = jnp.einsum("hij,hjv->hiv", second_a, first_b, precision=highest_setting) + second_b
    return (joined_a, joined_b)


def local(tokens, w_qk, w_vz, w_ab, conv_qk, conv_v, a_log, dt_bias, beta_bias, norm_gain, w_out):
    tok_count = tokens.shape[0]
    kernel_len = conv_v.shape[0]
    local_heads = a_log.shape[0]
    head_dim = norm_gain.shape[0]
    qk_width = w_qk.shape[2]
    key_dim = DK
    qk_heads = qk_width // key_dim
    group_size = V_HEADS // MATCHING_COUNT
    proj_qk = jnp.einsum("td,dcf->tcf", tokens, w_qk, preferred_element_type=jnp.float32)
    proj_vz = jnp.einsum("td,dcf->tcf", tokens, w_vz, preferred_element_type=jnp.float32)
    proj_ab = jnp.einsum("td,dcf->tcf", tokens, w_ab, preferred_element_type=jnp.float32)
    channels = jnp.concatenate([proj_qk.reshape(tok_count, 2 * qk_width), proj_vz[:, 0]], 1)
    taps = jnp.concatenate([conv_qk.reshape(kernel_len, 2 * qk_width), conv_v], 1)
    carried = from_behind(channels[tok_count - kernel_len + 1 :], "seq", 1)
    padded = jnp.concatenate([carried, channels], 0)
    conv_sum = padded[0:tok_count] * taps[0]
    for offset in range(1, kernel_len):
        conv_sum = conv_sum + padded[offset : offset + tok_count] * taps[offset]
    conv_out = jax.nn.silu(conv_sum)
    query_rows = jnp.repeat(
        unit_rows(conv_out[:, :qk_width].reshape(tok_count, qk_heads, key_dim)), group_size, axis=1
    ) * key_dim ** (-0.5)
    key_rows = jnp.repeat(
        unit_rows(conv_out[:, qk_width : 2 * qk_width].reshape(tok_count, qk_heads, key_dim)),
        group_size,
        axis=1,
    )
    value_rows = conv_out[:, 2 * qk_width :].reshape(tok_count, local_heads, head_dim)
    beta_rows = jax.nn.sigmoid(proj_ab[:, 0] + beta_bias)
    log_decay = -jnp.exp(a_log) * jax.nn.softplus(proj_ab[:, 1] + dt_bias)
    block_count = tok_count // SPAN
    queries = by_blocks(query_rows, SPAN)
    key_blocks = by_blocks(key_rows, SPAN)
    value_blocks = by_blocks(value_rows, SPAN)
    beta_blocks = beta_rows.reshape(block_count, SPAN, local_heads).transpose(0, 2, 1)
    gammas = jnp.cumsum(log_decay.reshape(block_count, SPAN, local_heads), axis=1).transpose(
        0, 2, 1
    )
    row_ids = lax.broadcasted_iota(jnp.int32, (SPAN, SPAN), 0)
    col_ids = lax.broadcasted_iota(jnp.int32, (SPAN, SPAN), 1)
    lower_masked = row_ids >= col_ids
    strict = row_ids > col_ids
    spread = gammas[..., :, None] - gammas[..., None, :]
    fading_quotient = jnp.where(lower_masked, jnp.exp(jnp.where(lower_masked, spread, 0.0)), 0.0)
    weighted = fading_quotient * beta_blocks[..., None, :]
    key_gram = jnp.einsum("nhik,nhjk->nhij", key_blocks, key_blocks, precision=highest_setting)
    lower = jnp.where(strict, weighted * key_gram, 0.0) + jnp.eye(SPAN, dtype=jnp.float32)
    query_key = jnp.einsum("nhik,nhjk->nhij", queries, key_blocks, precision=highest_setting)
    mixing = weighted * query_key
    growth = jnp.exp(gammas)
    growth_end = growth[..., -1]
    right_side = jnp.concatenate([growth[..., None] * key_blocks, value_blocks], -1)
    solved = jax.scipy.linalg.solve_triangular(lower, right_side, lower=True, unit_diagonal=True)
    erasers = solved[..., :key_dim]
    fresh_values = solved[..., key_dim:]
    closing = beta_blocks * jnp.exp(gammas[..., -1:] - gammas)
    keys_end = key_blocks * closing[..., None]
    identity_mat = jnp.eye(key_dim, dtype=jnp.float32)
    transfer = growth_end[..., None, None] * identity_mat - jnp.einsum(
        "nhck,nhcj->nhkj", keys_end, erasers, precision=highest_setting
    )
    offset_map = jnp.einsum("nhck,nhcv->nhkv", keys_end, fresh_values, precision=highest_setting)
    start_a = jnp.broadcast_to(identity_mat, (local_heads, key_dim, key_dim))
    start_b = jnp.zeros((local_heads, key_dim, head_dim), jnp.float32)

    def compose(carry, pieces):
        return (chain_maps(carry, pieces), carry)

    totals, prefixes = lax.scan(compose, (start_a, start_b), (transfer, offset_map))
    total_a, total_b = totals

    def relay(step_index, received_prior):
        leaving = (
            jnp.einsum("hij,hjv->hiv", total_a, received_prior, precision=highest_setting) + total_b
        )
        return from_behind(leaving, "seq", 1)

    incoming = lax.fori_loop(0, lax.axis_size("seq") - 1, relay, start_b)

    def replay(current_state, pieces):
        (
            current_eraser,
            current_fresh_values,
            current_query,
            mixing_now,
            growth_now,
            current_keys_end,
            growth_end_now,
        ) = pieces
        state_update = current_fresh_values - jnp.einsum(
            "trz,tzs->trs", current_eraser, current_state, precision=highest_setting
        )
        output = growth_now[..., None] * jnp.einsum(
            "trz,tzs->trs", current_query, current_state, precision=highest_setting
        )
        output = output + jnp.einsum(
            "hij,hjv->hiv", mixing_now, state_update, precision=highest_setting
        )
        state_next = growth_end_now[:, None, None] * current_state + jnp.einsum(
            "yfw,yfr->ywr", current_keys_end, state_update, precision=highest_setting
        )
        return (state_next, output)

    final_state, core = lax.scan(
        replay, incoming, (erasers, fresh_values, queries, mixing, growth, keys_end, growth_end)
    )
    core = core.transpose(0, 2, 1, 3).reshape(tok_count, local_heads, head_dim)
    gates = proj_vz[:, 1].reshape(tok_count, local_heads, head_dim)
    normed = (
        core
        * lax.rsqrt(jnp.mean(core * core, -1, keepdims=True) + 1e-06)
        * norm_gain
        * jax.nn.silu(gates)
    )
    normed = normed.astype(jnp.bfloat16).reshape(tok_count, local_heads * head_dim)
    local_portion = lax.psum_scatter(
        lax.dot_general(
            w_out, normed, (((0,), (1,)), ((), ())), preferred_element_type=jnp.float32
        ),
        "head",
        scatter_dimension=0,
        tiled=True,
    )
    return local_portion.T.astype(jnp.bfloat16)


def solution(mesh):
    in_specs = (
        P("seq", None),
        P(None, None, "head"),
        P(None, None, "head"),
        P(None, None, "head"),
        P(None, None, "head"),
        P(None, "head"),
        P("head"),
        P("head"),
        P("head"),
        P(),
        P("head", None),
    )
    out_specs = P("seq", "head")
    return jax.shard_map(local, mesh=mesh, in_specs=in_specs, out_specs=out_specs, check_vma=False)
```

profile of v0, /device:TPU:14, one launch (start us, length us, event | category | flops | bytes accessed | tf_op | source)
XLA Modules:
  0.0 583.3 jit_solution(9337198718888128765)
XLA Ops:
  35.7 80.0 %custom-call.4 = f32[4,4,1,64,64]{3,4,2,1,0:T(8,128)} custom-call(f32[4,4,1,64,64]{4,3,2,1,0:T(8,128)} %fusion.37), custom_call_target="InvertDiagBlocksLowerTriangular" | custom-call | tf_op jit(solution)/shard_map/jit(_solve_triangular)/vmap(vmap())/triangular_solve | solution.py:93
  126.8 11.4 %while.37 = (s32[]{:T(128)}, f32[4,128,128]{2,1,0:T(8,128)S(1)}, f32[4,128,128]{2,1,0:T(8,128)S(1)}, f32[4,4,128,128]{3,2,1,0:T(8,128)}, f32[4,4,128,128]{3,2,1,0:T(8,128)}, /*index=5*/s32[]{:T(128)}, s32[]{:T(128)}) while((s32[]{:T(128)}, f32[4,128,128]{2,1,0:T(8,128)S(1)}, f32[4,128,128]{2,1,0:T(8,128)S(1)}, ...), condition=%wide.region_3.4_spmd.clone, body=%wide.region_2.3_spmd.clone.sunk | while | flops 201457664 | bytes 2885207 | solution.py:109
  138.3 381.4 %while.35 = (s32[]{:T(128)}, f32[4,128,128]{2,1,0:T(8,128)S(1)}, f32[4,128,128]{2,1,0:T(8,128)S(1)}, f32[4,128,128]{2,1,0:T(8,128)S(1)}, s32[]{:T(128)}) while((s32[]{:T(128)}, f32[4,128,128]{2,1,0:T(8,128)S(1)}, f32[4,128,128]{2,1,0:T(8,128)S(1)}, f32[4,128,128]{2,1,0:T(8,128)S(1)}, s32[]{:T(128)}) %tuple.68), condition=%wide.region_5.6_spmd, body=%wide.region_4.5_spmd.sunk | while | flops 100728832 | bytes 2097253 | solution.py:118
  154.7 9.5 %collective-permute-done = f32[4,128,128]{2,1,0:T(8,128)S(1)} collective-permute-done((f32[4,128,128]{2,1,0:T(8,128)}, f32[4,128,128]{2,1,0:T(8,128)S(1)}, u32[]{:S(2)}, u32[]{:S(2)}) %collective-permute-start) | collective-permute-done | bytes 262176 | tf_op jit(solution)/shard_map/while/body/eval_jaxpr/ppermute | solution.py:18
  167.2 8.7 %collective-permute-done = f32[4,128,128]{2,1,0:T(8,128)S(1)} collective-permute-done((f32[4,128,128]{2,1,0:T(8,128)}, f32[4,128,128]{2,1,0:T(8,128)S(1)}, u32[]{:S(2)}, u32[]{:S(2)}) %collective-permute-start) | collective-permute-done | bytes 262176 | tf_op jit(solution)/shard_map/while/body/eval_jaxpr/ppermute | solution.py:18
  178.9 8.7 %collective-permute-done = f32[4,128,128]{2,1,0:T(8,128)S(1)} collective-permute-done((f32[4,128,128]{2,1,0:T(8,128)}, f32[4,128,128]{2,1,0:T(8,128)S(1)}, u32[]{:S(2)}, u32[]{:S(2)}) %collective-permute-start) | collective-permute-done | bytes 262176 | tf_op jit(solution)/shard_map/while/body/eval_jaxpr/ppermute | solution.py:18
  190.6 8.7 %collective-permute-done = f32[4,128,128]{2,1,0:T(8,128)S(1)} collective-permute-done((f32[4,128,128]{2,1,0:T(8,128)}, f32[4,128,128]{2,1,0:T(8,128)S(1)}, u32[]{:S(2)}, u32[]{:S(2)}) %collective-permute-start) | collective-permute-done | bytes 262176 | tf_op jit(solution)/shard_map/while/body/eval_jaxpr/ppermute | solution.py:18
  202.3 8.7 %collective-permute-done = f32[4,128,128]{2,1,0:T(8,128)S(1)} collective-permute-done((f32[4,128,128]{2,1,0:T(8,128)}, f32[4,128,128]{2,1,0:T(8,128)S(1)}, u32[]{:S(2)}, u32[]{:S(2)}) %collective-permute-start) | collective-permute-done | bytes 262176 | tf_op jit(solution)/shard_map/while/body/eval_jaxpr/ppermute | solution.py:18
  214.0 8.7 %collective-permute-done = f32[4,128,128]{2,1,0:T(8,128)S(1)} collective-permute-done((f32[4,128,128]{2,1,0:T(8,128)}, f32[4,128,128]{2,1,0:T(8,128)S(1)}, u32[]{:S(2)}, u32[]{:S(2)}) %collective-permute-start) | collective-permute-done | bytes 262176 | tf_op jit(solution)/shard_map/while/body/eval_jaxpr/ppermute | solution.py:18
  225.7 9.5 %collective-permute-done = f32[4,128,128]{2,1,0:T(8,128)S(1)} collective-permute-done((f32[4,128,128]{2,1,0:T(8,128)}, f32[4,128,128]{2,1,0:T(8,128)S(1)}, u32[]{:S(2)}, u32[]{:S(2)}) %collective-permute-start) | collective-permute-done | bytes 262176 | tf_op jit(solution)/shard_map/while/body/eval_jaxpr/ppermute | solution.py:18
  238.2 10.7 %collective-permute-done = f32[4,128,128]{2,1,0:T(8,128)S(1)} collective-permute-done((f32[4,128,128]{2,1,0:T(8,128)}, f32[4,128,128]{2,1,0:T(8,128)S(1)}, u32[]{:S(2)}, u32[]{:S(2)}) %collective-permute-start) | collective-permute-done | bytes 262176 | tf_op jit(solution)/shard_map/while/body/eval_jaxpr/ppermute | solution.py:18
  252.0 11.1 %collective-permute-done = f32[4,128,128]{2,1,0:T(8,128)S(1)} collective-permute-done((f32[4,128,128]{2,1,0:T(8,128)}, f32[4,128,128]{2,1,0:T(8,128)S(1)}, u32[]{:S(2)}, u32[]{:S(2)}) %collective-permute-start) | collective-permute-done | bytes 262176 | tf_op jit(solution)/shard_map/while/body/eval_jaxpr/ppermute | solution.py:18
  266.1 10.3 %collective-permute-done = f32[4,128,128]{2,1,0:T(8,128)S(1)} collective-permute-done((f32[4,128,128]{2,1,0:T(8,128)}, f32[4,128,128]{2,1,0:T(8,128)S(1)}, u32[]{:S(2)}, u32[]{:S(2)}) %collective-permute-start) | collective-permute-done | bytes 262176 | tf_op jit(solution)/shard_map/while/body/eval_jaxpr/ppermute | solution.py:18
  279.4 9.4 %collective-permute-done = f32[4,128,128]{2,1,0:T(8,128)S(1)} collective-permute-done((f32[4,128,128]{2,1,0:T(8,128)}, f32[4,128,128]{2,1,0:T(8,128)S(1)}, u32[]{:S(2)}, u32[]{:S(2)}) %collective-permute-start) | collective-permute-done | bytes 262176 | tf_op jit(solution)/shard_map/while/body/eval_jaxpr/ppermute | solution.py:18
  291.9 8.7 %collective-permute-done = f32[4,128,128]{2,1,0:T(8,128)S(1)} collective-permute-done((f32[4,128,128]{2,1,0:T(8,128)}, f32[4,128,128]{2,1,0:T(8,128)S(1)}, u32[]{:S(2)}, u32[]{:S(2)}) %collective-permute-start) | collective-permute-done | bytes 262176 | tf_op jit(solution)/shard_map/while/body/eval_jaxpr/ppermute | solution.py:18
  303.6 8.7 %collective-permute-done = f32[4,128,128]{2,1,0:T(8,128)S(1)} collective-permute-done((f32[4,128,128]{2,1,0:T(8,128)}, f32[4,128,128]{2,1,0:T(8,128)S(1)}, u32[]{:S(2)}, u32[]{:S(2)}) %collective-permute-start) | collective-permute-done | bytes 262176 | tf_op jit(solution)/shard_map/while/body/eval_jaxpr/ppermute | solution.py:18
  315.3 8.7 %collective-permute-done = f32[4,128,128]{2,1,0:T(8,128)S(1)} collective-permute-done((f32[4,128,128]{2,1,0:T(8,128)}, f32[4,128,128]{2,1,0:T(8,128)S(1)}, u32[]{:S(2)}, u32[]{:S(2)}) %collective-permute-start) | collective-permute-done | bytes 262176 | tf_op jit(solution)/shard_map/while/body/eval_jaxpr/ppermute | solution.py:18
  327.0 8.7 %collective-permute-done = f32[4,128,128]{2,1,0:T(8,128)S(1)} collective-permute-done((f32[4,128,128]{2,1,0:T(8,128)}, f32[4,128,128]{2,1,0:T(8,128)S(1)}, u32[]{:S(2)}, u32[]{:S(2)}) %collective-permute-start) | collective-permute-done | bytes 262176 | tf_op jit(solution)/shard_map/while/body/eval_jaxpr/ppermute | solution.py:18
  338.7 8.7 %collective-permute-done = f32[4,128,128]{2,1,0:T(8,128)S(1)} collective-permute-done((f32[4,128,128]{2,1,0:T(8,128)}, f32[4,128,128]{2,1,0:T(8,128)S(1)}, u32[]{:S(2)}, u32[]{:S(2)}) %collective-permute-start) | collective-permute-done | bytes 262176 | tf_op jit(solution)/shard_map/while/body/eval_jaxpr/ppermute | solution.py:18
  350.4 9.6 %collective-permute-done = f32[4,128,128]{2,1,0:T(8,128)S(1)} collective-permute-done((f32[4,128,128]{2,1,0:T(8,128)}, f32[4,128,128]{2,1,0:T(8,128)S(1)}, u32[]{:S(2)}, u32[]{:S(2)}) %collective-permute-start) | collective-permute-done | bytes 262176 | tf_op jit(solution)/shard_map/while/body/eval_jaxpr/ppermute | solution.py:18
  363.0 10.7 %collective-permute-done = f32[4,128,128]{2,1,0:T(8,128)S(1)} collective-permute-done((f32[4,128,128]{2,1,0:T(8,128)}, f32[4,128,128]{2,1,0:T(8,128)S(1)}, u32[]{:S(2)}, u32[]{:S(2)}) %collective-permute-start) | collective-permute-done | bytes 262176 | tf_op jit(solution)/shard_map/while/body/eval_jaxpr/ppermute | solution.py:18
  376.8 11.0 %collective-permute-done = f32[4,128,128]{2,1,0:T(8,128)S(1)} collective-permute-done((f32[4,128,128]{2,1,0:T(8,128)}, f32[4,128,128]{2,1,0:T(8,128)S(1)}, u32[]{:S(2)}, u32[]{:S(2)}) %collective-permute-start) | collective-permute-done | bytes 262176 | tf_op jit(solution)/shard_map/while/body/eval_jaxpr/ppermute | solution.py:18
  390.8 10.3 %collective-permute-done = f32[4,128,128]{2,1,0:T(8,128)S(1)} collective-permute-done((f32[4,128,128]{2,1,0:T(8,128)}, f32[4,128,128]{2,1,0:T(8,128)S(1)}, u32[]{:S(2)}, u32[]{:S(2)}) %collective-permute-start) | collective-permute-done | bytes 262176 | tf_op jit(solution)/shard_map/while/body/eval_jaxpr/ppermute | solution.py:18
  404.1 9.4 %collective-permute-done = f32[4,128,128]{2,1,0:T(8,128)S(1)} collective-permute-done((f32[4,128,128]{2,1,0:T(8,128)}, f32[4,128,128]{2,1,0:T(8,128)S(1)}, u32[]{:S(2)}, u32[]{:S(2)}) %collective-permute-start) | collective-permute-done | bytes 262176 | tf_op jit(solution)/shard_map/while/body/eval_jaxpr/ppermute | solution.py:18
  416.5 8.7 %collective-permute-done = f32[4,128,128]{2,1,0:T(8,128)S(1)} collective-permute-done((f32[4,128,128]{2,1,0:T(8,128)}, f32[4,128,128]{2,1,0:T(8,128)S(1)}, u32[]{:S(2)}, u32[]{:S(2)}) %collective-permute-start) | collective-permute-done | bytes 262176 | tf_op jit(solution)/shard_map/while/body/eval_jaxpr/ppermute | solution.py:18
  428.2 8.7 %collective-permute-done = f32[4,128,128]{2,1,0:T(8,128)S(1)} collective-permute-done((f32[4,128,128]{2,1,0:T(8,128)}, f32[4,128,128]{2,1,0:T(8,128)S(1)}, u32[]{:S(2)}, u32[]{:S(2)}) %collective-permute-start) | collective-permute-done | bytes 262176 | tf_op jit(solution)/shard_map/while/body/eval_jaxpr/ppermute | solution.py:18
  439.9 8.7 %collective-permute-done = f32[4,128,128]{2,1,0:T(8,128)S(1)} collective-permute-done((f32[4,128,128]{2,1,0:T(8,128)}, f32[4,128,128]{2,1,0:T(8,128)S(1)}, u32[]{:S(2)}, u32[]{:S(2)}) %collective-permute-start) | collective-permute-done | bytes 262176 | tf_op jit(solution)/shard_map/while/body/eval_jaxpr/ppermute | solution.py:18
  451.6 8.7 %collective-permute-done = f32[4,128,128]{2,1,0:T(8,128)S(1)} collective-permute-done((f32[4,128,128]{2,1,0:T(8,128)}, f32[4,128,128]{2,1,0:T(8,128)S(1)}, u32[]{:S(2)}, u32[]{:S(2)}) %collective-permute-start) | collective-permute-done | bytes 262176 | tf_op jit(solution)/shard_map/while/body/eval_jaxpr/ppermute | solution.py:18
  475.0 9.6 %collective-permute-done = f32[4,128,128]{2,1,0:T(8,128)S(1)} collective-permute-done((f32[4,128,128]{2,1,0:T(8,128)}, f32[4,128,128]{2,1,0:T(8,128)S(1)}, u32[]{:S(2)}, u32[]{:S(2)}) %collective-permute-start) | collective-permute-done | bytes 262176 | tf_op jit(solution)/shard_map/while/body/eval_jaxpr/ppermute | solution.py:18
  511.0 8.7 %collective-permute-done = f32[4,128,128]{2,1,0:T(8,128)S(1)} collective-permute-done((f32[4,128,128]{2,1,0:T(8,128)}, f32[4,128,128]{2,1,0:T(8,128)S(1)}, u32[]{:S(2)}, u32[]{:S(2)}) %collective-permute-start) | collective-permute-done | bytes 262176 | tf_op jit(solution)/shard_map/while/body/eval_jaxpr/ppermute | solution.py:18
  519.7 20.4 %while.36 = (s32[]{:T(128)}, f32[4,128,128]{2,1,0:T(8,128)S(1)}, f32[4,4,64,128]{3,2,1,0:T(8,128)}, f32[4,4]{1,0:T(4,128)S(1)}, f32[4,4,64,128]{3,2,1,0:T(8,128)...) while((s32[]{:T(128)}, f32[4,128,128]{2,1,0:T(8,128)S(1)}, ...), condition=%wide.region_8.9_spmd, body=%wide.region_7.8_spmd.sunk | while | flops 176390144 | bytes 2496665 | solution.py:144
  545.5 29.3 %reduce-scatter.2.cloned.1.call-done = f32[256,256]{0,1:T(8,128)} async-done(((f32[2048,256]{0,1:T(8,128)}), f32[256,256]{0,1:T(8,128)}) %reduce-scatter.2.cloned.1.call-update) | async-done | bytes 262160 | tf_op jit(solution)/shard_map/reduce_scatter | solution.py:156
  (213 shorter events, 208.6 us)
Async XLA Ops:
  6.5 568.3 %reduce-scatter.2.cloned.1.call-start = ((), (), s32[]{:S(2)}) async-start(), calls=%async_computation.1 | async-start | bytes 2359296 | tf_op jit(solution)/shard_map/reduce_scatter | solution.py:156
  14.3 11.5 %collective-permute-start.1 = (f32[3,1024]{1,0:T(4,128)}, f32[3,1024]{1,0:T(4,128)}, u32[]{:S(2)}, u32[]{:S(2)}) collective-permute-start(f32[3,1024]{1,0:T(4,128)} %fusion.64), channel_id=1, source_target_pairs={{0,8},{8,16},{16,24},{24,32},{32,40},{40,48},{48,56},{56,64},{64,7... | collective-permute-start | bytes 36872 | tf_op jit(solution)/shard_map/ppermute | solution.py:18
  139.4 12.2 %collective-permute-start = (f32[4,128,128]{2,1,0:T(8,128)}, f32[4,128,128]{2,1,0:T(8,128)S(1)}, u32[]{:S(2)}, u32[]{:S(2)}) collective-permute-start(f32[4,128,128]{2,1,0:T(8,128)} %convolution_add_fusion.6), channel_id=1, source_target_pairs={{0,8},{8,16},{16,24},{24,32},{32,40},{40,48},{48,56},{56,64},{64,7... | collective-permute-start | bytes 786440 | tf_op jit(solution)/shard_map/while/body/eval_jaxpr/ppermute | solution.py:18
  152.8 11.4 %collective-permute-start = (f32[4,128,128]{2,1,0:T(8,128)}, f32[4,128,128]{2,1,0:T(8,128)S(1)}, u32[]{:S(2)}, u32[]{:S(2)}) collective-permute-start(f32[4,128,128]{2,1,0:T(8,128)} %convolution_add_fusion.6), channel_id=1, source_target_pairs={{0,8},{8,16},{16,24},{24,32},{32,40},{40,48},{48,56},{56,64},{64,7... | collective-permute-start | bytes 786440 | tf_op jit(solution)/shard_map/while/body/eval_jaxpr/ppermute | solution.py:18
  165.3 10.6 %collective-permute-start = (f32[4,128,128]{2,1,0:T(8,128)}, f32[4,128,128]{2,1,0:T(8,128)S(1)}, u32[]{:S(2)}, u32[]{:S(2)}) collective-permute-start(f32[4,128,128]{2,1,0:T(8,128)} %convolution_add_fusion.6), channel_id=1, source_target_pairs={{0,8},{8,16},{16,24},{24,32},{32,40},{40,48},{48,56},{56,64},{64,7... | collective-permute-start | bytes 786440 | tf_op jit(solution)/shard_map/while/body/eval_jaxpr/ppermute | solution.py:18
  177.0 10.6 %collective-permute-start = (f32[4,128,128]{2,1,0:T(8,128)}, f32[4,128,128]{2,1,0:T(8,128)S(1)}, u32[]{:S(2)}, u32[]{:S(2)}) collective-permute-start(f32[4,128,128]{2,1,0:T(8,128)} %convolution_add_fusion.6), channel_id=1, source_target_pairs={{0,8},{8,16},{16,24},{24,32},{32,40},{40,48},{48,56},{56,64},{64,7... | collective-permute-start | bytes 786440 | tf_op jit(solution)/shard_map/while/body/eval_jaxpr/ppermute | solution.py:18
  188.7 10.6 %collective-permute-start = (f32[4,128,128]{2,1,0:T(8,128)}, f32[4,128,128]{2,1,0:T(8,128)S(1)}, u32[]{:S(2)}, u32[]{:S(2)}) collective-permute-start(f32[4,128,128]{2,1,0:T(8,128)} %convolution_add_fusion.6), channel_id=1, source_target_pairs={{0,8},{8,16},{16,24},{24,32},{32,40},{40,48},{48,56},{56,64},{64,7... | collective-permute-start | bytes 786440 | tf_op jit(solution)/shard_map/while/body/eval_jaxpr/ppermute | solution.py:18
  200.4 10.6 %collective-permute-start = (f32[4,128,128]{2,1,0:T(8,128)}, f32[4,128,128]{2,1,0:T(8,128)S(1)}, u32[]{:S(2)}, u32[]{:S(2)}) collective-permute-start(f32[4,128,128]{2,1,0:T(8,128)} %convolution_add_fusion.6), channel_id=1, source_target_pairs={{0,8},{8,16},{16,24},{24,32},{32,40},{40,48},{48,56},{56,64},{64,7... | collective-permute-start | bytes 786440 | tf_op jit(solution)/shard_map/while/body/eval_jaxpr/ppermute | solution.py:18
  212.1 10.6 %collective-permute-start = (f32[4,128,128]{2,1,0:T(8,128)}, f32[4,128,128]{2,1,0:T(8,128)S(1)}, u32[]{:S(2)}, u32[]{:S(2)}) collective-permute-start(f32[4,128,128]{2,1,0:T(8,128)} %convolution_add_fusion.6), channel_id=1, source_target_pairs={{0,8},{8,16},{16,24},{24,32},{32,40},{40,48},{48,56},{56,64},{64,7... | collective-permute-start | bytes 786440 | tf_op jit(solution)/shard_map/while/body/eval_jaxpr/ppermute | solution.py:18
  223.8 11.5 %collective-permute-start = (f32[4,128,128]{2,1,0:T(8,128)}, f32[4,128,128]{2,1,0:T(8,128)S(1)}, u32[]{:S(2)}, u32[]{:S(2)}) collective-permute-start(f32[4,128,128]{2,1,0:T(8,128)} %convolution_add_fusion.6), channel_id=1, source_target_pairs={{0,8},{8,16},{16,24},{24,32},{32,40},{40,48},{48,56},{56,64},{64,7... | collective-permute-start | bytes 786440 | tf_op jit(solution)/shard_map/while/body/eval_jaxpr/ppermute | solution.py:18
  236.3 12.6 %collective-permute-start = (f32[4,128,128]{2,1,0:T(8,128)}, f32[4,128,128]{2,1,0:T(8,128)S(1)}, u32[]{:S(2)}, u32[]{:S(2)}) collective-permute-start(f32[4,128,128]{2,1,0:T(8,128)} %convolution_add_fusion.6), channel_id=1, source_target_pairs={{0,8},{8,16},{16,24},{24,32},{32,40},{40,48},{48,56},{56,64},{64,7... | collective-permute-start | bytes 786440 | tf_op jit(solution)/shard_map/while/body/eval_jaxpr/ppermute | solution.py:18
  250.1 13.0 %collective-permute-start = (f32[4,128,128]{2,1,0:T(8,128)}, f32[4,128,128]{2,1,0:T(8,128)S(1)}, u32[]{:S(2)}, u32[]{:S(2)}) collective-permute-start(f32[4,128,128]{2,1,0:T(8,128)} %convolution_add_fusion.6), channel_id=1, source_target_pairs={{0,8},{8,16},{16,24},{24,32},{32,40},{40,48},{48,56},{56,64},{64,7... | collective-permute-start | bytes 786440 | tf_op jit(solution)/shard_map/while/body/eval_jaxpr/ppermute | solution.py:18
  264.2 12.2 %collective-permute-start = (f32[4,128,128]{2,1,0:T(8,128)}, f32[4,128,128]{2,1,0:T(8,128)S(1)}, u32[]{:S(2)}, u32[]{:S(2)}) collective-permute-start(f32[4,128,128]{2,1,0:T(8,128)} %convolution_add_fusion.6), channel_id=1, source_target_pairs={{0,8},{8,16},{16,24},{24,32},{32,40},{40,48},{48,56},{56,64},{64,7... | collective-permute-start | bytes 786440 | tf_op jit(solution)/shard_map/while/body/eval_jaxpr/ppermute | solution.py:18
  277.5 11.3 %collective-permute-start = (f32[4,128,128]{2,1,0:T(8,128)}, f32[4,128,128]{2,1,0:T(8,128)S(1)}, u32[]{:S(2)}, u32[]{:S(2)}) collective-permute-start(f32[4,128,128]{2,1,0:T(8,128)} %convolution_add_fusion.6), channel_id=1, source_target_pairs={{0,8},{8,16},{16,24},{24,32},{32,40},{40,48},{48,56},{56,64},{64,7... | collective-permute-start | bytes 786440 | tf_op jit(solution)/shard_map/while/body/eval_jaxpr/ppermute | solution.py:18
  290.0 10.6 %collective-permute-start = (f32[4,128,128]{2,1,0:T(8,128)}, f32[4,128,128]{2,1,0:T(8,128)S(1)}, u32[]{:S(2)}, u32[]{:S(2)}) collective-permute-start(f32[4,128,128]{2,1,0:T(8,128)} %convolution_add_fusion.6), channel_id=1, source_target_pairs={{0,8},{8,16},{16,24},{24,32},{32,40},{40,48},{48,56},{56,64},{64,7... | collective-permute-start | bytes 786440 | tf_op jit(solution)/shard_map/while/body/eval_jaxpr/ppermute | solution.py:18
  301.7 10.6 %collective-permute-start = (f32[4,128,128]{2,1,0:T(8,128)}, f32[4,128,128]{2,1,0:T(8,128)S(1)}, u32[]{:S(2)}, u32[]{:S(2)}) collective-permute-start(f32[4,128,128]{2,1,0:T(8,128)} %convolution_add_fusion.6), channel_id=1, source_target_pairs={{0,8},{8,16},{16,24},{24,32},{32,40},{40,48},{48,56},{56,64},{64,7... | collective-permute-start | bytes 786440 | tf_op jit(solution)/shard_map/while/body/eval_jaxpr/ppermute | solution.py:18
  313.4 10.6 %collective-permute-start = (f32[4,128,128]{2,1,0:T(8,128)}, f32[4,128,128]{2,1,0:T(8,128)S(1)}, u32[]{:S(2)}, u32[]{:S(2)}) collective-permute-start(f32[4,128,128]{2,1,0:T(8,128)} %convolution_add_fusion.6), channel_id=1, source_target_pairs={{0,8},{8,16},{16,24},{24,32},{32,40},{40,48},{48,56},{56,64},{64,7... | collective-permute-start | bytes 786440 | tf_op jit(solution)/shard_map/while/body/eval_jaxpr/ppermute | solution.py:18
  325.1 10.6 %collective-permute-start = (f32[4,128,128]{2,1,0:T(8,128)}, f32[4,128,128]{2,1,0:T(8,128)S(1)}, u32[]{:S(2)}, u32[]{:S(2)}) collective-permute-start(f32[4,128,128]{2,1,0:T(8,128)} %convolution_add_fusion.6), channel_id=1, source_target_pairs={{0,8},{8,16},{16,24},{24,32},{32,40},{40,48},{48,56},{56,64},{64,7... | collective-permute-start | bytes 786440 | tf_op jit(solution)/shard_map/while/body/eval_jaxpr/ppermute | solution.py:18
  336.8 10.6 %collective-permute-start = (f32[4,128,128]{2,1,0:T(8,128)}, f32[4,128,128]{2,1,0:T(8,128)S(1)}, u32[]{:S(2)}, u32[]{:S(2)}) collective-permute-start(f32[4,128,128]{2,1,0:T(8,128)} %convolution_add_fusion.6), channel_id=1, source_target_pairs={{0,8},{8,16},{16,24},{24,32},{32,40},{40,48},{48,56},{56,64},{64,7... | collective-permute-start | bytes 786440 | tf_op jit(solution)/shard_map/while/body/eval_jaxpr/ppermute | solution.py:18
  348.4 11.5 %collective-permute-start = (f32[4,128,128]{2,1,0:T(8,128)}, f32[4,128,128]{2,1,0:T(8,128)S(1)}, u32[]{:S(2)}, u32[]{:S(2)}) collective-permute-start(f32[4,128,128]{2,1,0:T(8,128)} %convolution_add_fusion.6), channel_id=1, source_target_pairs={{0,8},{8,16},{16,24},{24,32},{32,40},{40,48},{48,56},{56,64},{64,7... | collective-permute-start | bytes 786440 | tf_op jit(solution)/shard_map/while/body/eval_jaxpr/ppermute | solution.py:18
  361.1 12.7 %collective-permute-start = (f32[4,128,128]{2,1,0:T(8,128)}, f32[4,128,128]{2,1,0:T(8,128)S(1)}, u32[]{:S(2)}, u32[]{:S(2)}) collective-permute-start(f32[4,128,128]{2,1,0:T(8,128)} %convolution_add_fusion.6), channel_id=1, source_target_pairs={{0,8},{8,16},{16,24},{24,32},{32,40},{40,48},{48,56},{56,64},{64,7... | collective-permute-start | bytes 786440 | tf_op jit(solution)/shard_map/while/body/eval_jaxpr/ppermute | solution.py:18
  374.8 12.9 %collective-permute-start = (f32[4,128,128]{2,1,0:T(8,128)}, f32[4,128,128]{2,1,0:T(8,128)S(1)}, u32[]{:S(2)}, u32[]{:S(2)}) collective-permute-start(f32[4,128,128]{2,1,0:T(8,128)} %convolution_add_fusion.6), channel_id=1, source_target_pairs={{0,8},{8,16},{16,24},{24,32},{32,40},{40,48},{48,56},{56,64},{64,7... | collective-permute-start | bytes 786440 | tf_op jit(solution)/shard_map/while/body/eval_jaxpr/ppermute | solution.py:18
  388.9 12.2 %collective-permute-start = (f32[4,128,128]{2,1,0:T(8,128)}, f32[4,128,128]{2,1,0:T(8,128)S(1)}, u32[]{:S(2)}, u32[]{:S(2)}) collective-permute-start(f32[4,128,128]{2,1,0:T(8,128)} %convolution_add_fusion.6), channel_id=1, source_target_pairs={{0,8},{8,16},{16,24},{24,32},{32,40},{40,48},{48,56},{56,64},{64,7... | collective-permute-start | bytes 786440 | tf_op jit(solution)/shard_map/while/body/eval_jaxpr/ppermute | solution.py:18
  402.2 11.3 %collective-permute-start = (f32[4,128,128]{2,1,0:T(8,128)}, f32[4,128,128]{2,1,0:T(8,128)S(1)}, u32[]{:S(2)}, u32[]{:S(2)}) collective-permute-start(f32[4,128,128]{2,1,0:T(8,128)} %convolution_add_fusion.6), channel_id=1, source_target_pairs={{0,8},{8,16},{16,24},{24,32},{32,40},{40,48},{48,56},{56,64},{64,7... | collective-permute-start | bytes 786440 | tf_op jit(solution)/shard_map/while/body/eval_jaxpr/ppermute | solution.py:18
  426.3 10.6 %collective-permute-start = (f32[4,128,128]{2,1,0:T(8,128)}, f32[4,128,128]{2,1,0:T(8,128)S(1)}, u32[]{:S(2)}, u32[]{:S(2)}) collective-permute-start(f32[4,128,128]{2,1,0:T(8,128)} %convolution_add_fusion.6), channel_id=1, source_target_pairs={{0,8},{8,16},{16,24},{24,32},{32,40},{40,48},{48,56},{56,64},{64,7... | collective-permute-start | bytes 786440 | tf_op jit(solution)/shard_map/while/body/eval_jaxpr/ppermute | solution.py:18
  438.0 10.6 %collective-permute-start = (f32[4,128,128]{2,1,0:T(8,128)}, f32[4,128,128]{2,1,0:T(8,128)S(1)}, u32[]{:S(2)}, u32[]{:S(2)}) collective-permute-start(f32[4,128,128]{2,1,0:T(8,128)} %convolution_add_fusion.6), channel_id=1, source_target_pairs={{0,8},{8,16},{16,24},{24,32},{32,40},{40,48},{48,56},{56,64},{64,7... | collective-permute-start | bytes 786440 | tf_op jit(solution)/shard_map/while/body/eval_jaxpr/ppermute | solution.py:18
  449.7 10.6 %collective-permute-start = (f32[4,128,128]{2,1,0:T(8,128)}, f32[4,128,128]{2,1,0:T(8,128)S(1)}, u32[]{:S(2)}, u32[]{:S(2)}) collective-permute-start(f32[4,128,128]{2,1,0:T(8,128)} %convolution_add_fusion.6), channel_id=1, source_target_pairs={{0,8},{8,16},{16,24},{24,32},{32,40},{40,48},{48,56},{56,64},{64,7... | collective-permute-start | bytes 786440 | tf_op jit(solution)/shard_map/while/body/eval_jaxpr/ppermute | solution.py:18
  461.4 10.6 %collective-permute-start = (f32[4,128,128]{2,1,0:T(8,128)}, f32[4,128,128]{2,1,0:T(8,128)S(1)}, u32[]{:S(2)}, u32[]{:S(2)}) collective-permute-start(f32[4,128,128]{2,1,0:T(8,128)} %convolution_add_fusion.6), channel_id=1, source_target_pairs={{0,8},{8,16},{16,24},{24,32},{32,40},{40,48},{48,56},{56,64},{64,7... | collective-permute-start | bytes 786440 | tf_op jit(solution)/shard_map/while/body/eval_jaxpr/ppermute | solution.py:18
  473.1 11.5 %collective-permute-start = (f32[4,128,128]{2,1,0:T(8,128)}, f32[4,128,128]{2,1,0:T(8,128)S(1)}, u32[]{:S(2)}, u32[]{:S(2)}) collective-permute-start(f32[4,128,128]{2,1,0:T(8,128)} %convolution_add_fusion.6), channel_id=1, source_target_pairs={{0,8},{8,16},{16,24},{24,32},{32,40},{40,48},{48,56},{56,64},{64,7... | collective-permute-start | bytes 786440 | tf_op jit(solution)/shard_map/while/body/eval_jaxpr/ppermute | solution.py:18
  485.7 10.6 %collective-permute-start = (f32[4,128,128]{2,1,0:T(8,128)}, f32[4,128,128]{2,1,0:T(8,128)S(1)}, u32[]{:S(2)}, u32[]{:S(2)}) collective-permute-start(f32[4,128,128]{2,1,0:T(8,128)} %convolution_add_fusion.6), channel_id=1, source_target_pairs={{0,8},{8,16},{16,24},{24,32},{32,40},{40,48},{48,56},{56,64},{64,7... | collective-permute-start | bytes 786440 | tf_op jit(solution)/shard_map/while/body/eval_jaxpr/ppermute | solution.py:18
  497.4 10.6 %collective-permute-start = (f32[4,128,128]{2,1,0:T(8,128)}, f32[4,128,128]{2,1,0:T(8,128)S(1)}, u32[]{:S(2)}, u32[]{:S(2)}) collective-permute-start(f32[4,128,128]{2,1,0:T(8,128)} %convolution_add_fusion.6), channel_id=1, source_target_pairs={{0,8},{8,16},{16,24},{24,32},{32,40},{40,48},{48,56},{56,64},{64,7... | collective-permute-start | bytes 786440 | tf_op jit(solution)/shard_map/while/body/eval_jaxpr/ppermute | solution.py:18
  509.1 10.6 %collective-permute-start = (f32[4,128,128]{2,1,0:T(8,128)}, f32[4,128,128]{2,1,0:T(8,128)S(1)}, u32[]{:S(2)}, u32[]{:S(2)}) collective-permute-start(f32[4,128,128]{2,1,0:T(8,128)} %convolution_add_fusion.6), channel_id=1, source_target_pairs={{0,8},{8,16},{16,24},{24,32},{32,40},{40,48},{48,56},{56,64},{64,7... | collective-permute-start | bytes 786440 | tf_op jit(solution)/shard_map/while/body/eval_jaxpr/ppermute | solution.py:18
  (21 other events, 714.4 us)
Sparse Core Ops, SparseCore 0:
  545.6 29.1 reduce-scatter.1
where the time goes:
time: 588 us; the launch traced here: 583 us
  waiting for transfers between devices  315 us (54%)
  other arithmetic  91 us (15%)
  matrix products  86.9 us (15%)
  starting transfers between devices  64.9 us (11%)
  between operations  13.8 us (2%)
  local copies, waits for them, and re-layouts  11.4 us (2%)
    ppermute x32, waiting for transfers between devices, from_behind(): return lax.ppermute(block, axis, route)  285 us
    another operation x4, other arithmetic, local(): jax.scipy.linalg.solve_triangular(lower, right_side, lower=True, unit_dia...  82 us
    ppermute x32, starting transfers between devices, from_behind(): return lax.ppermute(block, axis, route)  64.9 us
    dot_general x31, matrix products, relay(): jnp.einsum('hij,hjv->hiv', total_a, received_prior, precision=highest_set...  34.7 us
    reduce_scatter x1, waiting for transfers between devices, local(): lax.psum_scatter(lax.dot_general(w_out, normed, (((0,), (1,)), ((), ())),...  29.3 us
  transfers between devices with their start and end apart: 33, of which 32 were waited for; matrix products, arithmetic and copies ran while one was open for 1% of the time, Pallas kernels for 0%

commit v1 on v0

v1 whole, which is shorter than its diff:
```python
import functools

import jax
import jax.numpy as jnp
from jax import lax
from jax.experimental import pallas as pl
from jax.experimental.pallas import tpu as pltpu
from jax.sharding import Mesh, PartitionSpec as P

F32 = jnp.float32
BF16 = jnp.bfloat16
DK = 128
DV = 128
HALF = 128
SEG = 256
VH = 4
QKH = 2
EPS = 1e-06
FLOOR = -110.0

VMEM = pl.BlockSpec(memory_space=pltpu.VMEM)
SMEM = pl.BlockSpec(memory_space=pltpu.SMEM)


def params(mib):
    return pltpu.CompilerParams(vmem_limit_bytes=mib * 1024 * 1024)


def split2(x):
    hi = x.astype(BF16)
    return hi, (x - hi.astype(F32)).astype(BF16)


def split3(x):
    hi = x.astype(BF16)
    rest = x - hi.astype(F32)
    mid = rest.astype(BF16)
    return hi, mid, (rest - mid.astype(F32)).astype(BF16)


def mm(a, b):
    return jnp.dot(a, b, preferred_element_type=F32)


def mm_nt(a, b):
    return lax.dot_general(a, b, (((1,), (1,)), ((), ())), preferred_element_type=F32)


def dot3(a, b):
    ah, al = split2(a)
    bh, bl = split2(b)
    return mm(jnp.concatenate([ah, al, ah], 1), jnp.concatenate([bh, bh, bl], 0))


def dot3_nt(a, b):
    ah, al = split2(a)
    bh, bl = split2(b)
    return mm_nt(jnp.concatenate([ah, al, ah], 1), jnp.concatenate([bh, bh, bl], 1))


def spread_blocks(x):
    zero = jnp.zeros((HALF, HALF), x.dtype)
    return jnp.concatenate(
        [
            jnp.concatenate([x[:, :HALF], zero], 1),
            jnp.concatenate([zero, x[:, HALF:]], 1),
        ],
        0,
    )


def dot3_blocks(a, b):
    ah, al = split2(a)
    bh, bl = split2(b)
    bh, bl = spread_blocks(bh), spread_blocks(bl)
    return mm(jnp.concatenate([ah, al, ah], 1), jnp.concatenate([bh, bh, bl], 0))


def iota2(shape, dim):
    return lax.broadcasted_iota(jnp.int32, shape, dim)


def silu(x):
    return x / (1.0 + jnp.exp(-x))


def softplus(x):
    return jnp.maximum(x, 0.0) + jnp.log1p(jnp.exp(-jnp.abs(x)))


def unit(x):
    return x * lax.rsqrt(jnp.sum(x * x, -1, keepdims=True) + EPS)


def fades(decay_col, lower):
    rows, cols = iota2((SEG, SEG), 0), iota2((SEG, SEG), 1)
    terms = jnp.where(rows > cols, jnp.broadcast_to(decay_col, (SEG, SEG)), 0.0)
    hi, mid, lo = split3(terms)
    return jnp.exp(mm(lower, hi) + mm(lower, mid) + mm(lower, lo))


def lower_ones():
    rows, cols = iota2((SEG, SEG), 0), iota2((SEG, SEG), 1)
    return jnp.where(rows >= cols, 1.0, 0.0).astype(BF16)


def segment_kernel(
    place, a_log, dt_bias, beta_bias, qk, vz, halo, taps_qk, taps_v, ab,
    out0, out1, out2, out3, q_out, k_out, ef_out, cols_out,
    pad, maps,
):
    rows, cols = iota2((SEG, SEG), 0), iota2((SEG, SEG), 1)
    pad[0:8, :] = halo[...]
    pad[8:, 0:256] = qk[0]
    pad[8:, 256:512] = qk[1]
    pad[8:, 512:1024] = vz[0]

    def conv(start, width, tap):
        total = None
        for j in range(4):
            term = pad[5 + j : 5 + j + SEG, start : start + width] * tap(j)
            total = term if total is None else total + term
        return silu(total)

    head_rows = []
    for h in range(VH):
        head_rows.append(jax.nn.sigmoid(ab[0, h : h + 1, :] + beta_bias[h]))
    for h in range(VH):
        rate = jnp.exp(jnp.full((1, SEG), a_log[h], F32))
        head_rows.append(
            jnp.maximum(-rate * softplus(ab[1, h : h + 1, :] + dt_bias[h]), FLOOR)
        )
    col8 = jnp.concatenate(head_rows, 0).T
    cols_out[...] = col8
    lower = lower_ones()
    later = jnp.where(rows < cols, 1.0, 0.0).astype(BF16)
    dhi, dmid, dlo = split3(col8)
    growth8 = jnp.exp(mm(lower, dhi) + mm(lower, dmid) + mm(lower, dlo))
    closing8 = jnp.exp(mm(later, dhi) + mm(later, dmid) + mm(later, dlo))

    prow, pcol = iota2((HALF, SEG), 0), iota2((HALF, SEG), 1) & (HALF - 1)
    strict_pair = prow > pcol
    eye_pair = jnp.where(prow == pcol, 1.0, 0.0)
    eye = jnp.where(iota2((DK, DK), 0) == iota2((DK, DK), 1), 1.0, 0.0)

    for g in range(QKH):
        q = unit(conv(g * DK, DK, lambda j: taps_qk[j, 0:1, g * DK : (g + 1) * DK])) * DK ** -0.5
        k = unit(conv(256 + g * DK, DK, lambda j: taps_qk[j, 1:2, g * DK : (g + 1) * DK]))
        q_out[g] = q
        k_out[g] = k
        kk = dot3_nt(k, k)
        for h in (2 * g, 2 * g + 1):
            v = conv(512 + h * DV, DV, lambda j: taps_v[j : j + 1, h * DV : (h + 1) * DV])
            beta = col8[:, h : h + 1]
            growth = growth8[:, VH + h : VH + h + 1]
            closing = closing8[:, VH + h : VH + h + 1]
            weighted = fades(col8[:, VH + h : VH + h + 1], lower) * kk * beta
            m = jnp.concatenate([weighted[:HALF, :HALF], weighted[HALF:, HALF:]], 1)
            m = jnp.where(strict_pair, m, 0.0)
            corner = weighted[HALF:, :HALF]
            t = eye_pair - jnp.where((prow ^ pcol) == 1, m, 0.0)
            for level in range(1, 7):
                part = jnp.where(((prow >> level) ^ (pcol >> level)) == 1, m, 0.0)
                t = t - dot3_blocks(t, dot3_blocks(part, t))
            right = jnp.concatenate([k * growth, v], 1) * beta
            x1 = dot3(t[:, :HALF], right[:HALF])
            x2 = dot3(t[:, HALF:], right[HALF:] - dot3(corner, x1))
            ef = jnp.concatenate([x1, x2], 0)
            ef_out[h] = ef
            both = dot3((k * closing).T, ef)
            maps[h] = jnp.concatenate(
                [growth[SEG - 1 : SEG] * eye - both[:, :DK], both[:, DK:]], 1
            )
    mine = place[0]
    for slot, out in enumerate((out0, out1, out2, out3)):
        out[...] = maps[mine ^ slot]


def reply_kernel(q_in, k_in, ef, cols8, out):
    rows, cols = iota2((SEG, SEG), 0), iota2((SEG, SEG), 1)
    lower = lower_ones()
    col8 = cols8[...]
    dhi, dmid, dlo = split3(col8)
    growth8 = jnp.exp(mm(lower, dhi) + mm(lower, dmid) + mm(lower, dlo))
    for g in range(QKH):
        q = q_in[g]
        qk = dot3_nt(q, k_in[g])
        for h in (2 * g, 2 * g + 1):
            fade = fades(col8[:, VH + h : VH + h + 1], lower)
            mixing = jnp.where(rows >= cols, fade * qk, 0.0)
            both = dot3(mixing, ef[h])
            out[h] = jnp.concatenate(
                [q * growth8[:, VH + h : VH + h + 1] - both[:, :DK], both[:, DK:]], 1
            )


def after(second, first):
    prod = dot3(second[:, :DK], first)
    return jnp.concatenate([prod[:, :DK], prod[:, DK:] + second[:, DK:]], 1)


def quad_kernel(place, r0, r1, r2, r3, total, prefixes, maps):
    mine = place[0]
    for slot, r in enumerate((r0, r1, r2, r3)):
        maps[mine ^ slot] = r[...]
    first = maps[0]
    pair = after(maps[1], first)
    total[...] = after(after(maps[3], maps[2]), pair)
    prefixes[0] = first
    prefixes[1] = pair
    prefixes[2] = after(maps[2], pair)


def row_kernel(place, own, other, out):
    behind = place[1] == 1
    first = jnp.where(behind, other[...], own[...])
    second = jnp.where(behind, own[...], other[...])
    out[...] = after(second, first)


def state_kernel(place, y1, y2, y3, other, prefixes, out0, out1, out2, out3, states):
    s = y3[:, DK:]
    s = dot3(y2[:, :DK], s) + y2[:, DK:]
    s = dot3(y1[:, :DK], s) + y1[:, DK:]
    s = jnp.where(place[1] == 1, dot3(other[:, :DK], s) + other[:, DK:], s)
    states[0] = s
    for j in range(3):
        states[j + 1] = dot3(prefixes[j, :, :DK], s) + prefixes[j, :, DK:]
    mine = place[0]
    for slot, out in enumerate((out0, out1, out2, out3)):
        out[...] = states[mine ^ slot]


def normed_kernel(place, r0, r1, r2, r3, reply, vz, gain, w_out, normed, out, states):
    mine = place[0]
    for slot, r in enumerate((r0, r1, r2, r3)):
        states[mine ^ slot] = r[...]
    for h in range(VH):
        core = dot3(reply[h, :, :DK], states[h]) + reply[h, :, DK:]
        z = vz[1, :, h * DV : (h + 1) * DV]
        scale = lax.rsqrt(jnp.mean(core * core, -1, keepdims=True) + EPS)
        normed[:, h * DV : (h + 1) * DV] = (core * scale * gain[...] * silu(z)).astype(BF16)
    product_blocks(place[2], 1 - place[3], normed, w_out, out)


def product_blocks(x, core, normed, w_out, out):
    for r in range(4):
        start = pl.multiple_of((((x + r) & 3) * 2 + core) * 256, 256)
        out[r] = mm(normed[...], w_out[:, pl.ds(start, 256)])


def own_kernel(place, normed, w_out, out):
    product_blocks(place[2], place[3], normed, w_out, out)


def arr(*shape, dtype=F32):
    return jax.ShapeDtypeStruct(shape, dtype)


def swap(v, axis, size, mask):
    return lax.ppermute(v, axis, [(i, i ^ mask) for i in range(size)])


def shift(v, axis, size, step):
    return lax.ppermute(v, axis, [(i, (i + step) % size) for i in range(size)])


def forward(v, axis, size, step):
    return lax.ppermute(v, axis, [(i, i + step) for i in range(size - step)])


def local(tokens, w_qk, w_vz, w_ab, conv_qk, conv_v, a_log, dt_bias, beta_bias, norm_gain, w_out):
    y, z = lax.axis_index("y"), lax.axis_index("z")
    x, core = lax.axis_index("x"), lax.axis_index("core")
    place = jnp.stack([z & 3, z >> 2, x, core]).astype(jnp.int32)

    qk = jnp.einsum("td,dcf->ctf", tokens, w_qk, preferred_element_type=F32)
    vz = jnp.einsum("td,dcf->ctf", tokens, w_vz, preferred_element_type=F32)
    ab = jnp.einsum("td,dcf->cft", tokens, w_ab, preferred_element_type=F32)
    tail = jnp.concatenate([qk[0, SEG - 8 :], qk[1, SEG - 8 :], vz[0, SEG - 8 :]], 1)
    halo = lax.ppermute(tail, ("y", "z"), [(i, i + 1) for i in range(31)])

    seg = pl.pallas_call(
        segment_kernel,
        out_shape=[arr(DK, 256)] * 4
        + [arr(QKH, SEG, DK), arr(QKH, SEG, DK), arr(VH, SEG, 256), arr(SEG, 8)],
        in_specs=[SMEM] * 4 + [VMEM] * 6,
        out_specs=[VMEM] * 8,
        scratch_shapes=[pltpu.VMEM((SEG + 8, 1024), F32), pltpu.VMEM((VH, DK, 256), F32)],
        compiler_params=params(24),
        cost_estimate=pl.CostEstimate(flops=6 * 10**9, bytes_accessed=6 * 10**6, transcendentals=0),
        name="segment",
    )(place, a_log, dt_bias, beta_bias, qk, vz, halo, conv_qk, conv_v, ab)
    maps, (q, k, ef, cols8) = seg[:4], seg[4:]

    got = [maps[0]] + [swap(maps[m], "z", 8, m) for m in (1, 2, 3)]
    reply = pl.pallas_call(
        reply_kernel,
        out_shape=arr(VH, SEG, 256),
        in_specs=[VMEM] * 4,
        out_specs=VMEM,
        compiler_params=params(24),
        cost_estimate=pl.CostEstimate(flops=2 * 10**9, bytes_accessed=3 * 10**6, transcendentals=0),
        name="reply",
    )(q, k, ef, cols8)

    total, prefixes = pl.pallas_call(
        quad_kernel,
        out_shape=[arr(DK, 256), arr(3, DK, 256)],
        in_specs=[SMEM] + [VMEM] * 4,
        out_specs=[VMEM] * 2,
        scratch_shapes=[pltpu.VMEM((4, DK, 256), F32)],
        compiler_params=params(16),
        name="quad",
    )(place, *got)
    other = swap(total, "z", 8, 4)
    row = pl.pallas_call(
        row_kernel,
        out_shape=arr(DK, 256),
        in_specs=[SMEM] + [VMEM] * 2,
        out_specs=VMEM,
        compiler_params=params(16),
        name="row",
    )(place, total, other)
    rows = [forward(row, "y", 4, d) for d in (1, 2, 3)]
    states = pl.pallas_call(
        state_kernel,
        out_shape=[arr(DK, DV)] * 4,
        in_specs=[SMEM] + [VMEM] * 5,
        out_specs=[VMEM] * 4,
        scratch_shapes=[pltpu.VMEM((4, DK, DV), F32)],
        compiler_params=params(16),
        name="state",
    )(place, *rows, other, prefixes)
    came = [states[0]] + [swap(states[m], "z", 8, m) for m in (1, 2, 3)]

    normed, for_twin = pl.pallas_call(
        normed_kernel,
        out_shape=[arr(SEG, VH * DV, dtype=BF16), arr(4, SEG, 256)],
        in_specs=[SMEM] + [VMEM] * 8,
        out_specs=[VMEM] * 2,
        scratch_shapes=[pltpu.VMEM((4, DK, DV), F32)],
        compiler_params=params(24),
        name="normed",
    )(place, *came, reply, vz, norm_gain.reshape(1, DV), w_out)
    from_twin = swap(for_twin, "core", 2, 1)
    own = pl.pallas_call(
        own_kernel,
        out_shape=arr(4, SEG, 256),
        in_specs=[SMEM] + [VMEM] * 2,
        out_specs=VMEM,
        compiler_params=params(24),
        cost_estimate=pl.CostEstimate(flops=10**9, bytes_accessed=3 * 10**6, transcendentals=0),
        name="own",
    )(place, normed, w_out)

    far = own[2] + from_twin[2]
    from_left = shift(far[:HALF], "x", 4, 1)
    from_right = shift(far[HALF:], "x", 4, -1)
    chip = own + from_twin
    to_right = jnp.concatenate([chip[1, :HALF] + from_left, chip[1, HALF:]], 0)
    to_left = jnp.concatenate([chip[3, :HALF], chip[3, HALF:] + from_right], 0)
    last_left = shift(to_right, "x", 4, 1)
    last_right = shift(to_left, "x", 4, -1)
    return (chip[0] + (last_left + last_right)).astype(BF16)


def solution(mesh):
    split = Mesh(mesh.devices.reshape(4, 8, 4, 2), ("y", "z", "x", "core"))
    seq, head = ("y", "z"), ("x", "core")
    in_specs = (
        P(seq, None),
        P(None, None, head),
        P(None, None, head),
        P(None, None, head),
        P(None, None, head),
        P(None, head),
        P(head),
        P(head),
        P(head),
        P(),
        P(head, None),
    )
    return jax.shard_map(
        local, mesh=split, in_specs=in_specs, out_specs=P(seq, head), check_vma=False
    )
```

time: 588 us -> 105 us (0.18)
  waiting for transfers between devices: 315 us -> 38.4 us
  other arithmetic: 91 us -> 1.03 us
  matrix products: 86.9 us -> 7.02 us
  starting transfers between devices: 64.9 us -> 31.5 us
  Pallas kernels: 0 us -> 23.5 us
  between operations: 13.8 us -> 0.3 us
  local copies, waits for them, and re-layouts: 11.4 us -> 3.49 us
    ppermute x32 -> x16, waiting for transfers between devices: 285 us -> 38.4 us  [the longest x8 18 us: swap(): return lax.ppermute(v, axis, [(i, i ^ mask) for i in range(size)])]
    another operation x5 -> x1, other arithmetic: 82.1 us -> 0.08 us  [local(): place = jnp.stack([z & 3, z >> 2, x, core]).astype(jnp.int32)]
    dot_general x63 -> x3, matrix products: 84.6 us -> 7.02 us  [the longest x1 3.48 us: local(): vz = jnp.einsum('td,dcf->ctf', tokens, w_vz, preferred_element_type=F32)]
    ppermute x32 -> x16, starting transfers between devices: 64.9 us -> 31.5 us  [the longest x8 13.5 us: swap(): return lax.ppermute(v, axis, [(i, i ^ mask) for i in range(size)])]
    reduce_scatter x1 -> x0, waiting for transfers between devices: 29.3 us -> none  [local(): lax.psum_scatter(lax.dot_general(w_out, normed, (((0,), (1,)), ((), ())),...]
    pallas_call x0 -> x7, Pallas kernels: none -> 23.5 us  [the longest x1 16.3 us: local(): pl.pallas_call(segment_kernel, out_shape=[arr(DK, 256)] * 4 + [arr(QKH, S...]
  transfers between devices with their start and end apart: 33 -> 16, of which waited for: 32 -> 12; matrix products, arithmetic and copies ran while one was open for 1% -> 2% of each run, Pallas kernels for 0% -> 3%
where the time goes in v1:
time: 105 us
  waiting for transfers between devices  38.4 us (37%)
  starting transfers between devices  31.5 us (30%)
  Pallas kernels  23.5 us (22%)
  matrix products  7.02 us (7%)
  local copies, waits for them, and re-layouts  3.49 us (3%)
    ppermute x8, waiting for transfers between devices, swap(): return lax.ppermute(v, axis, [(i, i ^ mask) for i in range(size)])  18 us
    pallas_call x1, Pallas kernels, local(): pl.pallas_call(segment_kernel, out_shape=[arr(DK, 256)] * 4 + [arr(QKH, S...  16.3 us
    ppermute x8, starting transfers between devices, swap(): return lax.ppermute(v, axis, [(i, i ^ mask) for i in range(size)])  13.5 us
    ppermute x4, waiting for transfers between devices, shift(): return lax.ppermute(v, axis, [(i, (i + step) % size) for i in range(size)])  11.5 us
    ppermute x3, starting transfers between devices, forward(): return lax.ppermute(v, axis, [(i, i + step) for i in range(size - step)])  7.72 us
    ppermute x4, starting transfers between devices, shift(): return lax.ppermute(v, axis, [(i, (i + step) % size) for i in range(size)])  6.43 us
    ppermute x3, waiting for transfers between devices, forward(): return lax.ppermute(v, axis, [(i, i + step) for i in range(size - step)])  4.92 us
    ppermute x1, waiting for transfers between devices, local(): halo = lax.ppermute(tail, ('y', 'z'), [(i, i + 1) for i in range(31)])  3.99 us
  transfers between devices with their start and end apart: 16, of which 12 were waited for; matrix products, arithmetic and copies ran while one was open for 2% of the time, Pallas kernels for 3%

profile of v1, /device:TPU:14, one launch (start us, length us, event | category | flops | bytes accessed | tf_op | source)
XLA Modules:
  0.0 105.2 jit_solution(3170346100813722262)
XLA Ops:
  0.0 1.6 %copy-done = bf16[2048,2,256]{2,1,0:T(2,128)(2,1)S(1)} copy-done((bf16[2048,2,256]{2,1,0:T(2,128)(2,1)S(1)}, bf16[2048,2,256]{2,1,0:T(2,128)(2,1)}, u32[]{:S(2)}) %copy-start) | copy-done | bytes 2097176
  1.6 1.9 %fusion.7.qk = f32[2,256,256]{2,1,0:T(8,128)S(1)} fusion(bf16[2048,2,256]{2,1,0:T(2,128)(2,1)S(1)} %copy-done, bf16[256,2048]{1,0:T(8,128)(2,1)} %param.11), kind=kOutput, calls=%fused_computation.5 | convolution fusion | flops 536870912 | bytes 3670016 | tf_op jit(solution)/shard_map/td,dcf->ctf/dot_general | solution.py:277
  4.4 3.5 %fusion.4.vz = f32[2,256,512]{2,1,0:T(8,128)S(1)} fusion(bf16[2048,2,512]{2,1,0:T(2,128)(2,1)} %param.13, bf16[256,2048]{1,0:T(8,128)(2,1)S(1)} %copy-done.10), kind=kOutput, calls=%fused_computation.4 | convolution fusion | flops 1073741824 | bytes 6291456 | tf_op jit(solution)/shard_map/td,dcf->ctf/dot_general | solution.py:278
  7.9 3.8 %collective-permute-start = (f32[8,1024]{1,0:T(8,128)S(1)}, f32[8,1024]{1,0:T(8,128)S(1)}, u32[]{:S(2)}, u32[]{:S(2)}) collective-permute-start(f32[8,1024]{1,0:T(8,128)S(1)} %pad_maximum_fusion.2), channel_id=1, source_target_pairs={{0,8},{8,16},{16,24},{24,32},{32,40},{40,48},{48,56},{56,64},{64,7... | collective-permute-start | bytes 98312 | tf_op jit(solution)/shard_map/ppermute | solution.py:281
  11.7 1.6 %fusion.10.ab = f32[2,4,256]{2,1,0:T(4,128)S(1)} fusion(bf16[2048,2,4]{0,2,1:T(4,128)(2,1)S(1)} %copy-done.11, bf16[256,2048]{1,0:T(8,128)(2,1)} %param.11), kind=kOutput, calls=%fused_computation.6 | convolution fusion | flops 8388608 | bytes 1089536 | tf_op jit(solution)/shard_map/td,dcf->cft/dot_general | solution.py:279
  13.4 4.0 %collective-permute-done.halo = f32[8,1024]{1,0:T(8,128)S(1)} collective-permute-done((f32[8,1024]{1,0:T(8,128)S(1)}, f32[8,1024]{1,0:T(8,128)S(1)}, u32[]{:S(2)}, u32[]{:S(2)}) %collective-permute-start) | collective-permute-done | bytes 32800 | tf_op jit(solution)/shard_map/ppermute | solution.py:281
  17.5 1.0 copy-done.4
  18.5 16.3 %segment.1 = (f32[128,256]{1,0:T(8,128)S(1)}, f32[128,256]{1,0:T(8,128)S(1)}, f32[128,256]{1,0:T(8,128)S(1)}, f32[128,256]{1,0:T(8,128)S(1)}, f32[2,256,128]{2,1...) custom-call(s32[4]{0:T(128)S(1)} %pad_add_fusion.place, ...), custom_call_target="tpu_custom_call" | custom-call | flops 6000000000 | bytes 6000000 | tf_op jit(solution)/shard_map/segment/pallas_call | solution.py:283
  34.9 2.4 %collective-permute-start.2 = (f32[128,256]{1,0:T(8,128)S(1)}, f32[128,256]{1,0:T(8,128)S(1)}, u32[]{:S(2)}, u32[]{:S(2)}) collective-permute-start(f32[128,256]{1,0:T(8,128)S(1)} %get-tuple-element.23), channel_id=1, source_target_pairs={{0,16},{8,24},{16,0},{24,8},{32,48},{40,56},{48,32},{56,40},{1,17}... | collective-permute-start | bytes 393224 | tf_op jit(solution)/shard_map/ppermute | solution.py:261
  37.3 2.0 %collective-permute-start.3 = (f32[128,256]{1,0:T(8,128)S(1)}, f32[128,256]{1,0:T(8,128)S(1)}, u32[]{:S(2)}, u32[]{:S(2)}) collective-permute-start(f32[128,256]{1,0:T(8,128)S(1)} %get-tuple-element.24), channel_id=1, source_target_pairs={{0,24},{8,16},{16,8},{24,0},{32,56},{40,48},{48,40},{56,32},{1,25}... | collective-permute-start | bytes 393224 | tf_op jit(solution)/shard_map/ppermute | solution.py:261
  39.2 1.7 %collective-permute-done.1.r1 = f32[128,256]{1,0:T(8,128)S(1)} collective-permute-done((f32[128,256]{1,0:T(8,128)S(1)}, f32[128,256]{1,0:T(8,128)S(1)}, u32[]{:S(2)}, u32[]{:S(2)}) %collective-permute-start.1) | collective-permute-done | bytes 131104 | tf_op jit(solution)/shard_map/ppermute | solution.py:261
  41.0 6.3 %collective-permute-done.2.r2 = f32[128,256]{1,0:T(8,128)S(1)} collective-permute-done((f32[128,256]{1,0:T(8,128)S(1)}, f32[128,256]{1,0:T(8,128)S(1)}, u32[]{:S(2)}, u32[]{:S(2)}) %collective-permute-start.2) | collective-permute-done | bytes 131104 | tf_op jit(solution)/shard_map/ppermute | solution.py:261
  47.3 1.0 quad.1
  48.3 4.5 %collective-permute-start.4 = (f32[128,256]{1,0:T(8,128)S(1)}, f32[128,256]{1,0:T(8,128)S(1)}, u32[]{:S(2)}, u32[]{:S(2)}) collective-permute-start(f32[128,256]{1,0:T(8,128)S(1)} %get-tuple-element.25.own), channel_id=1, source_target_pairs={{0,32},{8,40},{16,48},{24,56},{32,0},{40,8},{48,16},{56,24},{1,33}... | collective-permute-start | bytes 393224 | tf_op jit(solution)/shard_map/ppermute | solution.py:261
  52.8 5.9 %collective-permute-done.4.other = f32[128,256]{1,0:T(8,128)S(1)} collective-permute-done((f32[128,256]{1,0:T(8,128)S(1)}, f32[128,256]{1,0:T(8,128)S(1)}, u32[]{:S(2)}, u32[]{:S(2)}) %collective-permute-start.4) | collective-permute-done | bytes 131104 | tf_op jit(solution)/shard_map/ppermute | solution.py:261
  60.1 5.1 %collective-permute-start.6 = (f32[128,256]{1,0:T(8,128)S(1)}, f32[128,256]{1,0:T(8,128)S(1)}, u32[]{:S(2)}, u32[]{:S(2)}) collective-permute-start(f32[128,256]{1,0:T(8,128)S(1)} %row.1), channel_id=1, source_target_pairs={{0,128},{64,192},{1,129},{65,193},{2,130},{66,194},{3,131},{67,195... | collective-permute-start | bytes 393224 | tf_op jit(solution)/shard_map/ppermute | solution.py:269
  65.2 1.9 %collective-permute-start.5 = (f32[128,256]{1,0:T(8,128)S(1)}, f32[128,256]{1,0:T(8,128)S(1)}, u32[]{:S(2)}, u32[]{:S(2)}) collective-permute-start(f32[128,256]{1,0:T(8,128)S(1)} %row.1), channel_id=1, source_target_pairs={{0,64},{64,128},{128,192},{1,65},{65,129},{129,193},{2,66},{66,130... | collective-permute-start | bytes 393224 | tf_op jit(solution)/shard_map/ppermute | solution.py:269
  67.7 4.4 %collective-permute-done.5.y1 = f32[128,256]{1,0:T(8,128)S(1)} collective-permute-done((f32[128,256]{1,0:T(8,128)S(1)}, f32[128,256]{1,0:T(8,128)S(1)}, u32[]{:S(2)}, u32[]{:S(2)}) %collective-permute-start.5) | collective-permute-done | bytes 131104 | tf_op jit(solution)/shard_map/ppermute | solution.py:269
  72.1 1.3 %state.1 = (f32[128,128]{1,0:T(8,128)S(1)}, f32[128,128]{1,0:T(8,128)S(1)}, f32[128,128]{1,0:T(8,128)S(1)}, f32[128,128]{1,0:T(8,128)S(1)}) custom-call(s32[4]{0:T(128)S(1)} %pad_add_fusion.place, f32[128,256]{1,0:T(8,128)S(1)} %collective-permute-done.5.y1, f32[128,256]{1,0:T(8,128)S(1)} %collective-permute-done.6.y2, ...), custom_call_target="tpu_custom_call" | custom-call | tf_op jit(solution)/shard_map/state/pallas_call | solution.py:326
  73.4 1.4 %collective-permute-start.8 = (f32[128,128]{1,0:T(8,128)S(1)}, f32[128,128]{1,0:T(8,128)S(1)}, u32[]{:S(2)}, u32[]{:S(2)}) collective-permute-start(f32[128,128]{1,0:T(8,128)S(1)} %get-tuple-element.28), channel_id=1, source_target_pairs={{0,8},{8,0},{16,24},{24,16},{32,40},{40,32},{48,56},{56,48},{1,9},... | collective-permute-start | bytes 196616 | tf_op jit(solution)/shard_map/ppermute | solution.py:261
  74.8 1.2 %collective-permute-start.9 = (f32[128,128]{1,0:T(8,128)S(1)}, f32[128,128]{1,0:T(8,128)S(1)}, u32[]{:S(2)}, u32[]{:S(2)}) collective-permute-start(f32[128,128]{1,0:T(8,128)S(1)} %get-tuple-element.29), channel_id=1, source_target_pairs={{0,16},{8,24},{16,0},{24,8},{32,48},{40,56},{48,32},{56,40},{1,17}... | collective-permute-start | bytes 196616 | tf_op jit(solution)/shard_map/ppermute | solution.py:261
  76.0 1.9 %collective-permute-start.10 = (f32[128,128]{1,0:T(8,128)S(1)}, f32[128,128]{1,0:T(8,128)S(1)}, u32[]{:S(2)}, u32[]{:S(2)}) collective-permute-start(f32[128,128]{1,0:T(8,128)S(1)} %get-tuple-element.30), channel_id=1, source_target_pairs={{0,24},{8,16},{16,8},{24,0},{32,56},{40,48},{48,40},{56,32},{1,25}... | collective-permute-start | bytes 196616 | tf_op jit(solution)/shard_map/ppermute | solution.py:261
  77.9 1.7 %reply.1 = f32[4,256,256]{2,1,0:T(8,128)S(1)} custom-call(f32[2,256,128]{2,1,0:T(8,128)S(1)} %get-tuple-element.31.q_in, f32[2,256,128]{2,1,0:T(8,128)S(1)} %get-tuple-element.32.k_in, f32[4,256,256]{2,1,0:T(8,128)S(1)} %get-tuple-element.33.ef, f32[256,8]{1,0:T(8,128)S(1)} %get-tuple-element.34.cols8), custom_call_target="tpu_custom_call" | custom-call | flops 2000000000 | bytes 3000000 | tf_op jit(solution)/shard_map/reply/pallas_call | solution.py:297
  79.6 1.1 %collective-permute-done.9.r2 = f32[128,128]{1,0:T(8,128)S(1)} collective-permute-done((f32[128,128]{1,0:T(8,128)S(1)}, f32[128,128]{1,0:T(8,128)S(1)}, u32[]{:S(2)}, u32[]{:S(2)}) %collective-permute-start.9) | collective-permute-done | bytes 65568 | tf_op jit(solution)/shard_map/ppermute | solution.py:261
  80.7 1.4 %collective-permute-done.10.r3 = f32[128,128]{1,0:T(8,128)S(1)} collective-permute-done((f32[128,128]{1,0:T(8,128)S(1)}, f32[128,128]{1,0:T(8,128)S(1)}, u32[]{:S(2)}, u32[]{:S(2)}) %collective-permute-start.10) | collective-permute-done | bytes 65568 | tf_op jit(solution)/shard_map/ppermute | solution.py:261
  82.1 1.5 %normed.1 = (bf16[256,512]{1,0:T(8,128)(2,1)S(1)}, f32[4,256,256]{2,1,0:T(8,128)S(1)}) custom-call(s32[4]{0:T(128)S(1)} %pad_add_fusion.place, f32[128,128]{1,0:T(8,128)S(1)} %get-tuple-element.27.r0, f32[128,128]{1,0:T(8,128)S(1)} %collective-permute-done.8.r1, f32[128,128]{1,0:T(8,128)S(1)} %collective-permute-done.9.r2, ...), custom_call_target="tpu_custom_call" | custom-call | tf_op jit(solution)/shard_map/normed/pallas_call | solution.py:337
  84.7 1.6 %collective-permute-done.11 = f32[4,256,256]{2,1,0:T(8,128)S(1)} collective-permute-done((f32[4,256,256]{2,1,0:T(8,128)S(1)}, f32[4,256,256]{2,1,0:T(8,128)S(1)}, u32[]{:S(2)}, u32[]{:S(2)}) %collective-permute-start.11) | collective-permute-done | bytes 1048608 | tf_op jit(solution)/shard_map/ppermute | solution.py:261
  87.3 2.4 %collective-permute-start.12 = (f32[128,256]{1,0:T(8,128)S(1)}, f32[128,256]{1,0:T(8,128)S(1)}, u32[]{:S(2)}, u32[]{:S(2)}) collective-permute-start(f32[128,256]{1,0:T(8,128)S(1)} %get-tuple-element.44), channel_id=1, source_target_pairs={{0,2},{2,4},{4,6},{6,0},{1,3},{3,5},{5,7},{7,1},{8,10},{10,12},{12... | collective-permute-start | bytes 393224 | tf_op jit(solution)/shard_map/ppermute | solution.py:265
  89.8 3.3 %collective-permute-done.14 = f32[128,256]{1,0:T(8,128)S(1)} collective-permute-done((f32[128,256]{1,0:T(8,128)S(1)}, f32[128,256]{1,0:T(8,128)S(1)}, u32[]{:S(2)}, u32[]{:S(2)}) %collective-permute-start.14) | collective-permute-done | bytes 131104 | tf_op jit(solution)/shard_map/ppermute | solution.py:265
  93.2 3.0 %collective-permute-start.13 = (f32[256,256]{1,0:T(8,128)S(1)}, f32[256,256]{1,0:T(8,128)S(1)}, u32[]{:S(2)}, u32[]{:S(2)}) collective-permute-start(f32[256,256]{1,0:T(8,128)S(1)} %pad_maximum_fusion), channel_id=1, source_target_pairs={{0,2},{2,4},{4,6},{6,0},{1,3},{3,5},{5,7},{7,1},{8,10},{10,12},{12... | collective-permute-start | bytes 786440 | tf_op jit(solution)/shard_map/ppermute | solution.py:265
  96.4 4.6 %collective-permute-done.13 = f32[256,256]{1,0:T(8,128)S(1)} collective-permute-done((f32[256,256]{1,0:T(8,128)S(1)}, f32[256,256]{1,0:T(8,128)S(1)}, u32[]{:S(2)}, u32[]{:S(2)}) %collective-permute-start.13) | collective-permute-done | bytes 262176 | tf_op jit(solution)/shard_map/ppermute | solution.py:265
  101.0 3.5 %collective-permute-done.15 = f32[256,256]{1,0:T(8,128)S(1)} collective-permute-done((f32[256,256]{1,0:T(8,128)S(1)}, f32[256,256]{1,0:T(8,128)S(1)}, u32[]{:S(2)}, u32[]{:S(2)}) %collective-permute-start.15) | collective-permute-done | bytes 262176 | tf_op jit(solution)/shard_map/ppermute | solution.py:265
  (46 shorter events, 6.1 us)
Async XLA Ops:
  0.0 1.6 %copy-start = (bf16[2048,2,256]{2,1,0:T(2,128)(2,1)S(1)}, bf16[2048,2,256]{2,1,0:T(2,128)(2,1)}, u32[]{:S(2)}) copy-start(bf16[2048,2,256]{2,1,0:T(2,128)(2,1)} %param.12) | copy-start | bytes 6291460
  0.0 4.3 %copy-start.10 = (bf16[256,2048]{1,0:T(8,128)(2,1)S(1)}, bf16[256,2048]{1,0:T(8,128)(2,1)}, u32[]{:S(2)}) copy-start(bf16[256,2048]{1,0:T(8,128)(2,1)} %param.11) | copy-start | bytes 3145732
  3.5 0.8 copy-start.3
  4.3 7.4 %copy-start.11 = (bf16[2048,2,4]{0,2,1:T(4,128)(2,1)S(1)}, bf16[2048,2,4]{0,2,1:T(4,128)(2,1)}, u32[]{:S(2)}) copy-start(bf16[2048,2,4]{0,2,1:T(4,128)(2,1)} %param.14) | copy-start | bytes 98308
  4.3 13.1 %copy-start.5 = (f32[4,2,256]{2,1,0:T(2,128)S(1)}, f32[4,2,256]{2,1,0:T(2,128)}, u32[]{:S(2)}) copy-start(f32[4,2,256]{2,1,0:T(2,128)} %taps_qk.1) | copy-start | bytes 24580
  4.3 13.1 %copy-start.6 = (f32[4,512]{1,0:T(4,128)S(1)}, f32[4,512]{1,0:T(4,128)}, u32[]{:S(2)}) copy-start(f32[4,512]{1,0:T(4,128)} %taps_v.1) | copy-start | bytes 24580
  4.3 13.1 %copy-start.7 = (f32[4]{0:T(128)S(1)}, f32[4]{0:T(128)}, u32[]{:S(2)}) copy-start(f32[4]{0:T(128)} %a_log.1) | copy-start | bytes 52
  4.3 13.1 %copy-start.8 = (f32[4]{0:T(128)S(1)}, f32[4]{0:T(128)}, u32[]{:S(2)}) copy-start(f32[4]{0:T(128)} %dt_bias.1) | copy-start | bytes 52
  4.4 13.1 %copy-start.9 = (f32[4]{0:T(128)S(1)}, f32[4]{0:T(128)}, u32[]{:S(2)}) copy-start(f32[4]{0:T(128)} %beta_bias.1) | copy-start | bytes 52
  7.9 9.5 %collective-permute-start = (f32[8,1024]{1,0:T(8,128)S(1)}, f32[8,1024]{1,0:T(8,128)S(1)}, u32[]{:S(2)}, u32[]{:S(2)}) collective-permute-start(f32[8,1024]{1,0:T(8,128)S(1)} %pad_maximum_fusion.2), channel_id=1, source_target_pairs={{0,8},{8,16},{16,24},{24,32},{32,40},{40,48},{48,56},{56,64},{64,7... | collective-permute-start | bytes 98312 | tf_op jit(solution)/shard_map/ppermute | solution.py:281
  17.4 1.0 copy-start.4
  34.8 6.2 %collective-permute-start.1 = (f32[128,256]{1,0:T(8,128)S(1)}, f32[128,256]{1,0:T(8,128)S(1)}, u32[]{:S(2)}, u32[]{:S(2)}) collective-permute-start(f32[128,256]{1,0:T(8,128)S(1)} %get-tuple-element.22), channel_id=1, source_target_pairs={{0,8},{8,0},{16,24},{24,16},{32,40},{40,32},{48,56},{56,48},{1,9},... | collective-permute-start | bytes 393224 | tf_op jit(solution)/shard_map/ppermute | solution.py:261
  34.9 12.4 %collective-permute-start.2 = (f32[128,256]{1,0:T(8,128)S(1)}, f32[128,256]{1,0:T(8,128)S(1)}, u32[]{:S(2)}, u32[]{:S(2)}) collective-permute-start(f32[128,256]{1,0:T(8,128)S(1)} %get-tuple-element.23), channel_id=1, source_target_pairs={{0,16},{8,24},{16,0},{24,8},{32,48},{40,56},{48,32},{56,40},{1,17}... | collective-permute-start | bytes 393224 | tf_op jit(solution)/shard_map/ppermute | solution.py:261
  37.3 10.0 %collective-permute-start.3 = (f32[128,256]{1,0:T(8,128)S(1)}, f32[128,256]{1,0:T(8,128)S(1)}, u32[]{:S(2)}, u32[]{:S(2)}) collective-permute-start(f32[128,256]{1,0:T(8,128)S(1)} %get-tuple-element.24), channel_id=1, source_target_pairs={{0,24},{8,16},{16,8},{24,0},{32,56},{40,48},{48,40},{56,32},{1,25}... | collective-permute-start | bytes 393224 | tf_op jit(solution)/shard_map/ppermute | solution.py:261
  48.3 10.4 %collective-permute-start.4 = (f32[128,256]{1,0:T(8,128)S(1)}, f32[128,256]{1,0:T(8,128)S(1)}, u32[]{:S(2)}, u32[]{:S(2)}) collective-permute-start(f32[128,256]{1,0:T(8,128)S(1)} %get-tuple-element.25.own), channel_id=1, source_target_pairs={{0,32},{8,40},{16,48},{24,56},{32,0},{40,8},{48,16},{56,24},{1,33}... | collective-permute-start | bytes 393224 | tf_op jit(solution)/shard_map/ppermute | solution.py:261
  59.4 7.8 %collective-permute-start.7 = (f32[128,256]{1,0:T(8,128)S(1)}, f32[128,256]{1,0:T(8,128)S(1)}, u32[]{:S(2)}, u32[]{:S(2)}) collective-permute-start(f32[128,256]{1,0:T(8,128)S(1)} %row.1), channel_id=1, source_target_pairs={{0,192},{1,193},{2,194},{3,195},{4,196},{5,197},{6,198},{7,199},{8... | collective-permute-start | bytes 393224 | tf_op jit(solution)/shard_map/ppermute | solution.py:269
  60.1 7.6 %collective-permute-start.6 = (f32[128,256]{1,0:T(8,128)S(1)}, f32[128,256]{1,0:T(8,128)S(1)}, u32[]{:S(2)}, u32[]{:S(2)}) collective-permute-start(f32[128,256]{1,0:T(8,128)S(1)} %row.1), channel_id=1, source_target_pairs={{0,128},{64,192},{1,129},{65,193},{2,130},{66,194},{3,131},{67,195... | collective-permute-start | bytes 393224 | tf_op jit(solution)/shard_map/ppermute | solution.py:269
  65.2 6.9 %collective-permute-start.5 = (f32[128,256]{1,0:T(8,128)S(1)}, f32[128,256]{1,0:T(8,128)S(1)}, u32[]{:S(2)}, u32[]{:S(2)}) collective-permute-start(f32[128,256]{1,0:T(8,128)S(1)} %row.1), channel_id=1, source_target_pairs={{0,64},{64,128},{128,192},{1,65},{65,129},{129,193},{2,66},{66,130... | collective-permute-start | bytes 393224 | tf_op jit(solution)/shard_map/ppermute | solution.py:269
  73.4 6.2 %collective-permute-start.8 = (f32[128,128]{1,0:T(8,128)S(1)}, f32[128,128]{1,0:T(8,128)S(1)}, u32[]{:S(2)}, u32[]{:S(2)}) collective-permute-start(f32[128,128]{1,0:T(8,128)S(1)} %get-tuple-element.28), channel_id=1, source_target_pairs={{0,8},{8,0},{16,24},{24,16},{32,40},{40,32},{48,56},{56,48},{1,9},... | collective-permute-start | bytes 196616 | tf_op jit(solution)/shard_map/ppermute | solution.py:261
  74.8 5.9 %collective-permute-start.9 = (f32[128,128]{1,0:T(8,128)S(1)}, f32[128,128]{1,0:T(8,128)S(1)}, u32[]{:S(2)}, u32[]{:S(2)}) collective-permute-start(f32[128,128]{1,0:T(8,128)S(1)} %get-tuple-element.29), channel_id=1, source_target_pairs={{0,16},{8,24},{16,0},{24,8},{32,48},{40,56},{48,32},{56,40},{1,17}... | collective-permute-start | bytes 196616 | tf_op jit(solution)/shard_map/ppermute | solution.py:261
  76.0 6.1 %collective-permute-start.10 = (f32[128,128]{1,0:T(8,128)S(1)}, f32[128,128]{1,0:T(8,128)S(1)}, u32[]{:S(2)}, u32[]{:S(2)}) collective-permute-start(f32[128,128]{1,0:T(8,128)S(1)} %get-tuple-element.30), channel_id=1, source_target_pairs={{0,24},{8,16},{16,8},{24,0},{32,56},{40,48},{48,40},{56,32},{1,25}... | collective-permute-start | bytes 196616 | tf_op jit(solution)/shard_map/ppermute | solution.py:261
  77.9 4.2 %copy-start.1 = (bf16[512,2048]{1,0:T(8,128)(2,1)S(1)}, bf16[512,2048]{1,0:T(8,128)(2,1)}, u32[]{:S(2)}) copy-start(bf16[512,2048]{1,0:T(8,128)(2,1)} %w_out.3) | copy-start | bytes 6291460
  77.9 4.2 %copy-start.2 = (f32[128]{0:T(128)S(1)}, f32[128]{0:T(128)}, u32[]{:S(2)}) copy-start(f32[128]{0:T(128)} %param.20) | copy-start | bytes 1540
  83.5 2.7 %collective-permute-start.11 = (f32[4,256,256]{2,1,0:T(8,128)S(1)}, f32[4,256,256]{2,1,0:T(8,128)S(1)}, u32[]{:S(2)}, u32[]{:S(2)}) collective-permute-start(f32[4,256,256]{2,1,0:T(8,128)S(1)} %get-tuple-element.36), channel_id=1, source_target_pairs={{0,1},{1,0},{2,3},{3,2},{4,5},{5,4},{6,7},{7,6},{8,9},{9,8},{10,11... | collective-permute-start | bytes 3145736 | tf_op jit(solution)/shard_map/ppermute | solution.py:261
  86.3 6.8 %collective-permute-start.14 = (f32[128,256]{1,0:T(8,128)S(1)}, f32[128,256]{1,0:T(8,128)S(1)}, u32[]{:S(2)}, u32[]{:S(2)}) collective-permute-start(f32[128,256]{1,0:T(8,128)S(1)} %get-tuple-element.43), channel_id=1, source_target_pairs={{0,6},{2,0},{4,2},{6,4},{1,7},{3,1},{5,3},{7,5},{8,14},{10,8},{12,... | collective-permute-start | bytes 393224 | tf_op jit(solution)/shard_map/ppermute | solution.py:265
  87.3 5.9 %collective-permute-start.12 = (f32[128,256]{1,0:T(8,128)S(1)}, f32[128,256]{1,0:T(8,128)S(1)}, u32[]{:S(2)}, u32[]{:S(2)}) collective-permute-start(f32[128,256]{1,0:T(8,128)S(1)} %get-tuple-element.44), channel_id=1, source_target_pairs={{0,2},{2,4},{4,6},{6,0},{1,3},{3,5},{5,7},{7,1},{8,10},{10,12},{12... | collective-permute-start | bytes 393224 | tf_op jit(solution)/shard_map/ppermute | solution.py:265
  93.2 7.7 %collective-permute-start.13 = (f32[256,256]{1,0:T(8,128)S(1)}, f32[256,256]{1,0:T(8,128)S(1)}, u32[]{:S(2)}, u32[]{:S(2)}) collective-permute-start(f32[256,256]{1,0:T(8,128)S(1)} %pad_maximum_fusion), channel_id=1, source_target_pairs={{0,2},{2,4},{4,6},{6,0},{1,3},{3,5},{5,7},{7,1},{8,10},{10,12},{12... | collective-permute-start | bytes 786440 | tf_op jit(solution)/shard_map/ppermute | solution.py:265
  96.3 8.2 %collective-permute-start.15 = (f32[256,256]{1,0:T(8,128)S(1)}, f32[256,256]{1,0:T(8,128)S(1)}, u32[]{:S(2)}, u32[]{:S(2)}) collective-permute-start(f32[256,256]{1,0:T(8,128)S(1)} %pad_maximum_fusion.1), channel_id=1, source_target_pairs={{0,6},{2,0},{4,2},{6,4},{1,7},{3,1},{5,3},{7,5},{8,14},{10,8},{12,... | collective-permute-start | bytes 786440 | tf_op jit(solution)/shard_map/ppermute | solution.py:265

commit v2 on v1

--- a/solution.py
+++ b/solution.py
@@ -104,32 +104,50 @@
     return jnp.where(rows >= cols, 1.0, 0.0).astype(BF16)
 
 
+def conv_part(pad, taps, width):
+    total = None
+    for j in range(4):
+        term = pad[5 + j : 5 + j + SEG, :width] * taps(j)
+        total = term if total is None else total + term
+    return silu(total)
+
+
 def segment_kernel(
-    place, a_log, dt_bias, beta_bias, qk, vz, halo, taps_qk, taps_v, ab,
-    out0, out1, out2, out3, q_out, k_out, ef_out, cols_out,
-    pad, maps,
+    own_group, place, a_log, dt_bias, beta_bias, tokens, halo, w_qk, w_v, taps_qk, taps_v, w_ab,
+    out0, out1, q_out, k_out, ef_out, cols_out, pad, maps,
 ):
+    mine = place[0]
+    group = (mine >> 1) if own_group else 1 - (mine >> 1)
     rows, cols = iota2((SEG, SEG), 0), iota2((SEG, SEG), 1)
-    pad[0:8, :] = halo[...]
-    pad[8:, 0:256] = qk[0]
-    pad[8:, 256:512] = qk[1]
-    pad[8:, 512:1024] = vz[0]
-
-    def conv(start, width, tap):
-        total = None
-        for j in range(4):
-            term = pad[5 + j : 5 + j + SEG, start : start + width] * tap(j)
-            total = term if total is None else total + term
-        return silu(total)
-
+    tok = tokens[...]
+    before = halo[...].astype(BF16)
+    lanes = pl.ds(pl.multiple_of(group * DK, DK), DK)
+    wide = pl.ds(pl.multiple_of(group * 256, 256), 256)
+    key_lanes = pl.ds(pl.multiple_of(256 + group * DK, DK), DK)
+
+    def pick(taps, width):
+        return jnp.where(group == 1, taps[:, width : 2 * width], taps[:, :width])
+
+    def project(w, taps, width):
+        full = mm(tok, w)
+        pad[0:8, :width] = mm(before, w)
+        pad[8:, :width] = full
+        return conv_part(pad, taps, width)
+
+    k = unit(project(w_qk[:, key_lanes], lambda j: pick(taps_qk[j, 1:2, :], DK), DK))
+    kk = dot3_nt(k, k)
     head_rows = []
-    for h in range(VH):
-        head_rows.append(jax.nn.sigmoid(ab[0, h : h + 1, :] + beta_bias[h]))
-    for h in range(VH):
+    logits = [mm_nt(w_ab[c], tok) for c in (0, 1)]
+    for i in range(2):
+        h = group * 2 + i
+        mine_beta = jnp.where(group == 1, logits[0][2 + i : 3 + i], logits[0][i : i + 1])
+        head_rows.append(jax.nn.sigmoid(mine_beta + beta_bias[h]))
+    for i in range(2):
+        h = group * 2 + i
+        mine_decay = jnp.where(group == 1, logits[1][2 + i : 3 + i], logits[1][i : i + 1])
         rate = jnp.exp(jnp.full((1, SEG), a_log[h], F32))
-        head_rows.append(
-            jnp.maximum(-rate * softplus(ab[1, h : h + 1, :] + dt_bias[h]), FLOOR)
-        )
+        head_rows.append(jnp.maximum(-rate * softplus(mine_decay + dt_bias[h]), FLOOR))
+    head_rows.append(jnp.zeros((4, SEG), F32))
     col8 = jnp.concatenate(head_rows, 0).T
     cols_out[...] = col8
     lower = lower_ones()
@@ -138,59 +156,70 @@
     growth8 = jnp.exp(mm(lower, dhi) + mm(lower, dmid) + mm(lower, dlo))
     closing8 = jnp.exp(mm(later, dhi) + mm(later, dmid) + mm(later, dlo))
 
+    v = project(w_v[:, wide], lambda j: pick(taps_v[j : j + 1, :], 256), 256)
     prow, pcol = iota2((HALF, SEG), 0), iota2((HALF, SEG), 1) & (HALF - 1)
     strict_pair = prow > pcol
     eye_pair = jnp.where(prow == pcol, 1.0, 0.0)
     eye = jnp.where(iota2((DK, DK), 0) == iota2((DK, DK), 1), 1.0, 0.0)
-
-    for g in range(QKH):
-        q = unit(conv(g * DK, DK, lambda j: taps_qk[j, 0:1, g * DK : (g + 1) * DK])) * DK ** -0.5
-        k = unit(conv(256 + g * DK, DK, lambda j: taps_qk[j, 1:2, g * DK : (g + 1) * DK]))
-        q_out[g] = q
-        k_out[g] = k
-        kk = dot3_nt(k, k)
-        for h in (2 * g, 2 * g + 1):
-            v = conv(512 + h * DV, DV, lambda j: taps_v[j : j + 1, h * DV : (h + 1) * DV])
-            beta = col8[:, h : h + 1]
-            growth = growth8[:, VH + h : VH + h + 1]
-            closing = closing8[:, VH + h : VH + h + 1]
-            weighted = fades(col8[:, VH + h : VH + h + 1], lower) * kk * beta
-            m = jnp.concatenate([weighted[:HALF, :HALF], weighted[HALF:, HALF:]], 1)
-            m = jnp.where(strict_pair, m, 0.0)
-            corner = weighted[HALF:, :HALF]
-            t = eye_pair - jnp.where((prow ^ pcol) == 1, m, 0.0)
-            for level in range(1, 7):
-                part = jnp.where(((prow >> level) ^ (pcol >> level)) == 1, m, 0.0)
-                t = t - dot3_blocks(t, dot3_blocks(part, t))
-            right = jnp.concatenate([k * growth, v], 1) * beta
-            x1 = dot3(t[:, :HALF], right[:HALF])
-            x2 = dot3(t[:, HALF:], right[HALF:] - dot3(corner, x1))
-            ef = jnp.concatenate([x1, x2], 0)
-            ef_out[h] = ef
-            both = dot3((k * closing).T, ef)
-            maps[h] = jnp.concatenate(
-                [growth[SEG - 1 : SEG] * eye - both[:, :DK], both[:, DK:]], 1
-            )
-    mine = place[0]
-    for slot, out in enumerate((out0, out1, out2, out3)):
-        out[...] = maps[mine ^ slot]
-
-
-def reply_kernel(q_in, k_in, ef, cols8, out):
+    both_heads = (0, 1)
+    beta = [col8[:, i : i + 1] for i in both_heads]
+    growth = [growth8[:, 2 + i : 3 + i] for i in both_heads]
+    closing = [closing8[:, 2 + i : 3 + i] for i in both_heads]
+    weighted = [fades(col8[:, 2 + i : 3 + i], lower) * kk * beta[i] for i in both_heads]
+    m = [
+        jnp.where(strict_pair, jnp.concatenate([u[:HALF, :HALF], u[HALF:, HALF:]], 1), 0.0)
+        for u in weighted
+    ]
+    corner = [u[HALF:, :HALF] for u in weighted]
+    t = [eye_pair - jnp.where((prow ^ pcol) == 1, m[i], 0.0) for i in both_heads]
+    for level in range(1, 7):
+        keep = ((prow >> level) ^ (pcol >> level)) == 1
+        part = [jnp.where(keep, m[i], 0.0) for i in both_heads]
+        inner = [dot3_blocks(part[i], t[i]) for i in both_heads]
+        t = [t[i] - dot3_blocks(t[i], inner[i]) for i in both_heads]
+    right = [
+        jnp.concatenate([k * growth[i], v[:, i * DV : (i + 1) * DV]], 1) * beta[i]
+        for i in both_heads
+    ]
+    x1 = [dot3(t[i][:, :HALF], right[i][:HALF]) for i in both_heads]
+    rest = [right[i][HALF:] - dot3(corner[i], x1[i]) for i in both_heads]
+    x2 = [dot3(t[i][:, HALF:], rest[i]) for i in both_heads]
+    ef = [jnp.concatenate([x1[i], x2[i]], 0) for i in both_heads]
+    both = [dot3((k * closing[i]).T, ef[i]) for i in both_heads]
+    for i in both_heads:
+        ef_out[i] = ef[i]
+        maps[i] = jnp.concatenate(
+            [growth[i][SEG - 1 : SEG] * eye - both[i][:, :DK], both[i][:, DK:]], 1
+        )
+    out0[...] = maps[mine & 1]
+    out1[...] = maps[(mine & 1) ^ 1]
+    k_out[...] = k
+    q_out[...] = unit(project(w_qk[:, lanes], lambda j: pick(taps_qk[j, 0:1, :], DK), DK)) * DK ** -0.5
+
+
+def reply_kernel(place, tokens, w_z, gain, q_a, k_a, ef_a, cols_a, q_b, k_b, ef_b, cols_b, out, gates):
     rows, cols = iota2((SEG, SEG), 0), iota2((SEG, SEG), 1)
     lower = lower_ones()
-    col8 = cols8[...]
-    dhi, dmid, dlo = split3(col8)
-    growth8 = jnp.exp(mm(lower, dhi) + mm(lower, dmid) + mm(lower, dlo))
-    for g in range(QKH):
-        q = q_in[g]
-        qk = dot3_nt(q, k_in[g])
-        for h in (2 * g, 2 * g + 1):
-            fade = fades(col8[:, VH + h : VH + h + 1], lower)
+    mine = place[0] >> 1
+    z = mm(tokens[...], w_z[...])
+    for h in range(VH):
+        part = z[:, h * DV : (h + 1) * DV]
+        gates[:, h * DV : (h + 1) * DV] = gain[...] * silu(part)
+    for group, q_in, k_in, ef, cols4 in (
+        (mine, q_a, k_a, ef_a, cols_a),
+        (1 - mine, q_b, k_b, ef_b, cols_b),
+    ):
+        col8 = cols4[...]
+        dhi, dmid, dlo = split3(col8)
+        growth8 = jnp.exp(mm(lower, dhi) + mm(lower, dmid) + mm(lower, dlo))
+        q = q_in[...]
+        qk = dot3_nt(q, k_in[...])
+        for i in range(2):
+            fade = fades(col8[:, 2 + i : 3 + i], lower)
             mixing = jnp.where(rows >= cols, fade * qk, 0.0)
-            both = dot3(mixing, ef[h])
-            out[h] = jnp.concatenate(
-                [q * growth8[:, VH + h : VH + h + 1] - both[:, :DK], both[:, DK:]], 1
+            both = dot3(mixing, ef[i])
+            out[group * 2 + i] = jnp.concatenate(
+                [q * growth8[:, 2 + i : 3 + i] - both[:, :DK], both[:, DK:]], 1
             )
 
 
@@ -231,15 +260,14 @@
         out[...] = states[mine ^ slot]
 
 
-def normed_kernel(place, r0, r1, r2, r3, reply, vz, gain, w_out, normed, out, states):
+def normed_kernel(place, r0, r1, r2, r3, reply, gates, w_out, normed, out, states):
     mine = place[0]
     for slot, r in enumerate((r0, r1, r2, r3)):
         states[mine ^ slot] = r[...]
     for h in range(VH):
         core = dot3(reply[h, :, :DK], states[h]) + reply[h, :, DK:]
-        z = vz[1, :, h * DV : (h + 1) * DV]
         scale = lax.rsqrt(jnp.mean(core * core, -1, keepdims=True) + EPS)
-        normed[:, h * DV : (h + 1) * DV] = (core * scale * gain[...] * silu(z)).astype(BF16)
+        normed[:, h * DV : (h + 1) * DV] = (core * scale * gates[:, h * DV : (h + 1) * DV]).astype(BF16)
     product_blocks(place[2], 1 - place[3], normed, w_out, out)
 
 
@@ -269,40 +297,47 @@
     return lax.ppermute(v, axis, [(i, i + step) for i in range(size - step)])
 
 
+def segment_call(own_group, *args):
+    width = args[4].shape[1]
+    whole = pl.BlockSpec((width, VH * DV), lambda i: (0, 0))
+    return pl.pallas_call(
+        functools.partial(segment_kernel, own_group),
+        grid=(1,),
+        out_shape=[arr(DK, 256)] * 2
+        + [arr(SEG, DK), arr(SEG, DK), arr(2, SEG, 256), arr(SEG, 8)],
+        in_specs=[SMEM] * 4 + [VMEM, VMEM, VMEM, whole] + [VMEM] * 3,
+        out_specs=[VMEM] * 6,
+        scratch_shapes=[pltpu.VMEM((SEG + 8, 256), F32), pltpu.VMEM((2, DK, 256), F32)],
+        compiler_params=params(28),
+        cost_estimate=pl.CostEstimate(flops=6 * 10**9, bytes_accessed=6 * 10**6, transcendentals=0),
+        name="segment_own" if own_group else "segment_other",
+    )(*args)
+
+
 def local(tokens, w_qk, w_vz, w_ab, conv_qk, conv_v, a_log, dt_bias, beta_bias, norm_gain, w_out):
     y, z = lax.axis_index("y"), lax.axis_index("z")
     x, core = lax.axis_index("x"), lax.axis_index("core")
     place = jnp.stack([z & 3, z >> 2, x, core]).astype(jnp.int32)
 
-    qk = jnp.einsum("td,dcf->ctf", tokens, w_qk, preferred_element_type=F32)
-    vz = jnp.einsum("td,dcf->ctf", tokens, w_vz, preferred_element_type=F32)
-    ab = jnp.einsum("td,dcf->cft", tokens, w_ab, preferred_element_type=F32)
-    tail = jnp.concatenate([qk[0, SEG - 8 :], qk[1, SEG - 8 :], vz[0, SEG - 8 :]], 1)
+    tail = tokens[SEG - 8 :].astype(F32)
     halo = lax.ppermute(tail, ("y", "z"), [(i, i + 1) for i in range(31)])
-
-    seg = pl.pallas_call(
-        segment_kernel,
-        out_shape=[arr(DK, 256)] * 4
-        + [arr(QKH, SEG, DK), arr(QKH, SEG, DK), arr(VH, SEG, 256), arr(SEG, 8)],
-        in_specs=[SMEM] * 4 + [VMEM] * 6,
-        out_specs=[VMEM] * 8,
-        scratch_shapes=[pltpu.VMEM((SEG + 8, 1024), F32), pltpu.VMEM((VH, DK, 256), F32)],
-        compiler_params=params(24),
-        cost_estimate=pl.CostEstimate(flops=6 * 10**9, bytes_accessed=6 * 10**6, transcendentals=0),
-        name="segment",
-    )(place, a_log, dt_bias, beta_bias, qk, vz, halo, conv_qk, conv_v, ab)
-    maps, (q, k, ef, cols8) = seg[:4], seg[4:]
-
-    got = [maps[0]] + [swap(maps[m], "z", 8, m) for m in (1, 2, 3)]
-    reply = pl.pallas_call(
+    flat_qk = w_qk.reshape(w_qk.shape[0], 2 * QKH * DK)
+    flat_vz = w_vz.reshape(w_vz.shape[0], 2 * VH * DV)
+    ab = w_ab.transpose(1, 2, 0)
+    args = (place, a_log, dt_bias, beta_bias, tokens, halo, flat_qk, flat_vz, conv_qk, conv_v, ab)
+    far = segment_call(False, *args)
+    near = segment_call(True, *args)
+    got = [near[0], swap(near[1], "z", 8, 1), swap(far[0], "z", 8, 2), swap(far[1], "z", 8, 3)]
+    reply, gates = pl.pallas_call(
         reply_kernel,
-        out_shape=arr(VH, SEG, 256),
-        in_specs=[VMEM] * 4,
-        out_specs=VMEM,
-        compiler_params=params(24),
+        grid=(1,),
+        out_shape=[arr(VH, SEG, 256), arr(SEG, VH * DV)],
+        in_specs=[SMEM, VMEM, pl.BlockSpec((tokens.shape[1], VH * DV), lambda i: (0, 1))] + [VMEM] * 9,
+        out_specs=[VMEM] * 2,
+        compiler_params=params(28),
         cost_estimate=pl.CostEstimate(flops=2 * 10**9, bytes_accessed=3 * 10**6, transcendentals=0),
         name="reply",
-    )(q, k, ef, cols8)
+    )(place, tokens, flat_vz, norm_gain.reshape(1, DV), *near[2:], *far[2:])
 
     total, prefixes = pl.pallas_call(
         quad_kernel,
@@ -337,12 +372,12 @@
     normed, for_twin = pl.pallas_call(
         normed_kernel,
         out_shape=[arr(SEG, VH * DV, dtype=BF16), arr(4, SEG, 256)],
-        in_specs=[SMEM] + [VMEM] * 8,
+        in_specs=[SMEM] + [VMEM] * 7,
         out_specs=[VMEM] * 2,
         scratch_shapes=[pltpu.VMEM((4, DK, DV), F32)],
         compiler_params=params(24),
         name="normed",
-    )(place, *came, reply, vz, norm_gain.reshape(1, DV), w_out)
+    )(place, *came, reply, gates, w_out)
     from_twin = swap(for_twin, "core", 2, 1)
     own = pl.pallas_call(
         own_kernel,
@@ -354,9 +389,9 @@
         name="own",
     )(place, normed, w_out)
 
-    far = own[2] + from_twin[2]
-    from_left = shift(far[:HALF], "x", 4, 1)
-    from_right = shift(far[HALF:], "x", 4, -1)
+    across = own[2] + from_twin[2]
+    from_left = shift(across[:HALF], "x", 4, 1)
+    from_right = shift(across[HALF:], "x", 4, -1)
     chip = own + from_twin
     to_right = jnp.concatenate([chip[1, :HALF] + from_left, chip[1, HALF:]], 0)
     to_left = jnp.concatenate([chip[3, :HALF], chip[3, HALF:] + from_right], 0)

time: 105 us -> 92.6 us (0.88)
  matrix products: 7.02 us -> 0 us
  waiting for transfers between devices: 38.4 us -> 32.2 us
    dot_general x3 -> x0, matrix products: 7.02 us -> none  [the longest x1 3.48 us: local(): vz = jnp.einsum('td,dcf->ctf', tokens, w_vz, preferred_element_type=F32)]
    ppermute x8, waiting for transfers between devices: 18 us -> 13.9 us  [swap(): return lax.ppermute(v, axis, [(i, i ^ mask) for i in range(size)])]
    ppermute x1, waiting for transfers between devices: 3.99 us -> 1.9 us  [local(): halo = lax.ppermute(tail, ('y', 'z'), [(i, i + 1) for i in range(31)])]
    unnamed x24 -> x22, local copies, waits for them, and re-layouts: 3.44 us -> 4.04 us
    pallas_call x2 -> x3, Pallas kernels: 17.9 us -> 17.8 us  [the longest x2 15 us: segment_call(): pl.pallas_call(functools.partial(segment_kernel, own_group), grid=(1,), o...]
  transfers between devices with their start and end apart: 16 -> 16, of which waited for: 12 -> 11; matrix products, arithmetic and copies ran while one was open for 2% -> 4% of each run, Pallas kernels for 3% -> 12%
where the time goes in v2:
time: 92.6 us; the launch traced here: 92.3 us
  waiting for transfers between devices  32.2 us (35%)
  starting transfers between devices  30.8 us (33%)
  Pallas kernels  23.3 us (25%)
  local copies, waits for them, and re-layouts  4.08 us (4%)
  other arithmetic  1.79 us (2%)
    pallas_call x2, Pallas kernels, segment_call(): pl.pallas_call(functools.partial(segment_kernel, own_group), grid=(1,), o...  15 us
    ppermute x8, waiting for transfers between devices, swap(): return lax.ppermute(v, axis, [(i, i ^ mask) for i in range(size)])  13.9 us
    ppermute x8, starting transfers between devices, swap(): return lax.ppermute(v, axis, [(i, i ^ mask) for i in range(size)])  13.1 us
    ppermute x4, waiting for transfers between devices, shift(): return lax.ppermute(v, axis, [(i, (i + step) % size) for i in range(size)])  11.5 us
    ppermute x3, starting transfers between devices, forward(): return lax.ppermute(v, axis, [(i, i + step) for i in range(size - step)])  7.42 us
    ppermute x4, starting transfers between devices, shift(): return lax.ppermute(v, axis, [(i, (i + step) % size) for i in range(size)])  6.43 us
    ppermute x3, waiting for transfers between devices, forward(): return lax.ppermute(v, axis, [(i, i + step) for i in range(size - step)])  4.92 us
    unnamed x22, local copies, waits for them, and re-layouts  4.04 us
  transfers between devices with their start and end apart: 16, of which 11 were waited for; matrix products, arithmetic and copies ran while one was open for 4% of the time, Pallas kernels for 12%

profile of v2, /device:TPU:14, one launch (start us, length us, event | category | flops | bytes accessed | tf_op | source)
XLA Modules:
  0.0 92.3 jit_solution(3957426997075437242)
XLA Ops:
  0.0 0.8 slice_convert_fusion
  0.8 3.8 %collective-permute-start = (f32[8,2048]{1,0:T(8,128)S(1)}, f32[8,2048]{1,0:T(8,128)S(1)}, u32[]{:S(2)}, u32[]{:S(2)}) collective-permute-start(f32[8,2048]{1,0:T(8,128)S(1)} %slice_convert_fusion), channel_id=1, source_target_pairs={{0,8},{8,16},{16,24},{24,32},{32,40},{40,48},{48,56},{56,64},{64,7... | collective-permute-start | bytes 196616 | tf_op jit(solution)/shard_map/ppermute | solution.py:323
  4.6 2.2 %copy.12 = bf16[256,8,2,256]{3,1,2,0:T(8,128)(2,1)S(1)} copy(bf16[256,8,2,256]{3,2,1,0:T(2,128)(2,1)} %bitcast.41) | data formatting | bytes 4194304
  7.5 1.2 %copy.13 = bf16[256,8,2,512]{3,1,2,0:T(8,128)(2,1)S(1)} copy(bf16[256,8,2,512]{3,2,1,0:T(2,128)(2,1)S(1)} %bitcast.40) | data formatting | bytes 8388608
  8.7 1.9 %collective-permute-done.halo = f32[8,2048]{1,0:T(8,128)S(1)} collective-permute-done((f32[8,2048]{1,0:T(8,128)S(1)}, f32[8,2048]{1,0:T(8,128)S(1)}, u32[]{:S(2)}, u32[]{:S(2)}) %collective-permute-start) | collective-permute-done | bytes 65568 | tf_op jit(solution)/shard_map/ppermute | solution.py:323
  10.7 7.5 %segment_other.1 = (f32[128,256]{1,0:T(8,128)S(1)}, f32[128,256]{1,0:T(8,128)S(1)}, f32[256,128]{1,0:T(8,128)S(1)}, f32[256,128]{1,0:T(8,128)S(1)}, f32[2,256,256]{2,1,0:T(8,128)S(1)}, /*index=5*/f32[256,8]{1,0:T(8,128)S(1)}) custom-call(s32[4]{0:T(128)S(1)} %pad_add_fusion.place, f32[4]{0:T(128)S(1)} %copy-done.5, f32[4]{0:T(128)S(1)} %copy-done.6, ...), custom_call_target="tpu_custom_call" | custom-call | flops 6000000000 | bytes 6000000 | tf_op jit(solution)/shard_map/segment_other/pallas_call | solution.py:303
  18.2 1.4 %collective-permute-start.2 = (f32[128,256]{1,0:T(8,128)S(1)}, f32[128,256]{1,0:T(8,128)S(1)}, u32[]{:S(2)}, u32[]{:S(2)}) collective-permute-start(f32[128,256]{1,0:T(8,128)S(1)} %get-tuple-element.29), channel_id=1, source_target_pairs={{0,16},{8,24},{16,0},{24,8},{32,48},{40,56},{48,32},{56,40},{1,17}... | collective-permute-start | bytes 393224 | tf_op jit(solution)/shard_map/ppermute | solution.py:289
  19.7 2.9 %collective-permute-start.3 = (f32[128,256]{1,0:T(8,128)S(1)}, f32[128,256]{1,0:T(8,128)S(1)}, u32[]{:S(2)}, u32[]{:S(2)}) collective-permute-start(f32[128,256]{1,0:T(8,128)S(1)} %get-tuple-element.30), channel_id=1, source_target_pairs={{0,24},{8,16},{16,8},{24,0},{32,56},{40,48},{48,40},{56,32},{1,25}... | collective-permute-start | bytes 393224 | tf_op jit(solution)/shard_map/ppermute | solution.py:289
  22.5 7.5 %segment_own.1 = (f32[128,256]{1,0:T(8,128)S(1)}, f32[128,256]{1,0:T(8,128)S(1)}, f32[256,128]{1,0:T(8,128)S(1)}, f32[256,128]{1,0:T(8,128)S(1)}, f32[2,256,256]{2,1,0:T(8,128)S(1)}, /*index=5*/f32[256,8]{1,0:T(8,128)S(1)}) custom-call(s32[4]{0:T(128)S(1)} %pad_add_fusion.place, f32[4]{0:T(128)S(1)} %copy-done.5, f32[4]{0:T(128)S(1)} %copy-done.6, ...), custom_call_target="tpu_custom_call" | custom-call | flops 6000000000 | bytes 6000000 | tf_op jit(solution)/shard_map/segment_own/pallas_call | solution.py:303
  31.0 4.1 %collective-permute-done.1.r1 = f32[128,256]{1,0:T(8,128)S(1)} collective-permute-done((f32[128,256]{1,0:T(8,128)S(1)}, f32[128,256]{1,0:T(8,128)S(1)}, u32[]{:S(2)}, u32[]{:S(2)}) %collective-permute-start.1) | collective-permute-done | bytes 131104 | tf_op jit(solution)/shard_map/ppermute | solution.py:289
  35.1 1.0 %quad.1 = (f32[128,256]{1,0:T(8,128)S(1)}, f32[3,128,256]{2,1,0:T(8,128)S(1)}) custom-call(s32[4]{0:T(128)S(1)} %pad_add_fusion.place, f32[128,256]{1,0:T(8,128)S(1)} %get-tuple-element.27.r0, f32[128,256]{1,0:T(8,128)S(1)} %collective-permute-done.1.r1, f32[128,256]{1,0:T(8,128)S(1)} %collective-permute-done.2.r2, f32[128,256]{1,0:T(8,128)S(1)} %collective-permute-done.3.r3), custom_call_target="tpu_custom_call" | custom-call | tf_op jit(solution)/shard_map/quad/pallas_call | solution.py:342
  36.1 3.7 %collective-permute-start.4 = (f32[128,256]{1,0:T(8,128)S(1)}, f32[128,256]{1,0:T(8,128)S(1)}, u32[]{:S(2)}, u32[]{:S(2)}) collective-permute-start(f32[128,256]{1,0:T(8,128)S(1)} %get-tuple-element.31.own), channel_id=1, source_target_pairs={{0,32},{8,40},{16,48},{24,56},{32,0},{40,8},{48,16},{56,24},{1,33}... | collective-permute-start | bytes 393224 | tf_op jit(solution)/shard_map/ppermute | solution.py:289
  39.7 6.8 %collective-permute-done.4.other = f32[128,256]{1,0:T(8,128)S(1)} collective-permute-done((f32[128,256]{1,0:T(8,128)S(1)}, f32[128,256]{1,0:T(8,128)S(1)}, u32[]{:S(2)}, u32[]{:S(2)}) %collective-permute-start.4) | collective-permute-done | bytes 131104 | tf_op jit(solution)/shard_map/ppermute | solution.py:289
  46.5 0.7 row.1
  47.9 4.8 %collective-permute-start.6 = (f32[128,256]{1,0:T(8,128)S(1)}, f32[128,256]{1,0:T(8,128)S(1)}, u32[]{:S(2)}, u32[]{:S(2)}) collective-permute-start(f32[128,256]{1,0:T(8,128)S(1)} %row.1), channel_id=1, source_target_pairs={{0,128},{64,192},{1,129},{65,193},{2,130},{66,194},{3,131},{67,195... | collective-permute-start | bytes 393224 | tf_op jit(solution)/shard_map/ppermute | solution.py:297
  52.8 1.9 %collective-permute-start.5 = (f32[128,256]{1,0:T(8,128)S(1)}, f32[128,256]{1,0:T(8,128)S(1)}, u32[]{:S(2)}, u32[]{:S(2)}) collective-permute-start(f32[128,256]{1,0:T(8,128)S(1)} %row.1), channel_id=1, source_target_pairs={{0,64},{64,128},{128,192},{1,65},{65,129},{129,193},{2,66},{66,130... | collective-permute-start | bytes 393224 | tf_op jit(solution)/shard_map/ppermute | solution.py:297
  55.3 4.4 %collective-permute-done.5.y1 = f32[128,256]{1,0:T(8,128)S(1)} collective-permute-done((f32[128,256]{1,0:T(8,128)S(1)}, f32[128,256]{1,0:T(8,128)S(1)}, u32[]{:S(2)}, u32[]{:S(2)}) %collective-permute-start.5) | collective-permute-done | bytes 131104 | tf_op jit(solution)/shard_map/ppermute | solution.py:297
  59.6 1.3 %state.1 = (f32[128,128]{1,0:T(8,128)S(1)}, f32[128,128]{1,0:T(8,128)S(1)}, f32[128,128]{1,0:T(8,128)S(1)}, f32[128,128]{1,0:T(8,128)S(1)}) custom-call(s32[4]{0:T(128)S(1)} %pad_add_fusion.place, f32[128,256]{1,0:T(8,128)S(1)} %collective-permute-done.5.y1, f32[128,256]{1,0:T(8,128)S(1)} %collective-permute-done.6.y2, ...), custom_call_target="tpu_custom_call" | custom-call | tf_op jit(solution)/shard_map/state/pallas_call | solution.py:361
  61.0 1.9 %collective-permute-start.9 = (f32[128,128]{1,0:T(8,128)S(1)}, f32[128,128]{1,0:T(8,128)S(1)}, u32[]{:S(2)}, u32[]{:S(2)}) collective-permute-start(f32[128,128]{1,0:T(8,128)S(1)} %get-tuple-element.35), channel_id=1, source_target_pairs={{0,16},{8,24},{16,0},{24,8},{32,48},{40,56},{48,32},{56,40},{1,17}... | collective-permute-start | bytes 196616 | tf_op jit(solution)/shard_map/ppermute | solution.py:289
  62.9 2.5 %collective-permute-start.10 = (f32[128,128]{1,0:T(8,128)S(1)}, f32[128,128]{1,0:T(8,128)S(1)}, u32[]{:S(2)}, u32[]{:S(2)}) collective-permute-start(f32[128,128]{1,0:T(8,128)S(1)} %get-tuple-element.36), channel_id=1, source_target_pairs={{0,24},{8,16},{16,8},{24,0},{32,56},{40,48},{48,40},{56,32},{1,25}... | collective-permute-start | bytes 196616 | tf_op jit(solution)/shard_map/ppermute | solution.py:289
  65.4 2.8 %reply.1 = (f32[4,256,256]{2,1,0:T(8,128)S(1)}, f32[256,512]{1,0:T(8,128)S(1)}) custom-call(s32[4]{0:T(128)S(1)} %pad_add_fusion.place, bf16[256,2048]{1,0:T(8,128)(2,1)S(1)} %copy-done.1, bf16[2048,1024]{1,0:T(8,128)(2,1)S(1)} %bitcast.34, f32[1,128]{1,0:T(1,128)S(1)} %bitcast.39, f32[256,128]{1,0:T(8,128)S(1)} %get-tuple-element.37.q_a, ...), custom_call_target="tpu_custom_call" | custom-call | flops 2000000000 | bytes 3000000 | tf_op jit(solution)/shard_map/reply/pallas_call | solution.py:331
  68.3 0.8 collective-permute-done.10.r3
  69.1 1.4 %normed.1 = (bf16[256,512]{1,0:T(8,128)(2,1)S(1)}, f32[4,256,256]{2,1,0:T(8,128)S(1)}) custom-call(s32[4]{0:T(128)S(1)} %pad_add_fusion.place, f32[128,128]{1,0:T(8,128)S(1)} %get-tuple-element.33.r0, f32[128,128]{1,0:T(8,128)S(1)} %collective-permute-done.8.r1, f32[128,128]{1,0:T(8,128)S(1)} %collective-permute-done.9.r2, ...), custom_call_target="tpu_custom_call" | custom-call | tf_op jit(solution)/shard_map/normed/pallas_call | solution.py:372
  70.8 1.0 %own.1 = f32[4,256,256]{2,1,0:T(8,128)S(1)} custom-call(s32[4]{0:T(128)S(1)} %pad_add_fusion.place, bf16[256,512]{1,0:T(8,128)(2,1)S(1)} %get-tuple-element.47.normed, bf16[512,2048]{1,0:T(8,128)(2,1)S(1)} %copy-done), custom_call_target="tpu_custom_call" | custom-call | flops 1000000000 | bytes 3000000 | tf_op jit(solution)/shard_map/own/pallas_call | solution.py:382
  71.8 1.6 %collective-permute-done.11 = f32[4,256,256]{2,1,0:T(8,128)S(1)} collective-permute-done((f32[4,256,256]{2,1,0:T(8,128)S(1)}, f32[4,256,256]{2,1,0:T(8,128)S(1)}, u32[]{:S(2)}, u32[]{:S(2)}) %collective-permute-start.11) | collective-permute-done | bytes 1048608 | tf_op jit(solution)/shard_map/ppermute | solution.py:289
  73.5 0.9 collective-permute-start.14
  74.4 2.4 %collective-permute-start.12 = (f32[128,256]{1,0:T(8,128)S(1)}, f32[128,256]{1,0:T(8,128)S(1)}, u32[]{:S(2)}, u32[]{:S(2)}) collective-permute-start(f32[128,256]{1,0:T(8,128)S(1)} %get-tuple-element.54), channel_id=1, source_target_pairs={{0,2},{2,4},{4,6},{6,0},{1,3},{3,5},{5,7},{7,1},{8,10},{10,12},{12... | collective-permute-start | bytes 393224 | tf_op jit(solution)/shard_map/ppermute | solution.py:293
  77.0 3.3 %collective-permute-done.14 = f32[128,256]{1,0:T(8,128)S(1)} collective-permute-done((f32[128,256]{1,0:T(8,128)S(1)}, f32[128,256]{1,0:T(8,128)S(1)}, u32[]{:S(2)}, u32[]{:S(2)}) %collective-permute-start.14) | collective-permute-done | bytes 131104 | tf_op jit(solution)/shard_map/ppermute | solution.py:293
  80.4 3.0 %collective-permute-start.13 = (f32[256,256]{1,0:T(8,128)S(1)}, f32[256,256]{1,0:T(8,128)S(1)}, u32[]{:S(2)}, u32[]{:S(2)}) collective-permute-start(f32[256,256]{1,0:T(8,128)S(1)} %pad_maximum_fusion), channel_id=1, source_target_pairs={{0,2},{2,4},{4,6},{6,0},{1,3},{3,5},{5,7},{7,1},{8,10},{10,12},{12... | collective-permute-start | bytes 786440 | tf_op jit(solution)/shard_map/ppermute | solution.py:293
  83.5 4.6 %collective-permute-done.13 = f32[256,256]{1,0:T(8,128)S(1)} collective-permute-done((f32[256,256]{1,0:T(8,128)S(1)}, f32[256,256]{1,0:T(8,128)S(1)}, u32[]{:S(2)}, u32[]{:S(2)}) %collective-permute-start.13) | collective-permute-done | bytes 262176 | tf_op jit(solution)/shard_map/ppermute | solution.py:293
  88.1 3.5 %collective-permute-done.15 = f32[256,256]{1,0:T(8,128)S(1)} collective-permute-done((f32[256,256]{1,0:T(8,128)S(1)}, f32[256,256]{1,0:T(8,128)S(1)}, u32[]{:S(2)}, u32[]{:S(2)}) %collective-permute-start.15) | collective-permute-done | bytes 262176 | tf_op jit(solution)/shard_map/ppermute | solution.py:293
  91.6 0.7 fusion.1
  (40 shorter events, 3.7 us)
Async XLA Ops:
  0.8 9.9 %collective-permute-start = (f32[8,2048]{1,0:T(8,128)S(1)}, f32[8,2048]{1,0:T(8,128)S(1)}, u32[]{:S(2)}, u32[]{:S(2)}) collective-permute-start(f32[8,2048]{1,0:T(8,128)S(1)} %slice_convert_fusion), channel_id=1, source_target_pairs={{0,8},{8,16},{16,24},{24,32},{32,40},{40,48},{48,56},{56,64},{64,7... | collective-permute-start | bytes 196616 | tf_op jit(solution)/shard_map/ppermute | solution.py:323
  4.6 2.8 %copy-start.9 = (bf16[2048,2,512]{2,1,0:T(2,128)(2,1)S(1)}, bf16[2048,2,512]{2,1,0:T(2,128)(2,1)}, u32[]{:S(2)}) copy-start(bf16[2048,2,512]{2,1,0:T(2,128)(2,1)} %param.13) | copy-start | bytes 12582916
  7.4 3.2 %copy-start.1 = (bf16[256,2048]{1,0:T(8,128)(2,1)S(1)}, bf16[256,2048]{1,0:T(8,128)(2,1)}, u32[]{:S(2)}) copy-start(bf16[256,2048]{1,0:T(8,128)(2,1)} %tokens.5) | copy-start | bytes 3145732
  7.4 3.2 %copy-start.2 = (bf16[2048,2,4]{0,2,1:T(4,128)(2,1)S(1)}, bf16[2048,2,4]{0,2,1:T(4,128)(2,1)}, u32[]{:S(2)}) copy-start(bf16[2048,2,4]{0,2,1:T(4,128)(2,1)} %param.14) | copy-start | bytes 98308
  7.4 3.2 %copy-start.3 = (f32[4,2,256]{2,1,0:T(2,128)S(1)}, f32[4,2,256]{2,1,0:T(2,128)}, u32[]{:S(2)}) copy-start(f32[4,2,256]{2,1,0:T(2,128)} %taps_qk.3) | copy-start | bytes 24580
  7.4 3.2 %copy-start.4 = (f32[4,512]{1,0:T(4,128)S(1)}, f32[4,512]{1,0:T(4,128)}, u32[]{:S(2)}) copy-start(f32[4,512]{1,0:T(4,128)} %taps_v.3) | copy-start | bytes 24580
  7.4 3.2 %copy-start.5 = (f32[4]{0:T(128)S(1)}, f32[4]{0:T(128)}, u32[]{:S(2)}) copy-start(f32[4]{0:T(128)} %a_log.3) | copy-start | bytes 52
  7.4 3.2 %copy-start.6 = (f32[4]{0:T(128)S(1)}, f32[4]{0:T(128)}, u32[]{:S(2)}) copy-start(f32[4]{0:T(128)} %dt_bias.3) | copy-start | bytes 52
  7.5 3.2 %copy-start.7 = (f32[4]{0:T(128)S(1)}, f32[4]{0:T(128)}, u32[]{:S(2)}) copy-start(f32[4]{0:T(128)} %beta_bias.3) | copy-start | bytes 52
  18.2 12.8 %collective-permute-start.2 = (f32[128,256]{1,0:T(8,128)S(1)}, f32[128,256]{1,0:T(8,128)S(1)}, u32[]{:S(2)}, u32[]{:S(2)}) collective-permute-start(f32[128,256]{1,0:T(8,128)S(1)} %get-tuple-element.29), channel_id=1, source_target_pairs={{0,16},{8,24},{16,0},{24,8},{32,48},{40,56},{48,32},{56,40},{1,17}... | collective-permute-start | bytes 393224 | tf_op jit(solution)/shard_map/ppermute | solution.py:289
  19.6 45.7 %copy-start.8 = (f32[128]{0:T(128)S(1)}, f32[128]{0:T(128)}, u32[]{:S(2)}) copy-start(f32[128]{0:T(128)} %param.20) | copy-start | bytes 1540
  19.7 11.3 %collective-permute-start.3 = (f32[128,256]{1,0:T(8,128)S(1)}, f32[128,256]{1,0:T(8,128)S(1)}, u32[]{:S(2)}, u32[]{:S(2)}) collective-permute-start(f32[128,256]{1,0:T(8,128)S(1)} %get-tuple-element.30), channel_id=1, source_target_pairs={{0,24},{8,16},{16,8},{24,0},{32,56},{40,48},{48,40},{56,32},{1,25}... | collective-permute-start | bytes 393224 | tf_op jit(solution)/shard_map/ppermute | solution.py:289
  30.0 5.1 %collective-permute-start.1 = (f32[128,256]{1,0:T(8,128)S(1)}, f32[128,256]{1,0:T(8,128)S(1)}, u32[]{:S(2)}, u32[]{:S(2)}) collective-permute-start(f32[128,256]{1,0:T(8,128)S(1)} %get-tuple-element.28), channel_id=1, source_target_pairs={{0,8},{8,0},{16,24},{24,16},{32,40},{40,32},{48,56},{56,48},{1,9},... | collective-permute-start | bytes 393224 | tf_op jit(solution)/shard_map/ppermute | solution.py:289
  36.1 10.4 %collective-permute-start.4 = (f32[128,256]{1,0:T(8,128)S(1)}, f32[128,256]{1,0:T(8,128)S(1)}, u32[]{:S(2)}, u32[]{:S(2)}) collective-permute-start(f32[128,256]{1,0:T(8,128)S(1)} %get-tuple-element.31.own), channel_id=1, source_target_pairs={{0,32},{8,40},{16,48},{24,56},{32,0},{40,8},{48,16},{56,24},{1,33}... | collective-permute-start | bytes 393224 | tf_op jit(solution)/shard_map/ppermute | solution.py:289
  47.2 7.4 %collective-permute-start.7 = (f32[128,256]{1,0:T(8,128)S(1)}, f32[128,256]{1,0:T(8,128)S(1)}, u32[]{:S(2)}, u32[]{:S(2)}) collective-permute-start(f32[128,256]{1,0:T(8,128)S(1)} %row.1), channel_id=1, source_target_pairs={{0,192},{1,193},{2,194},{3,195},{4,196},{5,197},{6,198},{7,199},{8... | collective-permute-start | bytes 393224 | tf_op jit(solution)/shard_map/ppermute | solution.py:297
  47.9 7.3 %collective-permute-start.6 = (f32[128,256]{1,0:T(8,128)S(1)}, f32[128,256]{1,0:T(8,128)S(1)}, u32[]{:S(2)}, u32[]{:S(2)}) collective-permute-start(f32[128,256]{1,0:T(8,128)S(1)} %row.1), channel_id=1, source_target_pairs={{0,128},{64,192},{1,129},{65,193},{2,130},{66,194},{3,131},{67,195... | collective-permute-start | bytes 393224 | tf_op jit(solution)/shard_map/ppermute | solution.py:297
  52.8 6.9 %collective-permute-start.5 = (f32[128,256]{1,0:T(8,128)S(1)}, f32[128,256]{1,0:T(8,128)S(1)}, u32[]{:S(2)}, u32[]{:S(2)}) collective-permute-start(f32[128,256]{1,0:T(8,128)S(1)} %row.1), channel_id=1, source_target_pairs={{0,64},{64,128},{128,192},{1,65},{65,129},{129,193},{2,66},{66,130... | collective-permute-start | bytes 393224 | tf_op jit(solution)/shard_map/ppermute | solution.py:297
  60.9 7.3 %collective-permute-start.8 = (f32[128,128]{1,0:T(8,128)S(1)}, f32[128,128]{1,0:T(8,128)S(1)}, u32[]{:S(2)}, u32[]{:S(2)}) collective-permute-start(f32[128,128]{1,0:T(8,128)S(1)} %get-tuple-element.34), channel_id=1, source_target_pairs={{0,8},{8,0},{16,24},{24,16},{32,40},{40,32},{48,56},{56,48},{1,9},... | collective-permute-start | bytes 196616 | tf_op jit(solution)/shard_map/ppermute | solution.py:289
  61.0 7.2 %collective-permute-start.9 = (f32[128,128]{1,0:T(8,128)S(1)}, f32[128,128]{1,0:T(8,128)S(1)}, u32[]{:S(2)}, u32[]{:S(2)}) collective-permute-start(f32[128,128]{1,0:T(8,128)S(1)} %get-tuple-element.35), channel_id=1, source_target_pairs={{0,16},{8,24},{16,0},{24,8},{32,48},{40,56},{48,32},{56,40},{1,17}... | collective-permute-start | bytes 196616 | tf_op jit(solution)/shard_map/ppermute | solution.py:289
  62.9 6.2 %collective-permute-start.10 = (f32[128,128]{1,0:T(8,128)S(1)}, f32[128,128]{1,0:T(8,128)S(1)}, u32[]{:S(2)}, u32[]{:S(2)}) collective-permute-start(f32[128,128]{1,0:T(8,128)S(1)} %get-tuple-element.36), channel_id=1, source_target_pairs={{0,24},{8,16},{16,8},{24,0},{32,56},{40,48},{48,40},{56,32},{1,25}... | collective-permute-start | bytes 196616 | tf_op jit(solution)/shard_map/ppermute | solution.py:289
  65.4 3.7 %copy-start = (bf16[512,2048]{1,0:T(8,128)(2,1)S(1)}, bf16[512,2048]{1,0:T(8,128)(2,1)}, u32[]{:S(2)}) copy-start(bf16[512,2048]{1,0:T(8,128)(2,1)} %w_out.3) | copy-start | bytes 6291460
  70.5 3.0 %collective-permute-start.11 = (f32[4,256,256]{2,1,0:T(8,128)S(1)}, f32[4,256,256]{2,1,0:T(8,128)S(1)}, u32[]{:S(2)}, u32[]{:S(2)}) collective-permute-start(f32[4,256,256]{2,1,0:T(8,128)S(1)} %get-tuple-element.48), channel_id=1, source_target_pairs={{0,1},{1,0},{2,3},{3,2},{4,5},{5,4},{6,7},{7,6},{8,9},{9,8},{10,11... | collective-permute-start | bytes 3145736 | tf_op jit(solution)/shard_map/ppermute | solution.py:289
  73.5 6.8 %collective-permute-start.14 = (f32[128,256]{1,0:T(8,128)S(1)}, f32[128,256]{1,0:T(8,128)S(1)}, u32[]{:S(2)}, u32[]{:S(2)}) collective-permute-start(f32[128,256]{1,0:T(8,128)S(1)} %get-tuple-element.53), channel_id=1, source_target_pairs={{0,6},{2,0},{4,2},{6,4},{1,7},{3,1},{5,3},{7,5},{8,14},{10,8},{12,... | collective-permute-start | bytes 393224 | tf_op jit(solution)/shard_map/ppermute | solution.py:293
  74.4 5.9 %collective-permute-start.12 = (f32[128,256]{1,0:T(8,128)S(1)}, f32[128,256]{1,0:T(8,128)S(1)}, u32[]{:S(2)}, u32[]{:S(2)}) collective-permute-start(f32[128,256]{1,0:T(8,128)S(1)} %get-tuple-element.54), channel_id=1, source_target_pairs={{0,2},{2,4},{4,6},{6,0},{1,3},{3,5},{5,7},{7,1},{8,10},{10,12},{12... | collective-permute-start | bytes 393224 | tf_op jit(solution)/shard_map/ppermute | solution.py:293
  80.4 7.7 %collective-permute-start.13 = (f32[256,256]{1,0:T(8,128)S(1)}, f32[256,256]{1,0:T(8,128)S(1)}, u32[]{:S(2)}, u32[]{:S(2)}) collective-permute-start(f32[256,256]{1,0:T(8,128)S(1)} %pad_maximum_fusion), channel_id=1, source_target_pairs={{0,2},{2,4},{4,6},{6,0},{1,3},{3,5},{5,7},{7,1},{8,10},{10,12},{12... | collective-permute-start | bytes 786440 | tf_op jit(solution)/shard_map/ppermute | solution.py:293
  83.4 8.2 %collective-permute-start.15 = (f32[256,256]{1,0:T(8,128)S(1)}, f32[256,256]{1,0:T(8,128)S(1)}, u32[]{:S(2)}, u32[]{:S(2)}) collective-permute-start(f32[256,256]{1,0:T(8,128)S(1)} %pad_maximum_fusion.1), channel_id=1, source_target_pairs={{0,6},{2,0},{4,2},{6,4},{1,7},{3,1},{5,3},{7,5},{8,14},{10,8},{12,... | collective-permute-start | bytes 786440 | tf_op jit(solution)/shard_map/ppermute | solution.py:293

commit v3 on v2

v3 whole, which is shorter than its diff:
```python
import functools

import jax
import jax.numpy as jnp
from jax import lax
from jax.experimental import pallas as pl
from jax.experimental.pallas import tpu as pltpu
from jax.sharding import Mesh, PartitionSpec as P

F32 = jnp.float32
BF16 = jnp.bfloat16
DK = 128
DV = 128
HALF = 128
SEG = 256
VH = 4
QKH = 2
EPS = 1e-06
FLOOR = -110.0

VMEM = pl.BlockSpec(memory_space=pltpu.VMEM)
SMEM = pl.BlockSpec(memory_space=pltpu.SMEM)


def params(mib):
    return pltpu.CompilerParams(vmem_limit_bytes=mib * 1024 * 1024)


def split2(x):
    hi = x.astype(BF16)
    return hi, (x - hi.astype(F32)).astype(BF16)


def split3(x):
    hi = x.astype(BF16)
    rest = x - hi.astype(F32)
    mid = rest.astype(BF16)
    return hi, mid, (rest - mid.astype(F32)).astype(BF16)


def mm(a, b):
    return jnp.dot(a, b, preferred_element_type=F32)


def mm_nt(a, b):
    return lax.dot_general(a, b, (((1,), (1,)), ((), ())), preferred_element_type=F32)


def dot3(a, b):
    ah, al = split2(a)
    bh, bl = split2(b)
    return mm(jnp.concatenate([ah, al, ah], 1), jnp.concatenate([bh, bh, bl], 0))


def dot3_nt(a, b):
    ah, al = split2(a)
    bh, bl = split2(b)
    return mm_nt(jnp.concatenate([ah, al, ah], 1), jnp.concatenate([bh, bh, bl], 1))


def spread_blocks(x):
    zero = jnp.zeros((HALF, HALF), x.dtype)
    return jnp.concatenate(
        [
            jnp.concatenate([x[:, :HALF], zero], 1),
            jnp.concatenate([zero, x[:, HALF:]], 1),
        ],
        0,
    )


def dot3_blocks(a, b):
    ah, al = split2(a)
    bh, bl = split2(b)
    bh, bl = spread_blocks(bh), spread_blocks(bl)
    return mm(jnp.concatenate([ah, al, ah], 1), jnp.concatenate([bh, bh, bl], 0))


def iota2(shape, dim):
    return lax.broadcasted_iota(jnp.int32, shape, dim)


def silu(x):
    return x / (1.0 + jnp.exp(-x))


def softplus(x):
    return jnp.maximum(x, 0.0) + jnp.log1p(jnp.exp(-jnp.abs(x)))


def unit(x):
    return x * lax.rsqrt(jnp.sum(x * x, -1, keepdims=True) + EPS)


def fades(decay_col, lower):
    rows, cols = iota2((SEG, SEG), 0), iota2((SEG, SEG), 1)
    terms = jnp.where(rows > cols, jnp.broadcast_to(decay_col, (SEG, SEG)), 0.0)
    hi, mid, lo = split3(terms)
    return jnp.exp(mm(lower, hi) + mm(lower, mid) + mm(lower, lo))


def lower_ones():
    rows, cols = iota2((SEG, SEG), 0), iota2((SEG, SEG), 1)
    return jnp.where(rows >= cols, 1.0, 0.0).astype(BF16)


def dot3_parts(ah, al, bh, bl):
    return mm(jnp.concatenate([ah, al, ah], 1), jnp.concatenate([bh, bh, bl], 0))


def conv(pad, block, tap):
    total = None
    for j in range(4):
        term = pad[block, 5 + j : 5 + j + SEG, :] * tap(j)
        total = term if total is None else total + term
    return silu(total)


def project(pad, tok, before, w, block, count):
    full, front = mm(tok, w), mm(before, w)
    for i in range(count):
        pad[block + i, 0:8, :] = front[:, i * 128 : (i + 1) * 128]
        pad[block + i, 8:, :] = full[:, i * 128 : (i + 1) * 128]


def sums_of(parts, weights):
    return jnp.exp(sum(mm(weights, part) for part in parts))


def affine_maps(keys, grams, values, col8, slots):
    rows, cols = iota2((SEG, SEG), 0), iota2((SEG, SEG), 1)
    lower = lower_ones()
    later = jnp.where(rows < cols, 1.0, 0.0).astype(BF16)
    parts = split3(col8)
    growth8, closing8 = sums_of(parts, lower), sums_of(parts, later)
    n = range(len(slots))
    beta = [col8[:, c : c + 1] for c in slots]
    growth = [growth8[:, 4 + c : 5 + c] for c in slots]
    closing = [closing8[:, 4 + c : 5 + c] for c in slots]
    prow, pcol = iota2((HALF, HALF), 0), iota2((HALF, HALF), 1)
    strict = prow > pcol
    eye = jnp.where(prow == pcol, 1.0, 0.0)
    m, corner = [], []
    for i in n:
        u = fades(col8[:, 4 + slots[i] : 5 + slots[i]], lower) * grams[i] * beta[i]
        m += [
            jnp.where(strict, u[:HALF, :HALF], 0.0),
            jnp.where(strict, u[HALF:, HALF:], 0.0),
        ]
        corner.append(u[HALF:, :HALF])
    def within(low, high):
        return ((prow >> high) == (pcol >> high)) & ((prow >> low) != (pcol >> low))

    def mul(a, b):
        return [dot3_parts(*p, *q) for p, q in zip(a, b)]

    def halves(a):
        return [split2(u) for u in a]

    def finish(inv, power):
        square = halves(mul(power, power))
        inv = [u + w for u, w in zip(inv, mul(square, halves(inv)))]
        fourth = halves(mul(square, square))
        return [u + w for u, w in zip(inv, mul(fourth, halves(inv)))]

    near_diag = [jnp.where(within(0, 3), u, 0.0) for u in m]
    t = finish([eye - u for u in near_diag], halves(near_diag))
    ts = halves(t)
    power = halves(mul(ts, halves([jnp.where(within(3, 6), u, 0.0) for u in m])))
    t = finish([u - w for u, w in zip(t, mul(power, ts))], power)
    ts = halves(t)
    inner = halves(mul(halves([jnp.where(within(6, 7), u, 0.0) for u in m]), ts))
    t = [u - w for u, w in zip(t, mul(ts, inner))]
    right = [jnp.concatenate([keys[i] * growth[i], values[i]], 1) * beta[i] for i in n]
    x1 = [dot3(t[2 * i], right[i][:HALF]) for i in n]
    later_half = [dot3(t[2 * i + 1], right[i][HALF:]) for i in n]
    carry = [dot3(t[2 * i + 1], corner[i]) for i in n]
    x2 = [later_half[i] - dot3(carry[i], x1[i]) for i in n]
    ef = [jnp.concatenate([x1[i], x2[i]], 0) for i in n]
    both = [dot3((keys[i] * closing[i]).T, ef[i]) for i in n]
    maps = [
        jnp.concatenate([growth[i][SEG - 1 : SEG] * eye - both[i][:, :DK], both[i][:, DK:]], 1)
        for i in n
    ]
    return maps, ef


def segment_kernel(
    own_group, place, a_log, dt_bias, beta_bias, tokens, halo, w_qk, w_v, taps_qk, taps_v, w_ab,
    out0, out1, k_out, ef_out, cols_out, pad, logits, values,
):
    mine = place[0]
    group = (mine >> 1) if own_group else 1 - (mine >> 1)
    tok = tokens[...]
    before = halo[...].astype(BF16)
    wide = pl.ds(pl.multiple_of(group * 256, 256), 256)
    key_lanes = pl.ds(pl.multiple_of(256 + group * DK, DK), DK)

    def pick(taps, width):
        return jnp.where(group == 1, taps[:, width : 2 * width], taps[:, :width])

    logits[...] = mm_nt(tok, jnp.concatenate([w_ab[0], w_ab[1]], 0)).T
    project(pad, tok, before, w_qk[:, key_lanes], 0, 1)
    project(pad, tok, before, w_v[:, wide], 1, 2)
    betas, decays = [], []
    for slot in range(2):
        h = group * 2 + ((mine & 1) ^ slot)
        betas.append(jax.nn.sigmoid(logits[pl.ds(h, 1), :] + beta_bias[h]))
        rate = jnp.exp(jnp.full((1, SEG), a_log[h], F32))
        decay = -rate * softplus(logits[pl.ds(h + 4, 1), :] + dt_bias[h])
        decays.append(jnp.maximum(decay, FLOOR))
    blank = jnp.zeros((2, SEG), F32)
    col8 = jnp.concatenate(betas + [blank] + decays + [blank], 0).T
    cols_out[...] = col8
    k = unit(conv(pad, 0, lambda j: pick(taps_qk[j, 1:2, :], DK)))
    k_out[...] = k
    gram = dot3_nt(k, k)
    for i in range(2):
        values[i] = conv(
            pad, 1 + i, lambda j: pick(taps_v[j : j + 1, :], 256)[:, i * DV : (i + 1) * DV]
        )
    maps, ef = affine_maps(
        [k, k], [gram, gram], [values[(mine & 1) ^ i] for i in range(2)], col8, (0, 1)
    )
    for i, out in enumerate((out0, out1)):
        out[...] = maps[i]
        ef_out[i] = ef[i]


def reply_kernel(
    place, tokens, halo, w_q, w_z, taps_qk, gain, k_near, ef_near, cols_near, k_far, ef_far, cols_far,
    out, gates, pad, queries,
):
    rows, cols = iota2((SEG, SEG), 0), iota2((SEG, SEG), 1)
    lower = lower_ones()
    mine = place[0]
    tok = tokens[...]
    project(pad, tok, halo[...].astype(BF16), w_q[...], 0, 2)
    z = mm(tok, w_z[...])
    for h in range(VH):
        part = z[:, h * DV : (h + 1) * DV]
        gates[:, h * DV : (h + 1) * DV] = gain[...] * silu(part)
    for g in range(QKH):
        taps = lambda j: taps_qk[j, 0:1, g * DK : (g + 1) * DK]
        queries[g] = unit(conv(pad, g, taps)) * DK ** -0.5
    for side, k, ef, cols8 in ((0, k_near, ef_near, cols_near), (1, k_far, ef_far, cols_far)):
        q = queries[(mine >> 1) ^ side]
        col8 = cols8[...]
        growth8 = sums_of(split3(col8), lower)
        qk = dot3_nt(q, k[...])
        for i in range(2):
            fade = fades(col8[:, 4 + i : 5 + i], lower)
            mixing = jnp.where(rows >= cols, fade * qk, 0.0)
            both = dot3(mixing, ef[i])
            out[mine ^ (2 * side + i)] = jnp.concatenate(
                [q * growth8[:, 4 + i : 5 + i] - both[:, :DK], both[:, DK:]], 1
            )


def after(second, first):
    prod = dot3(second[:, :DK], first)
    return jnp.concatenate([prod[:, :DK], prod[:, DK:] + second[:, DK:]], 1)


def pair_kernel(place, r2, r3, out):
    odd = (place[0] & 1) == 1
    out[...] = after(
        jnp.where(odd, r2[...], r3[...]), jnp.where(odd, r3[...], r2[...])
    )


def quad_kernel(place, r0, r1, r2, r3, far, total, prefixes):
    odd, upper = (place[0] & 1) == 1, place[0] >= 2
    near_first = jnp.where(odd, r1[...], r0[...])
    near_second = jnp.where(odd, r0[...], r1[...])
    near = after(near_second, near_first)
    far_first = jnp.where(odd, r3[...], r2[...])
    first, second = jnp.where(upper, far[...], near), jnp.where(upper, near, far[...])
    total[...] = after(second, first)
    prefixes[0] = jnp.where(upper, far_first, near_first)
    prefixes[1] = first
    prefixes[2] = after(jnp.where(upper, near_first, far_first), first)


def row_kernel(place, own, other, out):
    behind = place[1] == 1
    first = jnp.where(behind, other[...], own[...])
    second = jnp.where(behind, own[...], other[...])
    out[...] = after(second, first)


def early_kernel(y2, y3, out):
    out[...] = dot3(y2[:, :DK], y3[:, DK:]) + y2[:, DK:]


def state_kernel(place, y1, early, other, prefixes, out0, out1, out2, out3, states):
    s = dot3(y1[:, :DK], early[...]) + y1[:, DK:]
    s = jnp.where(place[1] == 1, dot3(other[:, :DK], s) + other[:, DK:], s)
    states[0] = s
    for j in range(3):
        states[j + 1] = dot3(prefixes[j, :, :DK], s) + prefixes[j, :, DK:]
    mine = place[0]
    for slot, out in enumerate((out0, out1, out2, out3)):
        out[...] = states[mine ^ slot]


def normed_kernel(place, r0, r1, r2, r3, reply, gates, w_out, normed, out, states):
    mine = place[0]
    for slot, r in enumerate((r0, r1, r2, r3)):
        states[mine ^ slot] = r[...]
    for h in range(VH):
        core = dot3(reply[h, :, :DK], states[h]) + reply[h, :, DK:]
        scale = lax.rsqrt(jnp.mean(core * core, -1, keepdims=True) + EPS)
        normed[:, h * DV : (h + 1) * DV] = (core * scale * gates[:, h * DV : (h + 1) * DV]).astype(BF16)
    for step in range(4):
        out[step] = block_product(normed, w_out, place, step, 1 - place[3])


def block_product(normed, w_out, place, step, core):
    start = pl.multiple_of((((place[2] + step) & 3) * 2 + core) * 256, 256)
    return mm(normed[...], w_out[:, pl.ds(start, 256)])


def own_kernel(place, normed, w_out, own):
    for step in range(4):
        own[step] = block_product(normed, w_out, place, step, place[3])


def arr(*shape, dtype=F32):
    return jax.ShapeDtypeStruct(shape, dtype)


def swap(v, axis, size, mask):
    return lax.ppermute(v, axis, [(i, i ^ mask) for i in range(size)])


def shift(v, axis, size, step):
    return lax.ppermute(v, axis, [(i, (i + step) % size) for i in range(size)])


def forward(v, axis, size, step):
    return lax.ppermute(v, axis, [(i, i + step) for i in range(size - step)])


def local(tokens, w_qk, w_vz, w_ab, conv_qk, conv_v, a_log, dt_bias, beta_bias, norm_gain, w_out):
    y, z = lax.axis_index("y"), lax.axis_index("z")
    x, core = lax.axis_index("x"), lax.axis_index("core")
    place = jnp.stack([z & 3, z >> 2, x, core]).astype(jnp.int32)

    tail = tokens[SEG - 8 :].astype(F32)
    halo = lax.ppermute(tail, ("y", "z"), [(i, i + 1) for i in range(31)])
    flat_qk = w_qk.reshape(w_qk.shape[0], 2 * QKH * DK)
    flat_vz = w_vz.reshape(w_vz.shape[0], 2 * VH * DV)
    ab = w_ab.transpose(1, 2, 0)
    width = tokens.shape[1]
    half_of = lambda size, c: pl.BlockSpec((width, size), lambda i: (0, c))

    def segment(own_group):
        return pl.pallas_call(
            functools.partial(segment_kernel, own_group),
            grid=(1,),
            out_shape=[arr(DK, 256)] * 2 + [arr(SEG, DK), arr(2, SEG, 256), arr(SEG, 8)],
            in_specs=[SMEM] * 4 + [VMEM, VMEM, VMEM, half_of(VH * DV, 0)] + [VMEM] * 3,
            out_specs=[VMEM] * 5,
            scratch_shapes=[
                pltpu.VMEM((3, SEG + 8, DK), F32),
                pltpu.VMEM((8, SEG), F32),
                pltpu.VMEM((2, SEG, DV), F32),
            ],
            compiler_params=params(28),
            cost_estimate=pl.CostEstimate(
                flops=6 * 10**9, bytes_accessed=6 * 10**6, transcendentals=0
            ),
            name="segment_own" if own_group else "segment_other",
        )(place, a_log, dt_bias, beta_bias, tokens, halo, flat_qk, flat_vz, conv_qk, conv_v, ab)

    far = segment(False)
    near = segment(True)
    got = [near[0], swap(near[1], "z", 8, 1), swap(far[0], "z", 8, 2), swap(far[1], "z", 8, 3)]
    reply, gates = pl.pallas_call(
        reply_kernel,
        grid=(1,),
        out_shape=[arr(VH, SEG, 256), arr(SEG, VH * DV)],
        in_specs=[SMEM, VMEM, VMEM, half_of(QKH * DK, 0), half_of(VH * DV, 1)] + [VMEM] * 8,
        out_specs=[VMEM] * 2,
        scratch_shapes=[pltpu.VMEM((2, SEG + 8, DK), F32), pltpu.VMEM((QKH, SEG, DK), F32)],
        compiler_params=params(28),
        cost_estimate=pl.CostEstimate(flops=4 * 10**9, bytes_accessed=3 * 10**6, transcendentals=0),
        name="reply",
    )(place, tokens, halo, flat_qk, flat_vz, conv_qk, norm_gain.reshape(1, DV), *near[2:], *far[2:])

    far_pair = pl.pallas_call(
        pair_kernel,
        out_shape=arr(DK, 256),
        in_specs=[SMEM] + [VMEM] * 2,
        out_specs=VMEM,
        compiler_params=params(16),
        name="pair",
    )(place, *got[2:])
    total, prefixes = pl.pallas_call(
        quad_kernel,
        out_shape=[arr(DK, 256), arr(3, DK, 256)],
        in_specs=[SMEM] + [VMEM] * 5,
        out_specs=[VMEM] * 2,
        compiler_params=params(16),
        name="quad",
    )(place, *got, far_pair)
    other = swap(total, "z", 8, 4)
    row = pl.pallas_call(
        row_kernel,
        out_shape=arr(DK, 256),
        in_specs=[SMEM] + [VMEM] * 2,
        out_specs=VMEM,
        compiler_params=params(16),
        name="row",
    )(place, total, other)
    rows = [forward(row, "y", 4, d) for d in (1, 2, 3)]
    early = pl.pallas_call(
        early_kernel,
        out_shape=arr(DK, DV),
        in_specs=[VMEM] * 2,
        out_specs=VMEM,
        compiler_params=params(16),
        name="early",
    )(*rows[1:])
    states = pl.pallas_call(
        state_kernel,
        out_shape=[arr(DK, DV)] * 4,
        in_specs=[SMEM] + [VMEM] * 4,
        out_specs=[VMEM] * 4,
        scratch_shapes=[pltpu.VMEM((4, DK, DV), F32)],
        compiler_params=params(16),
        name="state",
    )(place, rows[0], early, other, prefixes)
    came = [states[0]] + [swap(states[m], "z", 8, m) for m in (1, 2, 3)]

    normed, for_twin = pl.pallas_call(
        normed_kernel,
        out_shape=[arr(SEG, VH * DV, dtype=BF16), arr(4, SEG, 256)],
        in_specs=[SMEM] + [VMEM] * 7,
        out_specs=[VMEM] * 2,
        scratch_shapes=[pltpu.VMEM((4, DK, DV), F32)],
        compiler_params=params(24),
        name="normed",
    )(place, *came, reply, gates, w_out)
    from_twin = swap(for_twin, "core", 2, 1)
    own = pl.pallas_call(
        own_kernel,
        out_shape=arr(4, SEG, 256),
        in_specs=[SMEM] + [VMEM] * 2,
        out_specs=VMEM,
        compiler_params=params(24),
        cost_estimate=pl.CostEstimate(flops=10**9, bytes_accessed=3 * 10**6, transcendentals=0),
        name="own",
    )(place, normed, w_out)

    from_left = shift(own[2, :HALF] + from_twin[2, :HALF], "x", 4, 1)
    from_right = shift(own[2, HALF:] + from_twin[2, HALF:], "x", 4, -1)
    right = own[1] + from_twin[1]
    left = own[3] + from_twin[3]
    to_right = jnp.concatenate([right[:HALF] + from_left, right[HALF:]], 0)
    to_left = jnp.concatenate([left[:HALF], left[HALF:] + from_right], 0)
    last_left = shift(to_right, "x", 4, 1)
    last_right = shift(to_left, "x", 4, -1)
    return ((own[0] + from_twin[0]) + (last_left + last_right)).astype(BF16)


def solution(mesh):
    split = Mesh(mesh.devices.reshape(4, 8, 4, 2), ("y", "z", "x", "core"))
    seq, head = ("y", "z"), ("x", "core")
    in_specs = (
        P(seq, None),
        P(None, None, head),
        P(None, None, head),
        P(None, None, head),
        P(None, None, head),
        P(None, head),
        P(head),
        P(head),
        P(head),
        P(),
        P(head, None),
    )
    return jax.shard_map(
        local, mesh=split, in_specs=in_specs, out_specs=P(seq, head), check_vma=False
    )
```

time: 92.6 us -> 86.5 us (0.934)
  Pallas kernels: 23.3 us -> 19.1 us
  starting transfers between devices: 30.8 us -> 29.1 us
    pallas_call x2 -> x4, Pallas kernels: 15 us -> 10.6 us  [the longest x2 9.67 us: segment(): pl.pallas_call(functools.partial(segment_kernel, own_group), grid=(1,), o...]
    ppermute x4, starting transfers between devices: 6.43 us -> 4.28 us  [shift(): return lax.ppermute(v, axis, [(i, (i + step) % size) for i in range(size)])]
    ppermute x8, starting transfers between devices: 13.1 us -> 14.2 us  [swap(): return lax.ppermute(v, axis, [(i, i ^ mask) for i in range(size)])]
where the time goes in v3:
time: 86.5 us; the launch traced here: 86.2 us
  waiting for transfers between devices  31.9 us (37%)
  starting transfers between devices  29.1 us (34%)
  Pallas kernels  19.1 us (22%)
  local copies, waits for them, and re-layouts  4.06 us (5%)
  other arithmetic  1.74 us (2%)
    ppermute x8, starting transfers between devices, swap(): return lax.ppermute(v, axis, [(i, i ^ mask) for i in range(size)])  14.2 us
    ppermute x8, waiting for transfers between devices, swap(): return lax.ppermute(v, axis, [(i, i ^ mask) for i in range(size)])  13.7 us
    ppermute x4, waiting for transfers between devices, shift(): return lax.ppermute(v, axis, [(i, (i + step) % size) for i in range(size)])  11.6 us
    pallas_call x2, Pallas kernels, segment(): pl.pallas_call(functools.partial(segment_kernel, own_group), grid=(1,), o...  9.67 us
    ppermute x3, starting transfers between devices, forward(): return lax.ppermute(v, axis, [(i, i + step) for i in range(size - step)])  6.82 us
    ppermute x3, waiting for transfers between devices, forward(): return lax.ppermute(v, axis, [(i, i + step) for i in range(size - step)])  4.74 us
    ppermute x4, starting transfers between devices, shift(): return lax.ppermute(v, axis, [(i, (i + step) % size) for i in range(size)])  4.28 us
    unnamed x22, local copies, waits for them, and re-layouts  4.04 us
  transfers between devices with their start and end apart: 16, of which 11 were waited for; matrix products, arithmetic and copies ran while one was open for 4% of the time, Pallas kernels for 12%

profile of v3, /device:TPU:14, one launch (start us, length us, event | category | flops | bytes accessed | tf_op | source)
XLA Modules:
  0.0 86.2 jit_solution(9638693515556103859)
XLA Ops:
  0.0 0.8 slice_convert_fusion
  0.8 3.8 %collective-permute-start = (f32[8,2048]{1,0:T(8,128)S(1)}, f32[8,2048]{1,0:T(8,128)S(1)}, u32[]{:S(2)}, u32[]{:S(2)}) collective-permute-start(f32[8,2048]{1,0:T(8,128)S(1)} %slice_convert_fusion), channel_id=1, source_target_pairs={{0,8},{8,16},{16,24},{24,32},{32,40},{40,48},{48,56},{56,64},{64,7... | collective-permute-start | bytes 196616 | tf_op jit(solution)/shard_map/ppermute | solution.py:351
  4.6 2.2 %copy.12 = bf16[256,8,2,256]{3,1,2,0:T(8,128)(2,1)S(1)} copy(bf16[256,8,2,256]{3,2,1,0:T(2,128)(2,1)} %bitcast.42) | data formatting | bytes 4194304
  7.5 1.2 %copy.13 = bf16[256,8,2,512]{3,1,2,0:T(8,128)(2,1)S(1)} copy(bf16[256,8,2,512]{3,2,1,0:T(2,128)(2,1)S(1)} %bitcast.41) | data formatting | bytes 8388608
  8.7 1.9 %collective-permute-done.halo = f32[8,2048]{1,0:T(8,128)S(1)} collective-permute-done((f32[8,2048]{1,0:T(8,128)S(1)}, f32[8,2048]{1,0:T(8,128)S(1)}, u32[]{:S(2)}, u32[]{:S(2)}) %collective-permute-start) | collective-permute-done | bytes 65568 | tf_op jit(solution)/shard_map/ppermute | solution.py:351
  10.7 4.8 %segment_other.1 = (f32[128,256]{1,0:T(8,128)S(1)}, f32[128,256]{1,0:T(8,128)S(1)}, f32[256,128]{1,0:T(8,128)S(1)}, f32[2,256,256]{2,1,0:T(8,128)S(1)}, f32[256,8]{1,0:T(8,128)S(1)}) custom-call(s32[4]{0:T(128)S(1)} %pad_add_fusion.place, f32[4]{0:T(128)S(1)} %copy-done.5, f32[4]{0:T(128)S(1)} %copy-done.6, f32[4]{0:T(128)S(1)} %copy-done.7, ...), custom_call_target="tpu_custom_call" | custom-call | flops 6000000000 | bytes 6000000 | tf_op jit(solution)/shard_map/segment_other/pallas_call | solution.py:359
  15.5 1.5 %collective-permute-start.2 = (f32[128,256]{1,0:T(8,128)S(1)}, f32[128,256]{1,0:T(8,128)S(1)}, u32[]{:S(2)}, u32[]{:S(2)}) collective-permute-start(f32[128,256]{1,0:T(8,128)S(1)} %get-tuple-element.27), channel_id=1, source_target_pairs={{0,16},{8,24},{16,0},{24,8},{32,48},{40,56},{48,32},{56,40},{1,17}... | collective-permute-start | bytes 393224 | tf_op jit(solution)/shard_map/ppermute | solution.py:334
  17.0 2.7 %collective-permute-start.3 = (f32[128,256]{1,0:T(8,128)S(1)}, f32[128,256]{1,0:T(8,128)S(1)}, u32[]{:S(2)}, u32[]{:S(2)}) collective-permute-start(f32[128,256]{1,0:T(8,128)S(1)} %get-tuple-element.28), channel_id=1, source_target_pairs={{0,24},{8,16},{16,8},{24,0},{32,56},{40,48},{48,40},{56,32},{1,25}... | collective-permute-start | bytes 393224 | tf_op jit(solution)/shard_map/ppermute | solution.py:334
  19.7 4.8 %segment_own.1 = (f32[128,256]{1,0:T(8,128)S(1)}, f32[128,256]{1,0:T(8,128)S(1)}, f32[256,128]{1,0:T(8,128)S(1)}, f32[2,256,256]{2,1,0:T(8,128)S(1)}, f32[256,8]{1,0:T(8,128)S(1)}) custom-call(s32[4]{0:T(128)S(1)} %pad_add_fusion.place, f32[4]{0:T(128)S(1)} %copy-done.5, f32[4]{0:T(128)S(1)} %copy-done.6, f32[4]{0:T(128)S(1)} %copy-done.7, ...), custom_call_target="tpu_custom_call" | custom-call | flops 6000000000 | bytes 6000000 | tf_op jit(solution)/shard_map/segment_own/pallas_call | solution.py:359
  25.1 3.2 %collective-permute-done.2.r2 = f32[128,256]{1,0:T(8,128)S(1)} collective-permute-done((f32[128,256]{1,0:T(8,128)S(1)}, f32[128,256]{1,0:T(8,128)S(1)}, u32[]{:S(2)}, u32[]{:S(2)}) %collective-permute-start.2) | collective-permute-done | bytes 131104 | tf_op jit(solution)/shard_map/ppermute | solution.py:334
  28.3 0.7 pair.1.far
  29.1 1.2 %collective-permute-done.1.r1 = f32[128,256]{1,0:T(8,128)S(1)} collective-permute-done((f32[128,256]{1,0:T(8,128)S(1)}, f32[128,256]{1,0:T(8,128)S(1)}, u32[]{:S(2)}, u32[]{:S(2)}) %collective-permute-start.1) | collective-permute-done | bytes 131104 | tf_op jit(solution)/shard_map/ppermute | solution.py:334
  30.2 1.0 %quad.1 = (f32[128,256]{1,0:T(8,128)S(1)}, f32[3,128,256]{2,1,0:T(8,128)S(1)}) custom-call(s32[4]{0:T(128)S(1)} %pad_add_fusion.place, f32[128,256]{1,0:T(8,128)S(1)} %get-tuple-element.25.r0, f32[128,256]{1,0:T(8,128)S(1)} %collective-permute-done.1.r1, f32[128,256]{1,0:T(8,128)S(1)} %collective-permute-done.2.r2, ...), custom_call_target="tpu_custom_call" | custom-call | tf_op jit(solution)/shard_map/quad/pallas_call | solution.py:400
  31.2 4.3 %collective-permute-start.4 = (f32[128,256]{1,0:T(8,128)S(1)}, f32[128,256]{1,0:T(8,128)S(1)}, u32[]{:S(2)}, u32[]{:S(2)}) collective-permute-start(f32[128,256]{1,0:T(8,128)S(1)} %get-tuple-element.29.own), channel_id=1, source_target_pairs={{0,32},{8,40},{16,48},{24,56},{32,0},{40,8},{48,16},{56,24},{1,33}... | collective-permute-start | bytes 393224 | tf_op jit(solution)/shard_map/ppermute | solution.py:334
  35.5 6.3 %collective-permute-done.4.other = f32[128,256]{1,0:T(8,128)S(1)} collective-permute-done((f32[128,256]{1,0:T(8,128)S(1)}, f32[128,256]{1,0:T(8,128)S(1)}, u32[]{:S(2)}, u32[]{:S(2)}) %collective-permute-start.4) | collective-permute-done | bytes 131104 | tf_op jit(solution)/shard_map/ppermute | solution.py:334
  42.6 4.2 %collective-permute-start.6 = (f32[128,256]{1,0:T(8,128)S(1)}, f32[128,256]{1,0:T(8,128)S(1)}, u32[]{:S(2)}, u32[]{:S(2)}) collective-permute-start(f32[128,256]{1,0:T(8,128)S(1)} %row.1), channel_id=1, source_target_pairs={{0,128},{64,192},{1,129},{65,193},{2,130},{66,194},{3,131},{67,195... | collective-permute-start | bytes 393224 | tf_op jit(solution)/shard_map/ppermute | solution.py:342
  47.5 1.9 %collective-permute-start.5 = (f32[128,256]{1,0:T(8,128)S(1)}, f32[128,256]{1,0:T(8,128)S(1)}, u32[]{:S(2)}, u32[]{:S(2)}) collective-permute-start(f32[128,256]{1,0:T(8,128)S(1)} %row.1), channel_id=1, source_target_pairs={{0,64},{64,128},{128,192},{1,65},{65,129},{129,193},{2,66},{66,130... | collective-permute-start | bytes 393224 | tf_op jit(solution)/shard_map/ppermute | solution.py:342
  49.6 4.7 %collective-permute-done.5.y1 = f32[128,256]{1,0:T(8,128)S(1)} collective-permute-done((f32[128,256]{1,0:T(8,128)S(1)}, f32[128,256]{1,0:T(8,128)S(1)}, u32[]{:S(2)}, u32[]{:S(2)}) %collective-permute-start.5) | collective-permute-done | bytes 131104 | tf_op jit(solution)/shard_map/ppermute | solution.py:342
  54.3 1.1 %state.1 = (f32[128,128]{1,0:T(8,128)S(1)}, f32[128,128]{1,0:T(8,128)S(1)}, f32[128,128]{1,0:T(8,128)S(1)}, f32[128,128]{1,0:T(8,128)S(1)}) custom-call(s32[4]{0:T(128)S(1)} %pad_add_fusion.place, f32[128,256]{1,0:T(8,128)S(1)} %collective-permute-done.5.y1, f32[128,128]{1,0:T(8,128)S(1)} %early.1, f32[128,256]{1,0:T(8,128)S(1)} %collective-permute-done.4.other, ...), custom_call_target="tpu_custom_call" | custom-call | tf_op jit(solution)/shard_map/state/pallas_call | solution.py:426
  55.5 2.3 %collective-permute-start.8 = (f32[128,128]{1,0:T(8,128)S(1)}, f32[128,128]{1,0:T(8,128)S(1)}, u32[]{:S(2)}, u32[]{:S(2)}) collective-permute-start(f32[128,128]{1,0:T(8,128)S(1)} %get-tuple-element.32), channel_id=1, source_target_pairs={{0,8},{8,0},{16,24},{24,16},{32,40},{40,32},{48,56},{56,48},{1,9},... | collective-permute-start | bytes 196616 | tf_op jit(solution)/shard_map/ppermute | solution.py:334
  57.8 1.4 %collective-permute-start.9 = (f32[128,128]{1,0:T(8,128)S(1)}, f32[128,128]{1,0:T(8,128)S(1)}, u32[]{:S(2)}, u32[]{:S(2)}) collective-permute-start(f32[128,128]{1,0:T(8,128)S(1)} %get-tuple-element.33), channel_id=1, source_target_pairs={{0,16},{8,24},{16,0},{24,8},{32,48},{40,56},{48,32},{56,40},{1,17}... | collective-permute-start | bytes 196616 | tf_op jit(solution)/shard_map/ppermute | solution.py:334
  59.1 1.4 %collective-permute-start.10 = (f32[128,128]{1,0:T(8,128)S(1)}, f32[128,128]{1,0:T(8,128)S(1)}, u32[]{:S(2)}, u32[]{:S(2)}) collective-permute-start(f32[128,128]{1,0:T(8,128)S(1)} %get-tuple-element.34), channel_id=1, source_target_pairs={{0,24},{8,16},{16,8},{24,0},{32,56},{40,48},{48,40},{56,32},{1,25}... | collective-permute-start | bytes 196616 | tf_op jit(solution)/shard_map/ppermute | solution.py:334
  60.5 3.3 %reply.1 = (f32[4,256,256]{2,1,0:T(8,128)S(1)}, f32[256,512]{1,0:T(8,128)S(1)}) custom-call(s32[4]{0:T(128)S(1)} %pad_add_fusion.place, bf16[256,2048]{1,0:T(8,128)(2,1)S(1)} %copy-done.1, f32[8,2048]{1,0:T(8,128)S(1)} %collective-permute-done.halo, bf16[2048,512]{1,0:T(8,128)(2,1)S(1)} %bitcast.37, bf16[2048,1024]{1,0:T(8,128)(2,1)S(1)} %bitcast.34, ...), custom_call_target="tpu_custom_call" | custom-call | flops 4000000000 | bytes 3000000 | tf_op jit(solution)/shard_map/reply/pallas_call | solution.py:380
  64.3 1.0 %collective-permute-done.10.r3 = f32[128,128]{1,0:T(8,128)S(1)} collective-permute-done((f32[128,128]{1,0:T(8,128)S(1)}, f32[128,128]{1,0:T(8,128)S(1)}, u32[]{:S(2)}, u32[]{:S(2)}) %collective-permute-start.10) | collective-permute-done | bytes 65568 | tf_op jit(solution)/shard_map/ppermute | solution.py:334
  65.2 1.4 %normed.1 = (bf16[256,512]{1,0:T(8,128)(2,1)S(1)}, f32[4,256,256]{2,1,0:T(8,128)S(1)}) custom-call(s32[4]{0:T(128)S(1)} %pad_add_fusion.place, f32[128,128]{1,0:T(8,128)S(1)} %get-tuple-element.31.r0, f32[128,128]{1,0:T(8,128)S(1)} %collective-permute-done.8.r1, f32[128,128]{1,0:T(8,128)S(1)} %collective-permute-done.9.r2, ...), custom_call_target="tpu_custom_call" | custom-call | tf_op jit(solution)/shard_map/normed/pallas_call | solution.py:437
  66.7 1.0 %own.1 = f32[4,256,256]{2,1,0:T(8,128)S(1)} custom-call(s32[4]{0:T(128)S(1)} %pad_add_fusion.place, bf16[256,512]{1,0:T(8,128)(2,1)S(1)} %get-tuple-element.43.normed, bf16[512,2048]{1,0:T(8,128)(2,1)S(1)} %copy-done), custom_call_target="tpu_custom_call" | custom-call | flops 1000000000 | bytes 3000000 | tf_op jit(solution)/shard_map/own/pallas_call | solution.py:447
  67.7 1.6 %collective-permute-done.11 = f32[4,256,256]{2,1,0:T(8,128)S(1)} collective-permute-done((f32[4,256,256]{2,1,0:T(8,128)S(1)}, f32[4,256,256]{2,1,0:T(8,128)S(1)}, u32[]{:S(2)}, u32[]{:S(2)}) %collective-permute-start.11) | collective-permute-done | bytes 1048608 | tf_op jit(solution)/shard_map/ppermute | solution.py:334
  70.1 1.6 %collective-permute-start.14 = (f32[128,256]{1,0:T(8,128)S(1)}, f32[128,256]{1,0:T(8,128)S(1)}, u32[]{:S(2)}, u32[]{:S(2)}) collective-permute-start(f32[128,256]{1,0:T(8,128)S(1)} %get-tuple-element.47), channel_id=1, source_target_pairs={{0,6},{2,0},{4,2},{6,4},{1,7},{3,1},{5,3},{7,5},{8,14},{10,8},{12,... | collective-permute-start | bytes 393224 | tf_op jit(solution)/shard_map/ppermute | solution.py:338
  71.6 3.5 %collective-permute-done.12 = f32[128,256]{1,0:T(8,128)S(1)} collective-permute-done((f32[128,256]{1,0:T(8,128)S(1)}, f32[128,256]{1,0:T(8,128)S(1)}, u32[]{:S(2)}, u32[]{:S(2)}) %collective-permute-start.12) | collective-permute-done | bytes 131104 | tf_op jit(solution)/shard_map/ppermute | solution.py:338
  75.2 1.8 %collective-permute-start.13 = (f32[256,256]{1,0:T(8,128)S(1)}, f32[256,256]{1,0:T(8,128)S(1)}, u32[]{:S(2)}, u32[]{:S(2)}) collective-permute-start(f32[256,256]{1,0:T(8,128)S(1)} %pad_maximum_fusion), channel_id=1, source_target_pairs={{0,2},{2,4},{4,6},{6,0},{1,3},{3,5},{5,7},{7,1},{8,10},{10,12},{12... | collective-permute-start | bytes 786440 | tf_op jit(solution)/shard_map/ppermute | solution.py:338
  77.4 5.4 %collective-permute-done.13 = f32[256,256]{1,0:T(8,128)S(1)} collective-permute-done((f32[256,256]{1,0:T(8,128)S(1)}, f32[256,256]{1,0:T(8,128)S(1)}, u32[]{:S(2)}, u32[]{:S(2)}) %collective-permute-start.13) | collective-permute-done | bytes 262176 | tf_op jit(solution)/shard_map/ppermute | solution.py:338
  82.8 2.7 %collective-permute-done.15 = f32[256,256]{1,0:T(8,128)S(1)} collective-permute-done((f32[256,256]{1,0:T(8,128)S(1)}, f32[256,256]{1,0:T(8,128)S(1)}, u32[]{:S(2)}, u32[]{:S(2)}) %collective-permute-start.15) | collective-permute-done | bytes 262176 | tf_op jit(solution)/shard_map/ppermute | solution.py:338
  (43 shorter events, 5.3 us)
Async XLA Ops:
  0.8 9.9 %collective-permute-start = (f32[8,2048]{1,0:T(8,128)S(1)}, f32[8,2048]{1,0:T(8,128)S(1)}, u32[]{:S(2)}, u32[]{:S(2)}) collective-permute-start(f32[8,2048]{1,0:T(8,128)S(1)} %slice_convert_fusion), channel_id=1, source_target_pairs={{0,8},{8,16},{16,24},{24,32},{32,40},{40,48},{48,56},{56,64},{64,7... | collective-permute-start | bytes 196616 | tf_op jit(solution)/shard_map/ppermute | solution.py:351
  4.6 2.8 %copy-start.9 = (bf16[2048,2,512]{2,1,0:T(2,128)(2,1)S(1)}, bf16[2048,2,512]{2,1,0:T(2,128)(2,1)}, u32[]{:S(2)}) copy-start(bf16[2048,2,512]{2,1,0:T(2,128)(2,1)} %param.13) | copy-start | bytes 12582916
  7.4 3.2 %copy-start.1 = (bf16[256,2048]{1,0:T(8,128)(2,1)S(1)}, bf16[256,2048]{1,0:T(8,128)(2,1)}, u32[]{:S(2)}) copy-start(bf16[256,2048]{1,0:T(8,128)(2,1)} %tokens.5) | copy-start | bytes 3145732
  7.4 3.2 %copy-start.2 = (bf16[2048,2,4]{0,2,1:T(4,128)(2,1)S(1)}, bf16[2048,2,4]{0,2,1:T(4,128)(2,1)}, u32[]{:S(2)}) copy-start(bf16[2048,2,4]{0,2,1:T(4,128)(2,1)} %param.14) | copy-start | bytes 98308
  7.4 3.2 %copy-start.3 = (f32[4,512]{1,0:T(4,128)S(1)}, f32[4,512]{1,0:T(4,128)}, u32[]{:S(2)}) copy-start(f32[4,512]{1,0:T(4,128)} %taps_v.3) | copy-start | bytes 24580
  7.4 3.2 %copy-start.4 = (f32[4,2,256]{2,1,0:T(2,128)S(1)}, f32[4,2,256]{2,1,0:T(2,128)}, u32[]{:S(2)}) copy-start(f32[4,2,256]{2,1,0:T(2,128)} %taps_qk.5) | copy-start | bytes 24580
  7.4 3.2 %copy-start.5 = (f32[4]{0:T(128)S(1)}, f32[4]{0:T(128)}, u32[]{:S(2)}) copy-start(f32[4]{0:T(128)} %a_log.3) | copy-start | bytes 52
  7.4 3.2 %copy-start.6 = (f32[4]{0:T(128)S(1)}, f32[4]{0:T(128)}, u32[]{:S(2)}) copy-start(f32[4]{0:T(128)} %dt_bias.3) | copy-start | bytes 52
  7.5 3.2 %copy-start.7 = (f32[4]{0:T(128)S(1)}, f32[4]{0:T(128)}, u32[]{:S(2)}) copy-start(f32[4]{0:T(128)} %beta_bias.3) | copy-start | bytes 52
  15.5 12.8 %collective-permute-start.2 = (f32[128,256]{1,0:T(8,128)S(1)}, f32[128,256]{1,0:T(8,128)S(1)}, u32[]{:S(2)}, u32[]{:S(2)}) collective-permute-start(f32[128,256]{1,0:T(8,128)S(1)} %get-tuple-element.27), channel_id=1, source_target_pairs={{0,16},{8,24},{16,0},{24,8},{32,48},{40,56},{48,32},{56,40},{1,17}... | collective-permute-start | bytes 393224 | tf_op jit(solution)/shard_map/ppermute | solution.py:334
  17.0 11.3 %collective-permute-start.3 = (f32[128,256]{1,0:T(8,128)S(1)}, f32[128,256]{1,0:T(8,128)S(1)}, u32[]{:S(2)}, u32[]{:S(2)}) collective-permute-start(f32[128,256]{1,0:T(8,128)S(1)} %get-tuple-element.28), channel_id=1, source_target_pairs={{0,24},{8,16},{16,8},{24,0},{32,56},{40,48},{48,40},{56,32},{1,25}... | collective-permute-start | bytes 393224 | tf_op jit(solution)/shard_map/ppermute | solution.py:334
  24.5 35.9 %copy-start.8 = (f32[128]{0:T(128)S(1)}, f32[128]{0:T(128)}, u32[]{:S(2)}) copy-start(f32[128]{0:T(128)} %param.20) | copy-start | bytes 1540
  24.5 5.7 %collective-permute-start.1 = (f32[128,256]{1,0:T(8,128)S(1)}, f32[128,256]{1,0:T(8,128)S(1)}, u32[]{:S(2)}, u32[]{:S(2)}) collective-permute-start(f32[128,256]{1,0:T(8,128)S(1)} %get-tuple-element.26), channel_id=1, source_target_pairs={{0,8},{8,0},{16,24},{24,16},{32,40},{40,32},{48,56},{56,48},{1,9},... | collective-permute-start | bytes 393224 | tf_op jit(solution)/shard_map/ppermute | solution.py:334
  31.2 10.6 %collective-permute-start.4 = (f32[128,256]{1,0:T(8,128)S(1)}, f32[128,256]{1,0:T(8,128)S(1)}, u32[]{:S(2)}, u32[]{:S(2)}) collective-permute-start(f32[128,256]{1,0:T(8,128)S(1)} %get-tuple-element.29.own), channel_id=1, source_target_pairs={{0,32},{8,40},{16,48},{24,56},{32,0},{40,8},{48,16},{56,24},{1,33}... | collective-permute-start | bytes 393224 | tf_op jit(solution)/shard_map/ppermute | solution.py:334
  42.6 6.8 %collective-permute-start.6 = (f32[128,256]{1,0:T(8,128)S(1)}, f32[128,256]{1,0:T(8,128)S(1)}, u32[]{:S(2)}, u32[]{:S(2)}) collective-permute-start(f32[128,256]{1,0:T(8,128)S(1)} %row.1), channel_id=1, source_target_pairs={{0,128},{64,192},{1,129},{65,193},{2,130},{66,194},{3,131},{67,195... | collective-permute-start | bytes 393224 | tf_op jit(solution)/shard_map/ppermute | solution.py:342
  46.8 2.6 %collective-permute-start.7 = (f32[128,256]{1,0:T(8,128)S(1)}, f32[128,256]{1,0:T(8,128)S(1)}, u32[]{:S(2)}, u32[]{:S(2)}) collective-permute-start(f32[128,256]{1,0:T(8,128)S(1)} %row.1), channel_id=1, source_target_pairs={{0,192},{1,193},{2,194},{3,195},{4,196},{5,197},{6,198},{7,199},{8... | collective-permute-start | bytes 393224 | tf_op jit(solution)/shard_map/ppermute | solution.py:342
  47.5 6.9 %collective-permute-start.5 = (f32[128,256]{1,0:T(8,128)S(1)}, f32[128,256]{1,0:T(8,128)S(1)}, u32[]{:S(2)}, u32[]{:S(2)}) collective-permute-start(f32[128,256]{1,0:T(8,128)S(1)} %row.1), channel_id=1, source_target_pairs={{0,64},{64,128},{128,192},{1,65},{65,129},{129,193},{2,66},{66,130... | collective-permute-start | bytes 393224 | tf_op jit(solution)/shard_map/ppermute | solution.py:342
  55.5 8.4 %collective-permute-start.8 = (f32[128,128]{1,0:T(8,128)S(1)}, f32[128,128]{1,0:T(8,128)S(1)}, u32[]{:S(2)}, u32[]{:S(2)}) collective-permute-start(f32[128,128]{1,0:T(8,128)S(1)} %get-tuple-element.32), channel_id=1, source_target_pairs={{0,8},{8,0},{16,24},{24,16},{32,40},{40,32},{48,56},{56,48},{1,9},... | collective-permute-start | bytes 196616 | tf_op jit(solution)/shard_map/ppermute | solution.py:334
  57.8 6.5 %collective-permute-start.9 = (f32[128,128]{1,0:T(8,128)S(1)}, f32[128,128]{1,0:T(8,128)S(1)}, u32[]{:S(2)}, u32[]{:S(2)}) collective-permute-start(f32[128,128]{1,0:T(8,128)S(1)} %get-tuple-element.33), channel_id=1, source_target_pairs={{0,16},{8,24},{16,0},{24,8},{32,48},{40,56},{48,32},{56,40},{1,17}... | collective-permute-start | bytes 196616 | tf_op jit(solution)/shard_map/ppermute | solution.py:334
  59.1 6.1 %collective-permute-start.10 = (f32[128,128]{1,0:T(8,128)S(1)}, f32[128,128]{1,0:T(8,128)S(1)}, u32[]{:S(2)}, u32[]{:S(2)}) collective-permute-start(f32[128,128]{1,0:T(8,128)S(1)} %get-tuple-element.34), channel_id=1, source_target_pairs={{0,24},{8,16},{16,8},{24,0},{32,56},{40,48},{48,40},{56,32},{1,25}... | collective-permute-start | bytes 196616 | tf_op jit(solution)/shard_map/ppermute | solution.py:334
  60.5 4.8 %copy-start = (bf16[512,2048]{1,0:T(8,128)(2,1)S(1)}, bf16[512,2048]{1,0:T(8,128)(2,1)}, u32[]{:S(2)}) copy-start(bf16[512,2048]{1,0:T(8,128)(2,1)} %w_out.3) | copy-start | bytes 6291460
  66.6 2.7 %collective-permute-start.11 = (f32[4,256,256]{2,1,0:T(8,128)S(1)}, f32[4,256,256]{2,1,0:T(8,128)S(1)}, u32[]{:S(2)}, u32[]{:S(2)}) collective-permute-start(f32[4,256,256]{2,1,0:T(8,128)S(1)} %get-tuple-element.44), channel_id=1, source_target_pairs={{0,1},{1,0},{2,3},{3,2},{4,5},{5,4},{6,7},{7,6},{8,9},{9,8},{10,11... | collective-permute-start | bytes 3145736 | tf_op jit(solution)/shard_map/ppermute | solution.py:334
  69.5 5.6 %collective-permute-start.12 = (f32[128,256]{1,0:T(8,128)S(1)}, f32[128,256]{1,0:T(8,128)S(1)}, u32[]{:S(2)}, u32[]{:S(2)}) collective-permute-start(f32[128,256]{1,0:T(8,128)S(1)} %get-tuple-element.48), channel_id=1, source_target_pairs={{0,2},{2,4},{4,6},{6,0},{1,3},{3,5},{5,7},{7,1},{8,10},{10,12},{12... | collective-permute-start | bytes 393224 | tf_op jit(solution)/shard_map/ppermute | solution.py:338
  70.1 6.9 %collective-permute-start.14 = (f32[128,256]{1,0:T(8,128)S(1)}, f32[128,256]{1,0:T(8,128)S(1)}, u32[]{:S(2)}, u32[]{:S(2)}) collective-permute-start(f32[128,256]{1,0:T(8,128)S(1)} %get-tuple-element.47), channel_id=1, source_target_pairs={{0,6},{2,0},{4,2},{6,4},{1,7},{3,1},{5,3},{7,5},{8,14},{10,8},{12,... | collective-permute-start | bytes 393224 | tf_op jit(solution)/shard_map/ppermute | solution.py:338
  75.2 7.6 %collective-permute-start.13 = (f32[256,256]{1,0:T(8,128)S(1)}, f32[256,256]{1,0:T(8,128)S(1)}, u32[]{:S(2)}, u32[]{:S(2)}) collective-permute-start(f32[256,256]{1,0:T(8,128)S(1)} %pad_maximum_fusion), channel_id=1, source_target_pairs={{0,2},{2,4},{4,6},{6,0},{1,3},{3,5},{5,7},{7,1},{8,10},{10,12},{12... | collective-permute-start | bytes 786440 | tf_op jit(solution)/shard_map/ppermute | solution.py:338
  77.0 8.5 %collective-permute-start.15 = (f32[256,256]{1,0:T(8,128)S(1)}, f32[256,256]{1,0:T(8,128)S(1)}, u32[]{:S(2)}, u32[]{:S(2)}) collective-permute-start(f32[256,256]{1,0:T(8,128)S(1)} %pad_maximum_fusion.1), channel_id=1, source_target_pairs={{0,6},{2,0},{4,2},{6,4},{1,7},{3,1},{5,3},{7,5},{8,14},{10,8},{12,... | collective-permute-start | bytes 786440 | tf_op jit(solution)/shard_map/ppermute | solution.py:338

commit v4 on v3

--- a/solution.py
+++ b/solution.py
@@ -106,6 +106,10 @@
 
 def dot3_parts(ah, al, bh, bl):
     return mm(jnp.concatenate([ah, al, ah], 1), jnp.concatenate([bh, bh, bl], 0))
+
+
+def halo_rows(halo):
+    return jnp.concatenate([jnp.zeros((4, halo.shape[1]), F32), halo[...]], 0).astype(BF16)
 
 
 def conv(pad, block, tap):
@@ -192,7 +196,7 @@
     mine = place[0]
     group = (mine >> 1) if own_group else 1 - (mine >> 1)
     tok = tokens[...]
-    before = halo[...].astype(BF16)
+    before = halo_rows(halo)
     wide = pl.ds(pl.multiple_of(group * 256, 256), 256)
     key_lanes = pl.ds(pl.multiple_of(256 + group * DK, DK), DK)
 
@@ -235,7 +239,7 @@
     lower = lower_ones()
     mine = place[0]
     tok = tokens[...]
-    project(pad, tok, halo[...].astype(BF16), w_q[...], 0, 2)
+    project(pad, tok, halo_rows(halo), w_q[...], 0, 2)
     z = mm(tok, w_z[...])
     for h in range(VH):
         part = z[:, h * DV : (h + 1) * DV]
@@ -269,20 +273,24 @@
     )
 
 
-def quad_kernel(place, r0, r1, r2, r3, far, total, prefixes):
+def quad_kernel(place, r0, r1, far, total, first_pair):
+    odd, upper = (place[0] & 1) == 1, place[0] >= 2
+    near = after(jnp.where(odd, r0[...], r1[...]), jnp.where(odd, r1[...], r0[...]))
+    first, second = jnp.where(upper, far[...], near), jnp.where(upper, near, far[...])
+    total[...] = after(second, first)
+    first_pair[...] = first
+
+
+def prefix_kernel(place, r0, r1, r2, r3, first_pair, prefixes):
     odd, upper = (place[0] & 1) == 1, place[0] >= 2
     near_first = jnp.where(odd, r1[...], r0[...])
-    near_second = jnp.where(odd, r0[...], r1[...])
-    near = after(near_second, near_first)
     far_first = jnp.where(odd, r3[...], r2[...])
-    first, second = jnp.where(upper, far[...], near), jnp.where(upper, near, far[...])
-    total[...] = after(second, first)
     prefixes[0] = jnp.where(upper, far_first, near_first)
-    prefixes[1] = first
-    prefixes[2] = after(jnp.where(upper, near_first, far_first), first)
-
-
-def row_kernel(place, own, other, out):
+    prefixes[1] = first_pair[...]
+    prefixes[2] = after(jnp.where(upper, near_first, far_first), first_pair[...])
+
+
+def row_kernel(place, own, other, after_reply, after_prefixes, out):
     behind = place[1] == 1
     first = jnp.where(behind, other[...], own[...])
     second = jnp.where(behind, own[...], other[...])
@@ -347,7 +355,7 @@
     x, core = lax.axis_index("x"), lax.axis_index("core")
     place = jnp.stack([z & 3, z >> 2, x, core]).astype(jnp.int32)
 
-    tail = tokens[SEG - 8 :].astype(F32)
+    tail = tokens[SEG - 4 :].astype(F32)
     halo = lax.ppermute(tail, ("y", "z"), [(i, i + 1) for i in range(31)])
     flat_qk = w_qk.reshape(w_qk.shape[0], 2 * QKH * DK)
     flat_vz = w_vz.reshape(w_vz.shape[0], 2 * VH * DV)
@@ -397,23 +405,31 @@
         compiler_params=params(16),
         name="pair",
     )(place, *got[2:])
-    total, prefixes = pl.pallas_call(
+    total, first_pair = pl.pallas_call(
         quad_kernel,
-        out_shape=[arr(DK, 256), arr(3, DK, 256)],
-        in_specs=[SMEM] + [VMEM] * 5,
+        out_shape=[arr(DK, 256)] * 2,
+        in_specs=[SMEM] + [VMEM] * 3,
         out_specs=[VMEM] * 2,
         compiler_params=params(16),
         name="quad",
-    )(place, *got, far_pair)
+    )(place, got[0], got[1], far_pair)
+    prefixes = pl.pallas_call(
+        prefix_kernel,
+        out_shape=arr(3, DK, 256),
+        in_specs=[SMEM] + [VMEM] * 5,
+        out_specs=VMEM,
+        compiler_params=params(16),
+        name="prefix",
+    )(place, *got, first_pair)
     other = swap(total, "z", 8, 4)
     row = pl.pallas_call(
         row_kernel,
         out_shape=arr(DK, 256),
-        in_specs=[SMEM] + [VMEM] * 2,
+        in_specs=[SMEM] + [VMEM] * 4,
         out_specs=VMEM,
         compiler_params=params(16),
         name="row",
-    )(place, total, other)
+    )(place, total, other, gates, prefixes)
     rows = [forward(row, "y", 4, d) for d in (1, 2, 3)]
     early = pl.pallas_call(
         early_kernel,
@@ -462,7 +478,7 @@
     to_left = jnp.concatenate([left[:HALF], left[HALF:] + from_right], 0)
     last_left = shift(to_right, "x", 4, 1)
     last_right = shift(to_left, "x", 4, -1)
-    return ((own[0] + from_twin[0]) + (last_left + last_right)).astype(BF16)
+    return ((own[0] + from_twin[0]) + (last_right + last_left)).astype(BF16)
 
 
 def solution(mesh):

time: 86.5 us -> 85.7 us (level)
  waiting for transfers between devices: 31.9 us -> 28.8 us
  starting transfers between devices: 29.1 us -> 30.6 us
    ppermute x8, waiting for transfers between devices: 13.7 us -> 11.2 us  [swap(): return lax.ppermute(v, axis, [(i, i ^ mask) for i in range(size)])]
    ppermute x8, starting transfers between devices: 14.2 us -> 15.3 us  [swap(): return lax.ppermute(v, axis, [(i, i ^ mask) for i in range(size)])]
  transfers between devices with their start and end apart: 16 -> 16, of which waited for: 11 -> 12; matrix products, arithmetic and copies ran while one was open for 4% -> 5% of each run, Pallas kernels for 12% -> 13%
where the time goes in v4:
time: 85.7 us; the launch traced here: 85.4 us
  starting transfers between devices  30.6 us (36%)
  waiting for transfers between devices  28.8 us (34%)
  Pallas kernels  19.8 us (23%)
  local copies, waits for them, and re-layouts  4.13 us (5%)
  other arithmetic  1.73 us (2%)
    ppermute x8, starting transfers between devices, swap(): return lax.ppermute(v, axis, [(i, i ^ mask) for i in range(size)])  15.3 us
    ppermute x4, waiting for transfers between devices, shift(): return lax.ppermute(v, axis, [(i, (i + step) % size) for i in range(size)])  11.4 us
    ppermute x8, waiting for transfers between devices, swap(): return lax.ppermute(v, axis, [(i, i ^ mask) for i in range(size)])  11.2 us
    pallas_call x2, Pallas kernels, segment(): pl.pallas_call(functools.partial(segment_kernel, own_group), grid=(1,), o...  9.65 us
    ppermute x3, starting transfers between devices, forward(): return lax.ppermute(v, axis, [(i, i + step) for i in range(size - step)])  7.13 us
    ppermute x3, waiting for transfers between devices, forward(): return lax.ppermute(v, axis, [(i, i + step) for i in range(size - step)])  4.74 us
    ppermute x4, starting transfers between devices, shift(): return lax.ppermute(v, axis, [(i, (i + step) % size) for i in range(size)])  4.36 us
    unnamed x22, local copies, waits for them, and re-layouts  4.11 us
  transfers between devices with their start and end apart: 16, of which 12 were waited for; matrix products, arithmetic and copies ran while one was open for 5% of the time, Pallas kernels for 13%

profile of v4, /device:TPU:14, one launch (start us, length us, event | category | flops | bytes accessed | tf_op | source)
XLA Modules:
  0.0 85.4 jit_solution(4753184014205228056)
XLA Ops:
  0.0 0.8 slice_convert_fusion
  0.8 3.8 %collective-permute-start = (f32[4,2048]{1,0:T(4,128)S(1)}, f32[4,2048]{1,0:T(4,128)S(1)}, u32[]{:S(2)}, u32[]{:S(2)}) collective-permute-start(f32[4,2048]{1,0:T(4,128)S(1)} %slice_convert_fusion), channel_id=1, source_target_pairs={{0,8},{8,16},{16,24},{24,32},{32,40},{40,48},{48,56},{56,64},{64,7... | collective-permute-start | bytes 98312 | tf_op jit(solution)/shard_map/ppermute | solution.py:359
  4.7 3.5 %copy.13 = bf16[256,8,2,512]{3,1,2,0:T(8,128)(2,1)S(1)} copy(bf16[256,8,2,512]{3,2,1,0:T(2,128)(2,1)} %bitcast.41) | data formatting | bytes 8388608
  8.8 1.5 %collective-permute-done.halo = f32[4,2048]{1,0:T(4,128)S(1)} collective-permute-done((f32[4,2048]{1,0:T(4,128)S(1)}, f32[4,2048]{1,0:T(4,128)S(1)}, u32[]{:S(2)}, u32[]{:S(2)}) %collective-permute-start) | collective-permute-done | bytes 32800 | tf_op jit(solution)/shard_map/ppermute | solution.py:359
  10.4 4.8 %segment_other.1 = (f32[128,256]{1,0:T(8,128)S(1)}, f32[128,256]{1,0:T(8,128)S(1)}, f32[256,128]{1,0:T(8,128)S(1)}, f32[2,256,256]{2,1,0:T(8,128)S(1)}, f32[256,8]{1,0:T(8,128)S(1)}) custom-call(s32[4]{0:T(128)S(1)} %pad_add_fusion.place, f32[4]{0:T(128)S(1)} %copy-done.5, f32[4]{0:T(128)S(1)} %copy-done.6, f32[4]{0:T(128)S(1)} %copy-done.7, ...), custom_call_target="tpu_custom_call" | custom-call | flops 6000000000 | bytes 6000000 | tf_op jit(solution)/shard_map/segment_other/pallas_call | solution.py:367
  15.2 2.5 %collective-permute-start.2 = (f32[128,256]{1,0:T(8,128)S(1)}, f32[128,256]{1,0:T(8,128)S(1)}, u32[]{:S(2)}, u32[]{:S(2)}) collective-permute-start(f32[128,256]{1,0:T(8,128)S(1)} %get-tuple-element.27), channel_id=1, source_target_pairs={{0,16},{8,24},{16,0},{24,8},{32,48},{40,56},{48,32},{56,40},{1,17}... | collective-permute-start | bytes 393224 | tf_op jit(solution)/shard_map/ppermute | solution.py:342
  17.7 2.7 %collective-permute-start.3 = (f32[128,256]{1,0:T(8,128)S(1)}, f32[128,256]{1,0:T(8,128)S(1)}, u32[]{:S(2)}, u32[]{:S(2)}) collective-permute-start(f32[128,256]{1,0:T(8,128)S(1)} %get-tuple-element.28), channel_id=1, source_target_pairs={{0,24},{8,16},{16,8},{24,0},{32,56},{40,48},{48,40},{56,32},{1,25}... | collective-permute-start | bytes 393224 | tf_op jit(solution)/shard_map/ppermute | solution.py:342
  20.4 4.8 %segment_own.1 = (f32[128,256]{1,0:T(8,128)S(1)}, f32[128,256]{1,0:T(8,128)S(1)}, f32[256,128]{1,0:T(8,128)S(1)}, f32[2,256,256]{2,1,0:T(8,128)S(1)}, f32[256,8]{1,0:T(8,128)S(1)}) custom-call(s32[4]{0:T(128)S(1)} %pad_add_fusion.place, f32[4]{0:T(128)S(1)} %copy-done.5, f32[4]{0:T(128)S(1)} %copy-done.6, f32[4]{0:T(128)S(1)} %copy-done.7, ...), custom_call_target="tpu_custom_call" | custom-call | flops 6000000000 | bytes 6000000 | tf_op jit(solution)/shard_map/segment_own/pallas_call | solution.py:367
  25.8 1.3 %collective-permute-done.2.r2 = f32[128,256]{1,0:T(8,128)S(1)} collective-permute-done((f32[128,256]{1,0:T(8,128)S(1)}, f32[128,256]{1,0:T(8,128)S(1)}, u32[]{:S(2)}, u32[]{:S(2)}) %collective-permute-start.2) | collective-permute-done | bytes 131104 | tf_op jit(solution)/shard_map/ppermute | solution.py:342
  27.0 0.7 pair.1.far
  27.8 2.5 %collective-permute-done.1.r1 = f32[128,256]{1,0:T(8,128)S(1)} collective-permute-done((f32[128,256]{1,0:T(8,128)S(1)}, f32[128,256]{1,0:T(8,128)S(1)}, u32[]{:S(2)}, u32[]{:S(2)}) %collective-permute-start.1) | collective-permute-done | bytes 131104 | tf_op jit(solution)/shard_map/ppermute | solution.py:342
  30.3 1.0 %quad.1 = (f32[128,256]{1,0:T(8,128)S(1)}, f32[128,256]{1,0:T(8,128)S(1)}) custom-call(s32[4]{0:T(128)S(1)} %pad_add_fusion.place, f32[128,256]{1,0:T(8,128)S(1)} %get-tuple-element.25.r0, f32[128,256]{1,0:T(8,128)S(1)} %collective-permute-done.1.r1, f32[128,256]{1,0:T(8,128)S(1)} %pair.1.far), custom_call_target="tpu_custom_call" | custom-call | tf_op jit(solution)/shard_map/quad/pallas_call | solution.py:408
  31.2 5.0 %collective-permute-start.4 = (f32[128,256]{1,0:T(8,128)S(1)}, f32[128,256]{1,0:T(8,128)S(1)}, u32[]{:S(2)}, u32[]{:S(2)}) collective-permute-start(f32[128,256]{1,0:T(8,128)S(1)} %get-tuple-element.29.own), channel_id=1, source_target_pairs={{0,32},{8,40},{16,48},{24,56},{32,0},{40,8},{48,16},{56,24},{1,33}... | collective-permute-start | bytes 393224 | tf_op jit(solution)/shard_map/ppermute | solution.py:342
  36.2 3.4 %reply.1 = (f32[4,256,256]{2,1,0:T(8,128)S(1)}, f32[256,512]{1,0:T(8,128)S(1)}) custom-call(s32[4]{0:T(128)S(1)} %pad_add_fusion.place, bf16[256,2048]{1,0:T(8,128)(2,1)S(1)} %copy-done.1, f32[4,2048]{1,0:T(4,128)S(1)} %collective-permute-done.halo, bf16[2048,512]{1,0:T(8,128)(2,1)S(1)} %bitcast.37, bf16[2048,1024]{1,0:T(8,128)(2,1)S(1)} %bitcast.34, ...), custom_call_target="tpu_custom_call" | custom-call | flops 4000000000 | bytes 3000000 | tf_op jit(solution)/shard_map/reply/pallas_call | solution.py:388
  40.3 1.6 %collective-permute-done.4.other = f32[128,256]{1,0:T(8,128)S(1)} collective-permute-done((f32[128,256]{1,0:T(8,128)S(1)}, f32[128,256]{1,0:T(8,128)S(1)}, u32[]{:S(2)}, u32[]{:S(2)}) %collective-permute-start.4) | collective-permute-done | bytes 131104 | tf_op jit(solution)/shard_map/ppermute | solution.py:342
  42.6 4.5 %collective-permute-start.6 = (f32[128,256]{1,0:T(8,128)S(1)}, f32[128,256]{1,0:T(8,128)S(1)}, u32[]{:S(2)}, u32[]{:S(2)}) collective-permute-start(f32[128,256]{1,0:T(8,128)S(1)} %row.1), channel_id=1, source_target_pairs={{0,128},{64,192},{1,129},{65,193},{2,130},{66,194},{3,131},{67,195... | collective-permute-start | bytes 393224 | tf_op jit(solution)/shard_map/ppermute | solution.py:350
  47.9 1.9 %collective-permute-start.5 = (f32[128,256]{1,0:T(8,128)S(1)}, f32[128,256]{1,0:T(8,128)S(1)}, u32[]{:S(2)}, u32[]{:S(2)}) collective-permute-start(f32[128,256]{1,0:T(8,128)S(1)} %row.1), channel_id=1, source_target_pairs={{0,64},{64,128},{128,192},{1,65},{65,129},{129,193},{2,66},{66,130... | collective-permute-start | bytes 393224 | tf_op jit(solution)/shard_map/ppermute | solution.py:350
  50.0 4.7 %collective-permute-done.5.y1 = f32[128,256]{1,0:T(8,128)S(1)} collective-permute-done((f32[128,256]{1,0:T(8,128)S(1)}, f32[128,256]{1,0:T(8,128)S(1)}, u32[]{:S(2)}, u32[]{:S(2)}) %collective-permute-start.5) | collective-permute-done | bytes 131104 | tf_op jit(solution)/shard_map/ppermute | solution.py:350
  54.7 1.1 %state.1 = (f32[128,128]{1,0:T(8,128)S(1)}, f32[128,128]{1,0:T(8,128)S(1)}, f32[128,128]{1,0:T(8,128)S(1)}, f32[128,128]{1,0:T(8,128)S(1)}) custom-call(s32[4]{0:T(128)S(1)} %pad_add_fusion.place, f32[128,256]{1,0:T(8,128)S(1)} %collective-permute-done.5.y1, f32[128,128]{1,0:T(8,128)S(1)} %early.1, f32[128,256]{1,0:T(8,128)S(1)} %collective-permute-done.4.other, ...), custom_call_target="tpu_custom_call" | custom-call | tf_op jit(solution)/shard_map/state/pallas_call | solution.py:442
  55.8 1.4 %collective-permute-start.10 = (f32[128,128]{1,0:T(8,128)S(1)}, f32[128,128]{1,0:T(8,128)S(1)}, u32[]{:S(2)}, u32[]{:S(2)}) collective-permute-start(f32[128,128]{1,0:T(8,128)S(1)} %get-tuple-element.41), channel_id=1, source_target_pairs={{0,24},{8,16},{16,8},{24,0},{32,56},{40,48},{48,40},{56,32},{1,25}... | collective-permute-start | bytes 196616 | tf_op jit(solution)/shard_map/ppermute | solution.py:342
  57.2 1.8 %collective-permute-start.8 = (f32[128,128]{1,0:T(8,128)S(1)}, f32[128,128]{1,0:T(8,128)S(1)}, u32[]{:S(2)}, u32[]{:S(2)}) collective-permute-start(f32[128,128]{1,0:T(8,128)S(1)} %get-tuple-element.39), channel_id=1, source_target_pairs={{0,8},{8,0},{16,24},{24,16},{32,40},{40,32},{48,56},{56,48},{1,9},... | collective-permute-start | bytes 196616 | tf_op jit(solution)/shard_map/ppermute | solution.py:342
  59.0 1.3 %collective-permute-start.9 = (f32[128,128]{1,0:T(8,128)S(1)}, f32[128,128]{1,0:T(8,128)S(1)}, u32[]{:S(2)}, u32[]{:S(2)}) collective-permute-start(f32[128,128]{1,0:T(8,128)S(1)} %get-tuple-element.40), channel_id=1, source_target_pairs={{0,16},{8,24},{16,0},{24,8},{32,48},{40,56},{48,32},{56,40},{1,17}... | collective-permute-start | bytes 196616 | tf_op jit(solution)/shard_map/ppermute | solution.py:342
  60.3 1.8 %collective-permute-done.10.r3 = f32[128,128]{1,0:T(8,128)S(1)} collective-permute-done((f32[128,128]{1,0:T(8,128)S(1)}, f32[128,128]{1,0:T(8,128)S(1)}, u32[]{:S(2)}, u32[]{:S(2)}) %collective-permute-start.10) | collective-permute-done | bytes 65568 | tf_op jit(solution)/shard_map/ppermute | solution.py:342
  62.4 2.1 %collective-permute-done.9.r2 = f32[128,128]{1,0:T(8,128)S(1)} collective-permute-done((f32[128,128]{1,0:T(8,128)S(1)}, f32[128,128]{1,0:T(8,128)S(1)}, u32[]{:S(2)}, u32[]{:S(2)}) %collective-permute-start.9) | collective-permute-done | bytes 65568 | tf_op jit(solution)/shard_map/ppermute | solution.py:342
  64.5 1.4 %normed.1 = (bf16[256,512]{1,0:T(8,128)(2,1)S(1)}, f32[4,256,256]{2,1,0:T(8,128)S(1)}) custom-call(s32[4]{0:T(128)S(1)} %pad_add_fusion.place, f32[128,128]{1,0:T(8,128)S(1)} %get-tuple-element.38.r0, f32[128,128]{1,0:T(8,128)S(1)} %collective-permute-done.8.r1, f32[128,128]{1,0:T(8,128)S(1)} %collective-permute-done.9.r2, ...), custom_call_target="tpu_custom_call" | custom-call | tf_op jit(solution)/shard_map/normed/pallas_call | solution.py:453
  66.0 1.0 %own.1 = f32[4,256,256]{2,1,0:T(8,128)S(1)} custom-call(s32[4]{0:T(128)S(1)} %pad_add_fusion.place, bf16[256,512]{1,0:T(8,128)(2,1)S(1)} %get-tuple-element.43.normed, bf16[512,2048]{1,0:T(8,128)(2,1)S(1)} %copy-done), custom_call_target="tpu_custom_call" | custom-call | flops 1000000000 | bytes 3000000 | tf_op jit(solution)/shard_map/own/pallas_call | solution.py:463
  67.0 1.6 %collective-permute-done.11 = f32[4,256,256]{2,1,0:T(8,128)S(1)} collective-permute-done((f32[4,256,256]{2,1,0:T(8,128)S(1)}, f32[4,256,256]{2,1,0:T(8,128)S(1)}, u32[]{:S(2)}, u32[]{:S(2)}) %collective-permute-start.11) | collective-permute-done | bytes 1048608 | tf_op jit(solution)/shard_map/ppermute | solution.py:342
  69.4 1.6 %collective-permute-start.12 = (f32[128,256]{1,0:T(8,128)S(1)}, f32[128,256]{1,0:T(8,128)S(1)}, u32[]{:S(2)}, u32[]{:S(2)}) collective-permute-start(f32[128,256]{1,0:T(8,128)S(1)} %get-tuple-element.46), channel_id=1, source_target_pairs={{0,6},{2,0},{4,2},{6,4},{1,7},{3,1},{5,3},{7,5},{8,14},{10,8},{12,... | collective-permute-start | bytes 393224 | tf_op jit(solution)/shard_map/ppermute | solution.py:346
  71.0 3.3 %collective-permute-done.14 = f32[128,256]{1,0:T(8,128)S(1)} collective-permute-done((f32[128,256]{1,0:T(8,128)S(1)}, f32[128,256]{1,0:T(8,128)S(1)}, u32[]{:S(2)}, u32[]{:S(2)}) %collective-permute-start.14) | collective-permute-done | bytes 131104 | tf_op jit(solution)/shard_map/ppermute | solution.py:346
  74.4 1.8 %collective-permute-start.15 = (f32[256,256]{1,0:T(8,128)S(1)}, f32[256,256]{1,0:T(8,128)S(1)}, u32[]{:S(2)}, u32[]{:S(2)}) collective-permute-start(f32[256,256]{1,0:T(8,128)S(1)} %pad_maximum_fusion.1), channel_id=1, source_target_pairs={{0,2},{2,4},{4,6},{6,0},{1,3},{3,5},{5,7},{7,1},{8,10},{10,12},{12... | collective-permute-start | bytes 786440 | tf_op jit(solution)/shard_map/ppermute | solution.py:346
  76.6 5.4 %collective-permute-done.15 = f32[256,256]{1,0:T(8,128)S(1)} collective-permute-done((f32[256,256]{1,0:T(8,128)S(1)}, f32[256,256]{1,0:T(8,128)S(1)}, u32[]{:S(2)}, u32[]{:S(2)}) %collective-permute-start.15) | collective-permute-done | bytes 262176 | tf_op jit(solution)/shard_map/ppermute | solution.py:346
  82.0 2.7 %collective-permute-done.13 = f32[256,256]{1,0:T(8,128)S(1)} collective-permute-done((f32[256,256]{1,0:T(8,128)S(1)}, f32[256,256]{1,0:T(8,128)S(1)}, u32[]{:S(2)}, u32[]{:S(2)}) %collective-permute-start.13) | collective-permute-done | bytes 262176 | tf_op jit(solution)/shard_map/ppermute | solution.py:346
  (44 shorter events, 5.8 us)
Async XLA Ops:
  0.8 9.5 %collective-permute-start = (f32[4,2048]{1,0:T(4,128)S(1)}, f32[4,2048]{1,0:T(4,128)S(1)}, u32[]{:S(2)}, u32[]{:S(2)}) collective-permute-start(f32[4,2048]{1,0:T(4,128)S(1)} %slice_convert_fusion), channel_id=1, source_target_pairs={{0,8},{8,16},{16,24},{24,32},{32,40},{40,48},{48,56},{56,64},{64,7... | collective-permute-start | bytes 98312 | tf_op jit(solution)/shard_map/ppermute | solution.py:359
  4.7 3.5 %copy-start.9 = (bf16[2048,2,256]{2,1,0:T(2,128)(2,1)S(1)}, bf16[2048,2,256]{2,1,0:T(2,128)(2,1)}, u32[]{:S(2)}) copy-start(bf16[2048,2,256]{2,1,0:T(2,128)(2,1)} %param.12) | copy-start | bytes 6291460
  8.2 2.1 %copy-start.1 = (bf16[256,2048]{1,0:T(8,128)(2,1)S(1)}, bf16[256,2048]{1,0:T(8,128)(2,1)}, u32[]{:S(2)}) copy-start(bf16[256,2048]{1,0:T(8,128)(2,1)} %tokens.5) | copy-start | bytes 3145732
  8.2 2.1 %copy-start.2 = (bf16[2048,2,4]{0,2,1:T(4,128)(2,1)S(1)}, bf16[2048,2,4]{0,2,1:T(4,128)(2,1)}, u32[]{:S(2)}) copy-start(bf16[2048,2,4]{0,2,1:T(4,128)(2,1)} %param.14) | copy-start | bytes 98308
  8.3 2.1 %copy-start.3 = (f32[4,512]{1,0:T(4,128)S(1)}, f32[4,512]{1,0:T(4,128)}, u32[]{:S(2)}) copy-start(f32[4,512]{1,0:T(4,128)} %taps_v.3) | copy-start | bytes 24580
  8.3 2.1 %copy-start.4 = (f32[4,2,256]{2,1,0:T(2,128)S(1)}, f32[4,2,256]{2,1,0:T(2,128)}, u32[]{:S(2)}) copy-start(f32[4,2,256]{2,1,0:T(2,128)} %taps_qk.5) | copy-start | bytes 24580
  8.3 2.1 %copy-start.5 = (f32[4]{0:T(128)S(1)}, f32[4]{0:T(128)}, u32[]{:S(2)}) copy-start(f32[4]{0:T(128)} %a_log.3) | copy-start | bytes 52
  8.3 2.1 %copy-start.6 = (f32[4]{0:T(128)S(1)}, f32[4]{0:T(128)}, u32[]{:S(2)}) copy-start(f32[4]{0:T(128)} %dt_bias.3) | copy-start | bytes 52
  8.3 2.0 %copy-start.7 = (f32[4]{0:T(128)S(1)}, f32[4]{0:T(128)}, u32[]{:S(2)}) copy-start(f32[4]{0:T(128)} %beta_bias.3) | copy-start | bytes 52
  15.2 11.9 %collective-permute-start.2 = (f32[128,256]{1,0:T(8,128)S(1)}, f32[128,256]{1,0:T(8,128)S(1)}, u32[]{:S(2)}, u32[]{:S(2)}) collective-permute-start(f32[128,256]{1,0:T(8,128)S(1)} %get-tuple-element.27), channel_id=1, source_target_pairs={{0,16},{8,24},{16,0},{24,8},{32,48},{40,56},{48,32},{56,40},{1,17}... | collective-permute-start | bytes 393224 | tf_op jit(solution)/shard_map/ppermute | solution.py:342
  17.7 18.5 %copy-start.8 = (f32[128]{0:T(128)S(1)}, f32[128]{0:T(128)}, u32[]{:S(2)}) copy-start(f32[128]{0:T(128)} %param.20) | copy-start | bytes 1540
  17.7 9.4 %collective-permute-start.3 = (f32[128,256]{1,0:T(8,128)S(1)}, f32[128,256]{1,0:T(8,128)S(1)}, u32[]{:S(2)}, u32[]{:S(2)}) collective-permute-start(f32[128,256]{1,0:T(8,128)S(1)} %get-tuple-element.28), channel_id=1, source_target_pairs={{0,24},{8,16},{16,8},{24,0},{32,56},{40,48},{48,40},{56,32},{1,25}... | collective-permute-start | bytes 393224 | tf_op jit(solution)/shard_map/ppermute | solution.py:342
  25.2 5.1 %collective-permute-start.1 = (f32[128,256]{1,0:T(8,128)S(1)}, f32[128,256]{1,0:T(8,128)S(1)}, u32[]{:S(2)}, u32[]{:S(2)}) collective-permute-start(f32[128,256]{1,0:T(8,128)S(1)} %get-tuple-element.26), channel_id=1, source_target_pairs={{0,8},{8,0},{16,24},{24,16},{32,40},{40,32},{48,56},{56,48},{1,9},... | collective-permute-start | bytes 393224 | tf_op jit(solution)/shard_map/ppermute | solution.py:342
  31.2 10.7 %collective-permute-start.4 = (f32[128,256]{1,0:T(8,128)S(1)}, f32[128,256]{1,0:T(8,128)S(1)}, u32[]{:S(2)}, u32[]{:S(2)}) collective-permute-start(f32[128,256]{1,0:T(8,128)S(1)} %get-tuple-element.29.own), channel_id=1, source_target_pairs={{0,32},{8,40},{16,48},{24,56},{32,0},{40,8},{48,16},{56,24},{1,33}... | collective-permute-start | bytes 393224 | tf_op jit(solution)/shard_map/ppermute | solution.py:342
  39.6 25.0 %copy-start = (bf16[512,2048]{1,0:T(8,128)(2,1)S(1)}, bf16[512,2048]{1,0:T(8,128)(2,1)}, u32[]{:S(2)}) copy-start(bf16[512,2048]{1,0:T(8,128)(2,1)} %w_out.3) | copy-start | bytes 6291460
  42.6 7.2 %collective-permute-start.6 = (f32[128,256]{1,0:T(8,128)S(1)}, f32[128,256]{1,0:T(8,128)S(1)}, u32[]{:S(2)}, u32[]{:S(2)}) collective-permute-start(f32[128,256]{1,0:T(8,128)S(1)} %row.1), channel_id=1, source_target_pairs={{0,128},{64,192},{1,129},{65,193},{2,130},{66,194},{3,131},{67,195... | collective-permute-start | bytes 393224 | tf_op jit(solution)/shard_map/ppermute | solution.py:350
  47.2 2.6 %collective-permute-start.7 = (f32[128,256]{1,0:T(8,128)S(1)}, f32[128,256]{1,0:T(8,128)S(1)}, u32[]{:S(2)}, u32[]{:S(2)}) collective-permute-start(f32[128,256]{1,0:T(8,128)S(1)} %row.1), channel_id=1, source_target_pairs={{0,192},{1,193},{2,194},{3,195},{4,196},{5,197},{6,198},{7,199},{8... | collective-permute-start | bytes 393224 | tf_op jit(solution)/shard_map/ppermute | solution.py:350
  47.9 6.9 %collective-permute-start.5 = (f32[128,256]{1,0:T(8,128)S(1)}, f32[128,256]{1,0:T(8,128)S(1)}, u32[]{:S(2)}, u32[]{:S(2)}) collective-permute-start(f32[128,256]{1,0:T(8,128)S(1)} %row.1), channel_id=1, source_target_pairs={{0,64},{64,128},{128,192},{1,65},{65,129},{129,193},{2,66},{66,130... | collective-permute-start | bytes 393224 | tf_op jit(solution)/shard_map/ppermute | solution.py:350
  55.8 6.3 %collective-permute-start.10 = (f32[128,128]{1,0:T(8,128)S(1)}, f32[128,128]{1,0:T(8,128)S(1)}, u32[]{:S(2)}, u32[]{:S(2)}) collective-permute-start(f32[128,128]{1,0:T(8,128)S(1)} %get-tuple-element.41), channel_id=1, source_target_pairs={{0,24},{8,16},{16,8},{24,0},{32,56},{40,48},{48,40},{56,32},{1,25}... | collective-permute-start | bytes 196616 | tf_op jit(solution)/shard_map/ppermute | solution.py:342
  57.2 5.2 %collective-permute-start.8 = (f32[128,128]{1,0:T(8,128)S(1)}, f32[128,128]{1,0:T(8,128)S(1)}, u32[]{:S(2)}, u32[]{:S(2)}) collective-permute-start(f32[128,128]{1,0:T(8,128)S(1)} %get-tuple-element.39), channel_id=1, source_target_pairs={{0,8},{8,0},{16,24},{24,16},{32,40},{40,32},{48,56},{56,48},{1,9},... | collective-permute-start | bytes 196616 | tf_op jit(solution)/shard_map/ppermute | solution.py:342
  59.0 5.5 %collective-permute-start.9 = (f32[128,128]{1,0:T(8,128)S(1)}, f32[128,128]{1,0:T(8,128)S(1)}, u32[]{:S(2)}, u32[]{:S(2)}) collective-permute-start(f32[128,128]{1,0:T(8,128)S(1)} %get-tuple-element.40), channel_id=1, source_target_pairs={{0,16},{8,24},{16,0},{24,8},{32,48},{40,56},{48,32},{56,40},{1,17}... | collective-permute-start | bytes 196616 | tf_op jit(solution)/shard_map/ppermute | solution.py:342
  65.9 2.7 %collective-permute-start.11 = (f32[4,256,256]{2,1,0:T(8,128)S(1)}, f32[4,256,256]{2,1,0:T(8,128)S(1)}, u32[]{:S(2)}, u32[]{:S(2)}) collective-permute-start(f32[4,256,256]{2,1,0:T(8,128)S(1)} %get-tuple-element.44), channel_id=1, source_target_pairs={{0,1},{1,0},{2,3},{3,2},{4,5},{5,4},{6,7},{7,6},{8,9},{9,8},{10,11... | collective-permute-start | bytes 3145736 | tf_op jit(solution)/shard_map/ppermute | solution.py:342
  68.7 5.6 %collective-permute-start.14 = (f32[128,256]{1,0:T(8,128)S(1)}, f32[128,256]{1,0:T(8,128)S(1)}, u32[]{:S(2)}, u32[]{:S(2)}) collective-permute-start(f32[128,256]{1,0:T(8,128)S(1)} %get-tuple-element.45), channel_id=1, source_target_pairs={{0,2},{2,4},{4,6},{6,0},{1,3},{3,5},{5,7},{7,1},{8,10},{10,12},{12... | collective-permute-start | bytes 393224 | tf_op jit(solution)/shard_map/ppermute | solution.py:346
  69.4 6.8 %collective-permute-start.12 = (f32[128,256]{1,0:T(8,128)S(1)}, f32[128,256]{1,0:T(8,128)S(1)}, u32[]{:S(2)}, u32[]{:S(2)}) collective-permute-start(f32[128,256]{1,0:T(8,128)S(1)} %get-tuple-element.46), channel_id=1, source_target_pairs={{0,6},{2,0},{4,2},{6,4},{1,7},{3,1},{5,3},{7,5},{8,14},{10,8},{12,... | collective-permute-start | bytes 393224 | tf_op jit(solution)/shard_map/ppermute | solution.py:346
  74.4 7.6 %collective-permute-start.15 = (f32[256,256]{1,0:T(8,128)S(1)}, f32[256,256]{1,0:T(8,128)S(1)}, u32[]{:S(2)}, u32[]{:S(2)}) collective-permute-start(f32[256,256]{1,0:T(8,128)S(1)} %pad_maximum_fusion.1), channel_id=1, source_target_pairs={{0,2},{2,4},{4,6},{6,0},{1,3},{3,5},{5,7},{7,1},{8,10},{10,12},{12... | collective-permute-start | bytes 786440 | tf_op jit(solution)/shard_map/ppermute | solution.py:346
  76.2 8.5 %collective-permute-start.13 = (f32[256,256]{1,0:T(8,128)S(1)}, f32[256,256]{1,0:T(8,128)S(1)}, u32[]{:S(2)}, u32[]{:S(2)}) collective-permute-start(f32[256,256]{1,0:T(8,128)S(1)} %pad_maximum_fusion), channel_id=1, source_target_pairs={{0,6},{2,0},{4,2},{6,4},{1,7},{3,1},{5,3},{7,5},{8,14},{10,8},{12,... | collective-permute-start | bytes 786440 | tf_op jit(solution)/shard_map/ppermute | solution.py:346

commit v5 on v4

--- a/solution.py
+++ b/solution.py
@@ -266,15 +266,20 @@
     return jnp.concatenate([prod[:, :DK], prod[:, DK:] + second[:, DK:]], 1)
 
 
+def spot_of(place):
+    return place[0] ^ (3 * place[1])
+
+
 def pair_kernel(place, r2, r3, out):
-    odd = (place[0] & 1) == 1
+    odd = (spot_of(place) & 1) == 1
     out[...] = after(
         jnp.where(odd, r2[...], r3[...]), jnp.where(odd, r3[...], r2[...])
     )
 
 
 def quad_kernel(place, r0, r1, far, total, first_pair):
-    odd, upper = (place[0] & 1) == 1, place[0] >= 2
+    spot = spot_of(place)
+    odd, upper = (spot & 1) == 1, spot >= 2
     near = after(jnp.where(odd, r0[...], r1[...]), jnp.where(odd, r1[...], r0[...]))
     first, second = jnp.where(upper, far[...], near), jnp.where(upper, near, far[...])
     total[...] = after(second, first)
@@ -282,7 +287,8 @@
 
 
 def prefix_kernel(place, r0, r1, r2, r3, first_pair, prefixes):
-    odd, upper = (place[0] & 1) == 1, place[0] >= 2
+    spot = spot_of(place)
+    odd, upper = (spot & 1) == 1, spot >= 2
     near_first = jnp.where(odd, r1[...], r0[...])
     far_first = jnp.where(odd, r3[...], r2[...])
     prefixes[0] = jnp.where(upper, far_first, near_first)
@@ -307,9 +313,9 @@
     states[0] = s
     for j in range(3):
         states[j + 1] = dot3(prefixes[j, :, :DK], s) + prefixes[j, :, DK:]
-    mine = place[0]
+    spot = spot_of(place)
     for slot, out in enumerate((out0, out1, out2, out3)):
-        out[...] = states[mine ^ slot]
+        out[...] = states[spot ^ slot]
 
 
 def normed_kernel(place, r0, r1, r2, r3, reply, gates, w_out, normed, out, states):
@@ -353,7 +359,7 @@
 def local(tokens, w_qk, w_vz, w_ab, conv_qk, conv_v, a_log, dt_bias, beta_bias, norm_gain, w_out):
     y, z = lax.axis_index("y"), lax.axis_index("z")
     x, core = lax.axis_index("x"), lax.axis_index("core")
-    place = jnp.stack([z & 3, z >> 2, x, core]).astype(jnp.int32)
+    place = jnp.stack([(z & 3) ^ (3 * (z >> 2)), z >> 2, x, core]).astype(jnp.int32)
 
     tail = tokens[SEG - 4 :].astype(F32)
     halo = lax.ppermute(tail, ("y", "z"), [(i, i + 1) for i in range(31)])
@@ -421,7 +427,7 @@
         compiler_params=params(16),
         name="prefix",
     )(place, *got, first_pair)
-    other = swap(total, "z", 8, 4)
+    other = swap(total, "z", 8, 7)
     row = pl.pallas_call(
         row_kernel,
         out_shape=arr(DK, 256),

time: 85.7 us -> 83.6 us (0.975)
  starting transfers between devices: 30.6 us -> 28.3 us
    ppermute x8, starting transfers between devices: 15.3 us -> 13.4 us  [swap(): return lax.ppermute(v, axis, [(i, i ^ mask) for i in range(size)])]
where the time goes in v5:
time: 83.6 us; the launch traced here: 83.3 us
  waiting for transfers between devices  28.9 us (35%)
  starting transfers between devices  28.3 us (34%)
  Pallas kernels  19.8 us (24%)
  local copies, waits for them, and re-layouts  4.13 us (5%)
  other arithmetic  1.73 us (2%)
    ppermute x8, starting transfers between devices, swap(): return lax.ppermute(v, axis, [(i, i ^ mask) for i in range(size)])  13.4 us
    ppermute x4, waiting for transfers between devices, shift(): return lax.ppermute(v, axis, [(i, (i + step) % size) for i in range(size)])  11.4 us
    ppermute x8, waiting for transfers between devices, swap(): return lax.ppermute(v, axis, [(i, i ^ mask) for i in range(size)])  11.3 us
    pallas_call x2, Pallas kernels, segment(): pl.pallas_call(functools.partial(segment_kernel, own_group), grid=(1,), o...  9.65 us
    ppermute x3, starting transfers between devices, forward(): return lax.ppermute(v, axis, [(i, i + step) for i in range(size - step)])  6.8 us
    ppermute x3, waiting for transfers between devices, forward(): return lax.ppermute(v, axis, [(i, i + step) for i in range(size - step)])  4.74 us
    ppermute x4, starting transfers between devices, shift(): return lax.ppermute(v, axis, [(i, (i + step) % size) for i in range(size)])  4.36 us
    unnamed x22, local copies, waits for them, and re-layouts  4.11 us
  transfers between devices with their start and end apart: 16, of which 12 were waited for; matrix products, arithmetic and copies ran while one was open for 5% of the time, Pallas kernels for 13%

profile of v5, /device:TPU:14, one launch (start us, length us, event | category | flops | bytes accessed | tf_op | source)
XLA Modules:
  0.0 83.3 jit_solution(13956697899207253024)
XLA Ops:
  0.0 0.8 slice_convert_fusion
  0.8 3.8 %collective-permute-start = (f32[4,2048]{1,0:T(4,128)S(1)}, f32[4,2048]{1,0:T(4,128)S(1)}, u32[]{:S(2)}, u32[]{:S(2)}) collective-permute-start(f32[4,2048]{1,0:T(4,128)S(1)} %slice_convert_fusion), channel_id=1, source_target_pairs={{0,8},{8,16},{16,24},{24,32},{32,40},{40,48},{48,56},{56,64},{64,7... | collective-permute-start | bytes 98312 | tf_op jit(solution)/shard_map/ppermute | solution.py:365
  4.7 3.5 %copy.13 = bf16[256,8,2,512]{3,1,2,0:T(8,128)(2,1)S(1)} copy(bf16[256,8,2,512]{3,2,1,0:T(2,128)(2,1)} %bitcast.41) | data formatting | bytes 8388608
  8.8 1.5 %collective-permute-done.halo = f32[4,2048]{1,0:T(4,128)S(1)} collective-permute-done((f32[4,2048]{1,0:T(4,128)S(1)}, f32[4,2048]{1,0:T(4,128)S(1)}, u32[]{:S(2)}, u32[]{:S(2)}) %collective-permute-start) | collective-permute-done | bytes 32800 | tf_op jit(solution)/shard_map/ppermute | solution.py:365
  10.4 4.8 %segment_other.1 = (f32[128,256]{1,0:T(8,128)S(1)}, f32[128,256]{1,0:T(8,128)S(1)}, f32[256,128]{1,0:T(8,128)S(1)}, f32[2,256,256]{2,1,0:T(8,128)S(1)}, f32[256,8]{1,0:T(8,128)S(1)}) custom-call(s32[4]{0:T(128)S(1)} %pad_add_fusion.place, f32[4]{0:T(128)S(1)} %copy-done.5, f32[4]{0:T(128)S(1)} %copy-done.6, f32[4]{0:T(128)S(1)} %copy-done.7, ...), custom_call_target="tpu_custom_call" | custom-call | flops 6000000000 | bytes 6000000 | tf_op jit(solution)/shard_map/segment_other/pallas_call | solution.py:373
  15.2 2.5 %collective-permute-start.2 = (f32[128,256]{1,0:T(8,128)S(1)}, f32[128,256]{1,0:T(8,128)S(1)}, u32[]{:S(2)}, u32[]{:S(2)}) collective-permute-start(f32[128,256]{1,0:T(8,128)S(1)} %get-tuple-element.27), channel_id=1, source_target_pairs={{0,16},{8,24},{16,0},{24,8},{32,48},{40,56},{48,32},{56,40},{1,17}... | collective-permute-start | bytes 393224 | tf_op jit(solution)/shard_map/ppermute | solution.py:348
  17.7 2.7 %collective-permute-start.3 = (f32[128,256]{1,0:T(8,128)S(1)}, f32[128,256]{1,0:T(8,128)S(1)}, u32[]{:S(2)}, u32[]{:S(2)}) collective-permute-start(f32[128,256]{1,0:T(8,128)S(1)} %get-tuple-element.28), channel_id=1, source_target_pairs={{0,24},{8,16},{16,8},{24,0},{32,56},{40,48},{48,40},{56,32},{1,25}... | collective-permute-start | bytes 393224 | tf_op jit(solution)/shard_map/ppermute | solution.py:348
  20.4 4.8 %segment_own.1 = (f32[128,256]{1,0:T(8,128)S(1)}, f32[128,256]{1,0:T(8,128)S(1)}, f32[256,128]{1,0:T(8,128)S(1)}, f32[2,256,256]{2,1,0:T(8,128)S(1)}, f32[256,8]{1,0:T(8,128)S(1)}) custom-call(s32[4]{0:T(128)S(1)} %pad_add_fusion.place, f32[4]{0:T(128)S(1)} %copy-done.5, f32[4]{0:T(128)S(1)} %copy-done.6, f32[4]{0:T(128)S(1)} %copy-done.7, ...), custom_call_target="tpu_custom_call" | custom-call | flops 6000000000 | bytes 6000000 | tf_op jit(solution)/shard_map/segment_own/pallas_call | solution.py:373
  25.8 1.3 %collective-permute-done.2.r2 = f32[128,256]{1,0:T(8,128)S(1)} collective-permute-done((f32[128,256]{1,0:T(8,128)S(1)}, f32[128,256]{1,0:T(8,128)S(1)}, u32[]{:S(2)}, u32[]{:S(2)}) %collective-permute-start.2) | collective-permute-done | bytes 131104 | tf_op jit(solution)/shard_map/ppermute | solution.py:348
  27.0 0.7 pair.1.far
  27.8 2.5 %collective-permute-done.1.r1 = f32[128,256]{1,0:T(8,128)S(1)} collective-permute-done((f32[128,256]{1,0:T(8,128)S(1)}, f32[128,256]{1,0:T(8,128)S(1)}, u32[]{:S(2)}, u32[]{:S(2)}) %collective-permute-start.1) | collective-permute-done | bytes 131104 | tf_op jit(solution)/shard_map/ppermute | solution.py:348
  30.3 1.0 %quad.1 = (f32[128,256]{1,0:T(8,128)S(1)}, f32[128,256]{1,0:T(8,128)S(1)}) custom-call(s32[4]{0:T(128)S(1)} %pad_add_fusion.place, f32[128,256]{1,0:T(8,128)S(1)} %get-tuple-element.25.r0, f32[128,256]{1,0:T(8,128)S(1)} %collective-permute-done.1.r1, f32[128,256]{1,0:T(8,128)S(1)} %pair.1.far), custom_call_target="tpu_custom_call" | custom-call | tf_op jit(solution)/shard_map/quad/pallas_call | solution.py:414
  31.2 3.1 %collective-permute-start.4 = (f32[128,256]{1,0:T(8,128)S(1)}, f32[128,256]{1,0:T(8,128)S(1)}, u32[]{:S(2)}, u32[]{:S(2)}) collective-permute-start(f32[128,256]{1,0:T(8,128)S(1)} %get-tuple-element.29.own), channel_id=1, source_target_pairs={{0,56},{8,48},{16,40},{24,32},{32,24},{40,16},{48,8},{56,0},{1,57}... | collective-permute-start | bytes 393224 | tf_op jit(solution)/shard_map/ppermute | solution.py:348
  34.3 3.4 %reply.1 = (f32[4,256,256]{2,1,0:T(8,128)S(1)}, f32[256,512]{1,0:T(8,128)S(1)}) custom-call(s32[4]{0:T(128)S(1)} %pad_add_fusion.place, bf16[256,2048]{1,0:T(8,128)(2,1)S(1)} %copy-done.1, f32[4,2048]{1,0:T(4,128)S(1)} %collective-permute-done.halo, bf16[2048,512]{1,0:T(8,128)(2,1)S(1)} %bitcast.37, bf16[2048,1024]{1,0:T(8,128)(2,1)S(1)} %bitcast.34, ...), custom_call_target="tpu_custom_call" | custom-call | flops 4000000000 | bytes 3000000 | tf_op jit(solution)/shard_map/reply/pallas_call | solution.py:394
  38.4 2.0 %collective-permute-done.4.other = f32[128,256]{1,0:T(8,128)S(1)} collective-permute-done((f32[128,256]{1,0:T(8,128)S(1)}, f32[128,256]{1,0:T(8,128)S(1)}, u32[]{:S(2)}, u32[]{:S(2)}) %collective-permute-start.4) | collective-permute-done | bytes 131104 | tf_op jit(solution)/shard_map/ppermute | solution.py:348
  41.2 4.2 %collective-permute-start.6 = (f32[128,256]{1,0:T(8,128)S(1)}, f32[128,256]{1,0:T(8,128)S(1)}, u32[]{:S(2)}, u32[]{:S(2)}) collective-permute-start(f32[128,256]{1,0:T(8,128)S(1)} %row.1), channel_id=1, source_target_pairs={{0,128},{64,192},{1,129},{65,193},{2,130},{66,194},{3,131},{67,195... | collective-permute-start | bytes 393224 | tf_op jit(solution)/shard_map/ppermute | solution.py:356
  46.1 1.9 %collective-permute-start.5 = (f32[128,256]{1,0:T(8,128)S(1)}, f32[128,256]{1,0:T(8,128)S(1)}, u32[]{:S(2)}, u32[]{:S(2)}) collective-permute-start(f32[128,256]{1,0:T(8,128)S(1)} %row.1), channel_id=1, source_target_pairs={{0,64},{64,128},{128,192},{1,65},{65,129},{129,193},{2,66},{66,130... | collective-permute-start | bytes 393224 | tf_op jit(solution)/shard_map/ppermute | solution.py:356
  48.2 4.7 %collective-permute-done.5.y1 = f32[128,256]{1,0:T(8,128)S(1)} collective-permute-done((f32[128,256]{1,0:T(8,128)S(1)}, f32[128,256]{1,0:T(8,128)S(1)}, u32[]{:S(2)}, u32[]{:S(2)}) %collective-permute-start.5) | collective-permute-done | bytes 131104 | tf_op jit(solution)/shard_map/ppermute | solution.py:356
  52.9 1.1 %state.1 = (f32[128,128]{1,0:T(8,128)S(1)}, f32[128,128]{1,0:T(8,128)S(1)}, f32[128,128]{1,0:T(8,128)S(1)}, f32[128,128]{1,0:T(8,128)S(1)}) custom-call(s32[4]{0:T(128)S(1)} %pad_add_fusion.place, f32[128,256]{1,0:T(8,128)S(1)} %collective-permute-done.5.y1, f32[128,128]{1,0:T(8,128)S(1)} %early.1, f32[128,256]{1,0:T(8,128)S(1)} %collective-permute-done.4.other, ...), custom_call_target="tpu_custom_call" | custom-call | tf_op jit(solution)/shard_map/state/pallas_call | solution.py:448
  54.0 3.2 %collective-permute-start.10 = (f32[128,128]{1,0:T(8,128)S(1)}, f32[128,128]{1,0:T(8,128)S(1)}, u32[]{:S(2)}, u32[]{:S(2)}) collective-permute-start(f32[128,128]{1,0:T(8,128)S(1)} %get-tuple-element.41), channel_id=1, source_target_pairs={{0,24},{8,16},{16,8},{24,0},{32,56},{40,48},{48,40},{56,32},{1,25}... | collective-permute-start | bytes 196616 | tf_op jit(solution)/shard_map/ppermute | solution.py:348
  57.2 1.3 %collective-permute-start.9 = (f32[128,128]{1,0:T(8,128)S(1)}, f32[128,128]{1,0:T(8,128)S(1)}, u32[]{:S(2)}, u32[]{:S(2)}) collective-permute-start(f32[128,128]{1,0:T(8,128)S(1)} %get-tuple-element.40), channel_id=1, source_target_pairs={{0,16},{8,24},{16,0},{24,8},{32,48},{40,56},{48,32},{56,40},{1,17}... | collective-permute-start | bytes 196616 | tf_op jit(solution)/shard_map/ppermute | solution.py:348
  58.5 2.1 %collective-permute-done.10.r3 = f32[128,128]{1,0:T(8,128)S(1)} collective-permute-done((f32[128,128]{1,0:T(8,128)S(1)}, f32[128,128]{1,0:T(8,128)S(1)}, u32[]{:S(2)}, u32[]{:S(2)}) %collective-permute-start.10) | collective-permute-done | bytes 65568 | tf_op jit(solution)/shard_map/ppermute | solution.py:348
  60.7 0.8 collective-permute-done.8.r1
  61.5 0.9 %collective-permute-done.9.r2 = f32[128,128]{1,0:T(8,128)S(1)} collective-permute-done((f32[128,128]{1,0:T(8,128)S(1)}, f32[128,128]{1,0:T(8,128)S(1)}, u32[]{:S(2)}, u32[]{:S(2)}) %collective-permute-start.9) | collective-permute-done | bytes 65568 | tf_op jit(solution)/shard_map/ppermute | solution.py:348
  62.4 1.4 %normed.1 = (bf16[256,512]{1,0:T(8,128)(2,1)S(1)}, f32[4,256,256]{2,1,0:T(8,128)S(1)}) custom-call(s32[4]{0:T(128)S(1)} %pad_add_fusion.place, f32[128,128]{1,0:T(8,128)S(1)} %get-tuple-element.38.r0, f32[128,128]{1,0:T(8,128)S(1)} %collective-permute-done.8.r1, f32[128,128]{1,0:T(8,128)S(1)} %collective-permute-done.9.r2, ...), custom_call_target="tpu_custom_call" | custom-call | tf_op jit(solution)/shard_map/normed/pallas_call | solution.py:459
  63.9 1.0 %own.1 = f32[4,256,256]{2,1,0:T(8,128)S(1)} custom-call(s32[4]{0:T(128)S(1)} %pad_add_fusion.place, bf16[256,512]{1,0:T(8,128)(2,1)S(1)} %get-tuple-element.43.normed, bf16[512,2048]{1,0:T(8,128)(2,1)S(1)} %copy-done), custom_call_target="tpu_custom_call" | custom-call | flops 1000000000 | bytes 3000000 | tf_op jit(solution)/shard_map/own/pallas_call | solution.py:469
  64.9 1.6 %collective-permute-done.11 = f32[4,256,256]{2,1,0:T(8,128)S(1)} collective-permute-done((f32[4,256,256]{2,1,0:T(8,128)S(1)}, f32[4,256,256]{2,1,0:T(8,128)S(1)}, u32[]{:S(2)}, u32[]{:S(2)}) %collective-permute-start.11) | collective-permute-done | bytes 1048608 | tf_op jit(solution)/shard_map/ppermute | solution.py:348
  67.2 1.6 %collective-permute-start.12 = (f32[128,256]{1,0:T(8,128)S(1)}, f32[128,256]{1,0:T(8,128)S(1)}, u32[]{:S(2)}, u32[]{:S(2)}) collective-permute-start(f32[128,256]{1,0:T(8,128)S(1)} %get-tuple-element.46), channel_id=1, source_target_pairs={{0,6},{2,0},{4,2},{6,4},{1,7},{3,1},{5,3},{7,5},{8,14},{10,8},{12,... | collective-permute-start | bytes 393224 | tf_op jit(solution)/shard_map/ppermute | solution.py:352
  68.8 3.3 %collective-permute-done.14 = f32[128,256]{1,0:T(8,128)S(1)} collective-permute-done((f32[128,256]{1,0:T(8,128)S(1)}, f32[128,256]{1,0:T(8,128)S(1)}, u32[]{:S(2)}, u32[]{:S(2)}) %collective-permute-start.14) | collective-permute-done | bytes 131104 | tf_op jit(solution)/shard_map/ppermute | solution.py:352
  72.2 1.8 %collective-permute-start.15 = (f32[256,256]{1,0:T(8,128)S(1)}, f32[256,256]{1,0:T(8,128)S(1)}, u32[]{:S(2)}, u32[]{:S(2)}) collective-permute-start(f32[256,256]{1,0:T(8,128)S(1)} %pad_maximum_fusion.1), channel_id=1, source_target_pairs={{0,2},{2,4},{4,6},{6,0},{1,3},{3,5},{5,7},{7,1},{8,10},{10,12},{12... | collective-permute-start | bytes 786440 | tf_op jit(solution)/shard_map/ppermute | solution.py:352
  74.5 5.4 %collective-permute-done.15 = f32[256,256]{1,0:T(8,128)S(1)} collective-permute-done((f32[256,256]{1,0:T(8,128)S(1)}, f32[256,256]{1,0:T(8,128)S(1)}, u32[]{:S(2)}, u32[]{:S(2)}) %collective-permute-start.15) | collective-permute-done | bytes 262176 | tf_op jit(solution)/shard_map/ppermute | solution.py:352
  79.8 2.7 %collective-permute-done.13 = f32[256,256]{1,0:T(8,128)S(1)} collective-permute-done((f32[256,256]{1,0:T(8,128)S(1)}, f32[256,256]{1,0:T(8,128)S(1)}, u32[]{:S(2)}, u32[]{:S(2)}) %collective-permute-start.13) | collective-permute-done | bytes 262176 | tf_op jit(solution)/shard_map/ppermute | solution.py:352
  (44 shorter events, 5.5 us)
Async XLA Ops:
  0.8 9.5 %collective-permute-start = (f32[4,2048]{1,0:T(4,128)S(1)}, f32[4,2048]{1,0:T(4,128)S(1)}, u32[]{:S(2)}, u32[]{:S(2)}) collective-permute-start(f32[4,2048]{1,0:T(4,128)S(1)} %slice_convert_fusion), channel_id=1, source_target_pairs={{0,8},{8,16},{16,24},{24,32},{32,40},{40,48},{48,56},{56,64},{64,7... | collective-permute-start | bytes 98312 | tf_op jit(solution)/shard_map/ppermute | solution.py:365
  4.7 3.5 %copy-start.9 = (bf16[2048,2,256]{2,1,0:T(2,128)(2,1)S(1)}, bf16[2048,2,256]{2,1,0:T(2,128)(2,1)}, u32[]{:S(2)}) copy-start(bf16[2048,2,256]{2,1,0:T(2,128)(2,1)} %param.12) | copy-start | bytes 6291460
  8.2 2.1 %copy-start.1 = (bf16[256,2048]{1,0:T(8,128)(2,1)S(1)}, bf16[256,2048]{1,0:T(8,128)(2,1)}, u32[]{:S(2)}) copy-start(bf16[256,2048]{1,0:T(8,128)(2,1)} %tokens.5) | copy-start | bytes 3145732
  8.2 2.1 %copy-start.2 = (bf16[2048,2,4]{0,2,1:T(4,128)(2,1)S(1)}, bf16[2048,2,4]{0,2,1:T(4,128)(2,1)}, u32[]{:S(2)}) copy-start(bf16[2048,2,4]{0,2,1:T(4,128)(2,1)} %param.14) | copy-start | bytes 98308
  8.3 2.1 %copy-start.3 = (f32[4,512]{1,0:T(4,128)S(1)}, f32[4,512]{1,0:T(4,128)}, u32[]{:S(2)}) copy-start(f32[4,512]{1,0:T(4,128)} %taps_v.3) | copy-start | bytes 24580
  8.3 2.1 %copy-start.4 = (f32[4,2,256]{2,1,0:T(2,128)S(1)}, f32[4,2,256]{2,1,0:T(2,128)}, u32[]{:S(2)}) copy-start(f32[4,2,256]{2,1,0:T(2,128)} %taps_qk.5) | copy-start | bytes 24580
  8.3 2.1 %copy-start.5 = (f32[4]{0:T(128)S(1)}, f32[4]{0:T(128)}, u32[]{:S(2)}) copy-start(f32[4]{0:T(128)} %a_log.3) | copy-start | bytes 52
  8.3 2.0 %copy-start.6 = (f32[4]{0:T(128)S(1)}, f32[4]{0:T(128)}, u32[]{:S(2)}) copy-start(f32[4]{0:T(128)} %dt_bias.3) | copy-start | bytes 52
  8.3 2.0 %copy-start.7 = (f32[4]{0:T(128)S(1)}, f32[4]{0:T(128)}, u32[]{:S(2)}) copy-start(f32[4]{0:T(128)} %beta_bias.3) | copy-start | bytes 52
  15.2 11.9 %collective-permute-start.2 = (f32[128,256]{1,0:T(8,128)S(1)}, f32[128,256]{1,0:T(8,128)S(1)}, u32[]{:S(2)}, u32[]{:S(2)}) collective-permute-start(f32[128,256]{1,0:T(8,128)S(1)} %get-tuple-element.27), channel_id=1, source_target_pairs={{0,16},{8,24},{16,0},{24,8},{32,48},{40,56},{48,32},{56,40},{1,17}... | collective-permute-start | bytes 393224 | tf_op jit(solution)/shard_map/ppermute | solution.py:348
  17.7 16.6 %copy-start.8 = (f32[128]{0:T(128)S(1)}, f32[128]{0:T(128)}, u32[]{:S(2)}) copy-start(f32[128]{0:T(128)} %param.20) | copy-start | bytes 1540
  17.7 9.4 %collective-permute-start.3 = (f32[128,256]{1,0:T(8,128)S(1)}, f32[128,256]{1,0:T(8,128)S(1)}, u32[]{:S(2)}, u32[]{:S(2)}) collective-permute-start(f32[128,256]{1,0:T(8,128)S(1)} %get-tuple-element.28), channel_id=1, source_target_pairs={{0,24},{8,16},{16,8},{24,0},{32,56},{40,48},{48,40},{56,32},{1,25}... | collective-permute-start | bytes 393224 | tf_op jit(solution)/shard_map/ppermute | solution.py:348
  25.2 5.1 %collective-permute-start.1 = (f32[128,256]{1,0:T(8,128)S(1)}, f32[128,256]{1,0:T(8,128)S(1)}, u32[]{:S(2)}, u32[]{:S(2)}) collective-permute-start(f32[128,256]{1,0:T(8,128)S(1)} %get-tuple-element.26), channel_id=1, source_target_pairs={{0,8},{8,0},{16,24},{24,16},{32,40},{40,32},{48,56},{56,48},{1,9},... | collective-permute-start | bytes 393224 | tf_op jit(solution)/shard_map/ppermute | solution.py:348
  31.2 9.2 %collective-permute-start.4 = (f32[128,256]{1,0:T(8,128)S(1)}, f32[128,256]{1,0:T(8,128)S(1)}, u32[]{:S(2)}, u32[]{:S(2)}) collective-permute-start(f32[128,256]{1,0:T(8,128)S(1)} %get-tuple-element.29.own), channel_id=1, source_target_pairs={{0,56},{8,48},{16,40},{24,32},{32,24},{40,16},{48,8},{56,0},{1,57}... | collective-permute-start | bytes 393224 | tf_op jit(solution)/shard_map/ppermute | solution.py:348
  37.7 24.7 %copy-start = (bf16[512,2048]{1,0:T(8,128)(2,1)S(1)}, bf16[512,2048]{1,0:T(8,128)(2,1)}, u32[]{:S(2)}) copy-start(bf16[512,2048]{1,0:T(8,128)(2,1)} %w_out.3) | copy-start | bytes 6291460
  41.2 6.8 %collective-permute-start.6 = (f32[128,256]{1,0:T(8,128)S(1)}, f32[128,256]{1,0:T(8,128)S(1)}, u32[]{:S(2)}, u32[]{:S(2)}) collective-permute-start(f32[128,256]{1,0:T(8,128)S(1)} %row.1), channel_id=1, source_target_pairs={{0,128},{64,192},{1,129},{65,193},{2,130},{66,194},{3,131},{67,195... | collective-permute-start | bytes 393224 | tf_op jit(solution)/shard_map/ppermute | solution.py:356
  45.4 2.6 %collective-permute-start.7 = (f32[128,256]{1,0:T(8,128)S(1)}, f32[128,256]{1,0:T(8,128)S(1)}, u32[]{:S(2)}, u32[]{:S(2)}) collective-permute-start(f32[128,256]{1,0:T(8,128)S(1)} %row.1), channel_id=1, source_target_pairs={{0,192},{1,193},{2,194},{3,195},{4,196},{5,197},{6,198},{7,199},{8... | collective-permute-start | bytes 393224 | tf_op jit(solution)/shard_map/ppermute | solution.py:356
  46.1 6.9 %collective-permute-start.5 = (f32[128,256]{1,0:T(8,128)S(1)}, f32[128,256]{1,0:T(8,128)S(1)}, u32[]{:S(2)}, u32[]{:S(2)}) collective-permute-start(f32[128,256]{1,0:T(8,128)S(1)} %row.1), channel_id=1, source_target_pairs={{0,64},{64,128},{128,192},{1,65},{65,129},{129,193},{2,66},{66,130... | collective-permute-start | bytes 393224 | tf_op jit(solution)/shard_map/ppermute | solution.py:356
  54.0 6.6 %collective-permute-start.10 = (f32[128,128]{1,0:T(8,128)S(1)}, f32[128,128]{1,0:T(8,128)S(1)}, u32[]{:S(2)}, u32[]{:S(2)}) collective-permute-start(f32[128,128]{1,0:T(8,128)S(1)} %get-tuple-element.41), channel_id=1, source_target_pairs={{0,24},{8,16},{16,8},{24,0},{32,56},{40,48},{48,40},{56,32},{1,25}... | collective-permute-start | bytes 196616 | tf_op jit(solution)/shard_map/ppermute | solution.py:348
  57.2 4.3 %collective-permute-start.8 = (f32[128,128]{1,0:T(8,128)S(1)}, f32[128,128]{1,0:T(8,128)S(1)}, u32[]{:S(2)}, u32[]{:S(2)}) collective-permute-start(f32[128,128]{1,0:T(8,128)S(1)} %get-tuple-element.39), channel_id=1, source_target_pairs={{0,8},{8,0},{16,24},{24,16},{32,40},{40,32},{48,56},{56,48},{1,9},... | collective-permute-start | bytes 196616 | tf_op jit(solution)/shard_map/ppermute | solution.py:348
  57.2 5.2 %collective-permute-start.9 = (f32[128,128]{1,0:T(8,128)S(1)}, f32[128,128]{1,0:T(8,128)S(1)}, u32[]{:S(2)}, u32[]{:S(2)}) collective-permute-start(f32[128,128]{1,0:T(8,128)S(1)} %get-tuple-element.40), channel_id=1, source_target_pairs={{0,16},{8,24},{16,0},{24,8},{32,48},{40,56},{48,32},{56,40},{1,17}... | collective-permute-start | bytes 196616 | tf_op jit(solution)/shard_map/ppermute | solution.py:348
  63.8 2.7 %collective-permute-start.11 = (f32[4,256,256]{2,1,0:T(8,128)S(1)}, f32[4,256,256]{2,1,0:T(8,128)S(1)}, u32[]{:S(2)}, u32[]{:S(2)}) collective-permute-start(f32[4,256,256]{2,1,0:T(8,128)S(1)} %get-tuple-element.44), channel_id=1, source_target_pairs={{0,1},{1,0},{2,3},{3,2},{4,5},{5,4},{6,7},{7,6},{8,9},{9,8},{10,11... | collective-permute-start | bytes 3145736 | tf_op jit(solution)/shard_map/ppermute | solution.py:348
  66.6 5.6 %collective-permute-start.14 = (f32[128,256]{1,0:T(8,128)S(1)}, f32[128,256]{1,0:T(8,128)S(1)}, u32[]{:S(2)}, u32[]{:S(2)}) collective-permute-start(f32[128,256]{1,0:T(8,128)S(1)} %get-tuple-element.45), channel_id=1, source_target_pairs={{0,2},{2,4},{4,6},{6,0},{1,3},{3,5},{5,7},{7,1},{8,10},{10,12},{12... | collective-permute-start | bytes 393224 | tf_op jit(solution)/shard_map/ppermute | solution.py:352
  67.2 6.8 %collective-permute-start.12 = (f32[128,256]{1,0:T(8,128)S(1)}, f32[128,256]{1,0:T(8,128)S(1)}, u32[]{:S(2)}, u32[]{:S(2)}) collective-permute-start(f32[128,256]{1,0:T(8,128)S(1)} %get-tuple-element.46), channel_id=1, source_target_pairs={{0,6},{2,0},{4,2},{6,4},{1,7},{3,1},{5,3},{7,5},{8,14},{10,8},{12,... | collective-permute-start | bytes 393224 | tf_op jit(solution)/shard_map/ppermute | solution.py:352
  72.2 7.6 %collective-permute-start.15 = (f32[256,256]{1,0:T(8,128)S(1)}, f32[256,256]{1,0:T(8,128)S(1)}, u32[]{:S(2)}, u32[]{:S(2)}) collective-permute-start(f32[256,256]{1,0:T(8,128)S(1)} %pad_maximum_fusion.1), channel_id=1, source_target_pairs={{0,2},{2,4},{4,6},{6,0},{1,3},{3,5},{5,7},{7,1},{8,10},{10,12},{12... | collective-permute-start | bytes 786440 | tf_op jit(solution)/shard_map/ppermute | solution.py:352
  74.0 8.5 %collective-permute-start.13 = (f32[256,256]{1,0:T(8,128)S(1)}, f32[256,256]{1,0:T(8,128)S(1)}, u32[]{:S(2)}, u32[]{:S(2)}) collective-permute-start(f32[256,256]{1,0:T(8,128)S(1)} %pad_maximum_fusion), channel_id=1, source_target_pairs={{0,6},{2,0},{4,2},{6,4},{1,7},{3,1},{5,3},{7,5},{8,14},{10,8},{12,... | collective-permute-start | bytes 786440 | tf_op jit(solution)/shard_map/ppermute | solution.py:352
